TPU v7x, 32 devices: a whole 2x2x4 slice. The times are simulated.
32 devices in a mesh: fsdp: 4 (over x, core), tp: 8 (over z, y).
Axes of the slice: x: 2, y: 2, z: 4, core: 2. Of those that a mesh axis runs over, the one named last changes fastest.
Arguments:
- activations: bfloat16 [16384, 1280], P(('fsdp', 'tp')), may hold values from -6 to 6
- cotangent: bfloat16 [16384, 1280], P(('fsdp', 'tp'))
- lengths: int32 [8, 20], P('fsdp'), may hold values from 0 to 1024, as said below
- positions: int32 [2, 16384], P(None, 'fsdp'), may hold values from 0 to 127, as said below
- weights: float32 [1280, 12, 1280], P('fsdp', None, 'tp')
- first_moment: float32 [1280, 12, 1280], P('fsdp', None, 'tp')
- second_moment: float32 [1280, 12, 1280], P('fsdp', None, 'tp')
- vectors: float32 [13, 1280], replicated
- vector_first: float32 [13, 1280], replicated
- vector_second: float32 [13, 1280], replicated
Outputs:
- block_output: bfloat16 [16384, 1280], P(('fsdp', 'tp'))
- input_grad: bfloat16 [16384, 1280], P(('fsdp', 'tp'))
- next_first: float32 [1280, 12, 1280], P('fsdp', None, 'tp')
- next_second: float32 [1280, 12, 1280], P('fsdp', None, 'tp')
- next_weights: float32 [1280, 12, 1280], P('fsdp', None, 'tp')
- next_vector_first: float32 [13, 1280], replicated
- next_vector_second: float32 [13, 1280], replicated
- next_vectors: float32 [13, 1280], replicated
Inputs may be any that keep to these rules, and one draw needn't show every extreme that they name: `lengths`: each row lists its pictures' patch counts, each from 100 to 1024, then zeros; a row's counts sum to at most 2048; one of each row's first two pictures has exactly 1024 patches. `positions`: A picture's patches are numbered row by row with a width of 8 to 16 patches; padding patches have 0 and 0.
All inputs are finite; a program needn't handle non-finite values.
Results may differ from a plain program's by a relative error of at most 0.025.
Values may be sent and summed in bfloat16 or wider, within the bound.
No kernel may reach another device: no remote copies, remote signals or barrier semaphores. Data moves between devices by JAX's collectives and lax.ppermute only.
A program may use at most 192 MiB of HBM per device.

v0:
```python
import jax
import jax.numpy as jnp
from jax import lax
from jax.sharding import PartitionSpec as P

HD = 80
SEQ = 2048
BQ = 512
STEP = 10


norm_eps = 1e-06
beta_first = 0.9
beta_second = 0.999
adam_eps = 1e-08
rate_matrix = 0.08
rate_vector = 0.6
decay_matrix = 0.05
gelu_slope = 1.702
masked_score = -1e30


def picture_ids(lengths):
    ends = jnp.cumsum(lengths, axis=1)
    spots = jnp.arange(SEQ, dtype=jnp.int32)
    return jnp.sum((spots[None, :, None] >= ends[:, None, :]).astype(jnp.int32), axis=2)


def rotary_tables(positions):
    quarter = HD // 4
    freq = 10000.0 ** (-jnp.arange(quarter, dtype=jnp.float32) * 4.0 / HD)
    upward = positions[0].astype(jnp.float32)[:, None] * freq[None, :]
    sideways = positions[1].astype(jnp.float32)[:, None] * freq[None, :]
    angle = jnp.concatenate([upward, sideways], axis=1)
    return (jnp.cos(angle), jnp.sin(angle))


def rotate(value, cosine, sine):
    half = HD // 2
    first = value[..., :half]
    second = value[..., half:]
    cos_part = cosine[:, None, :]
    sin_part = sine[:, None, :]
    return jnp.concatenate(
        [first * cos_part - second * sin_part, second * cos_part + first * sin_part], axis=-1
    )


def unrotate(value, cosine, sine):
    half = HD // 2
    first = value[..., :half]
    second = value[..., half:]
    cos_part = cosine[:, None, :]
    sin_part = sine[:, None, :]
    return jnp.concatenate(
        [first * cos_part + second * sin_part, second * cos_part - first * sin_part], axis=-1
    )


def layer_norm(value, gain, shift):
    center = value - jnp.mean(value, axis=-1, keepdims=True)
    spread = jnp.mean(center * center, axis=-1, keepdims=True)
    return center * lax.rsqrt(spread + norm_eps) * gain + shift


def quick_gelu(value):
    return value * jax.nn.sigmoid(gelu_slope * value)


def adam_update(param, grad, first, second, rate, decay):
    first = beta_first * first + (1.0 - beta_first) * grad
    second = beta_second * second + (1.0 - beta_second) * grad * grad
    first_hat = first / (1.0 - beta_first**STEP)
    second_hat = second / (1.0 - beta_second**STEP)
    fresh = param - rate * (first_hat / (jnp.sqrt(second_hat) + adam_eps) + decay * param)
    return (first, second, fresh)


def spread_rows(normed):
    return lax.all_gather(normed, "tp", axis=0, tiled=True)


def regather(normed):
    return lax.all_gather(normed, "tp", axis=0, tiled=True)


def collect_back(grads):
    return lax.all_gather(grads, "tp", axis=0, tiled=True)


def sum_branch(left, right_w, pattern):

    def term(start, count):
        return jnp.einsum(pattern, left, right_w, preferred_element_type=jnp.float32)

    return lax.psum_scatter(
        term(jnp.int32(0), left.shape[0] // lax.axis_size("tp") * lax.axis_size("tp")).astype(
            jnp.bfloat16
        ),
        "tp",
        scatter_dimension=0,
        tiled=True,
    ).astype(jnp.float32)


def sum_inputs(left, right_w, pattern):

    def term(start, count):
        return jnp.einsum(pattern, left, right_w, preferred_element_type=jnp.float32)

    return lax.psum_scatter(
        term(jnp.int32(0), left.shape[0] // lax.axis_size("tp") * lax.axis_size("tp")).astype(
            jnp.bfloat16
        ),
        "tp",
        scatter_dimension=0,
        tiled=True,
    ).astype(jnp.float32)


def project_heads(rows, block_w, local_bias, cosine, sine):
    heads_pre = (
        jnp.einsum("td,dsc->tsc", rows, block_w[:, 0:3, :], preferred_element_type=jnp.float32)
        + local_bias[6:9][None, :, :]
    )
    count = rows.shape[0]
    heads = heads_pre.shape[2] // HD
    query = rotate(heads_pre[:, 0, :].reshape(count, heads, HD), cosine, sine).astype(jnp.bfloat16)
    keys = rotate(heads_pre[:, 1, :].reshape(count, heads, HD), cosine, sine).astype(jnp.bfloat16)
    values = heads_pre[:, 2, :].reshape(count, heads, HD).astype(jnp.bfloat16)
    return (query, keys, values)


def expand_hidden(rows, lift_w, bias_rows):
    return (
        jnp.einsum("td,drc->trc", rows, lift_w, preferred_element_type=jnp.float32)
        + bias_rows[None, :, :]
    )


def masked_scores(q_block, k_row, id_block, id_row, scale):
    scores = jnp.einsum("qhc,khc->hqk", q_block, k_row, preferred_element_type=jnp.float32) * scale
    return jnp.where((id_block[:, None] == id_row[None, :])[None], scores, masked_score)


def attention_forward(query, keys, values, ids, scale):
    count_rows = ids.shape[0]
    blocks = SEQ // BQ

    def attend(index):
        row = index // blocks
        part = index % blocks
        first = row * SEQ
        q_block = lax.dynamic_slice_in_dim(query, first + part * BQ, BQ, 0)
        k_row = lax.dynamic_slice_in_dim(keys, first, SEQ, 0)
        v_row = lax.dynamic_slice_in_dim(values, first, SEQ, 0)
        id_row = lax.dynamic_index_in_dim(ids, row, 0, keepdims=False)
        id_block = lax.dynamic_slice_in_dim(id_row, part * BQ, BQ, 0)
        scores = masked_scores(q_block, k_row, id_block, id_row, scale)
        top = jnp.max(scores, axis=2, keepdims=True)
        expo = jnp.exp(scores - top)
        summed = jnp.sum(expo, axis=2, keepdims=True)
        probs = (expo / summed).astype(jnp.bfloat16)
        result = jnp.einsum("hqk,khc->qhc", probs, v_row, preferred_element_type=jnp.float32)
        return (result, (top + jnp.log(summed))[:, :, 0])

    results, logsums = lax.map(attend, jnp.arange(count_rows * blocks, dtype=jnp.int32))
    return (results.reshape(count_rows * SEQ, -1), logsums)


def attention_backward(query, keys, values, grad_att, ids, logsums, scale):
    count_rows = ids.shape[0]
    blocks = SEQ // BQ
    heads = query.shape[1]

    def row_grads(row):
        first = row * SEQ
        k_row = lax.dynamic_slice_in_dim(keys, first, SEQ, 0)
        v_row = lax.dynamic_slice_in_dim(values, first, SEQ, 0)
        id_row = lax.dynamic_index_in_dim(ids, row, 0, keepdims=False)

        def step(carry, part):
            key_acc, value_acc = carry
            start = first + part * BQ
            q_block = lax.dynamic_slice_in_dim(query, start, BQ, 0)
            g_block = lax.dynamic_slice_in_dim(grad_att, start, BQ, 0)
            id_block = lax.dynamic_slice_in_dim(id_row, part * BQ, BQ, 0)
            lse_block = lax.dynamic_index_in_dim(logsums, row * blocks + part, 0, keepdims=False)
            scores = masked_scores(q_block, k_row, id_block, id_row, scale)
            probs = jnp.exp(scores - lse_block[:, :, None])
            prob_grad = jnp.einsum(
                "qhc,khc->hqk", g_block, v_row, preferred_element_type=jnp.float32
            )
            inner = jnp.sum(probs * prob_grad, axis=2, keepdims=True)
            score_grad = (probs * (prob_grad - inner)).astype(jnp.bfloat16)
            query_part = (
                jnp.einsum("hqk,khc->qhc", score_grad, k_row, preferred_element_type=jnp.float32)
                * scale
            )
            key_acc = (
                key_acc
                + jnp.einsum(
                    "hqk,qhc->khc", score_grad, q_block, preferred_element_type=jnp.float32
                )
                * scale
            )
            value_acc = value_acc + jnp.einsum(
                "hqk,qhc->khc",
                probs.astype(jnp.bfloat16),
                g_block,
                preferred_element_type=jnp.float32,
            )
            return ((key_acc, value_acc), query_part)

        zeros = jnp.zeros((SEQ, heads, HD), jnp.float32)
        (key_grad, value_grad), query_parts = lax.scan(
            step, (zeros, zeros), jnp.arange(blocks, dtype=jnp.int32)
        )
        return (query_parts.reshape(SEQ, heads, HD), key_grad, value_grad)

    query_grad, key_grad, value_grad = lax.map(row_grads, jnp.arange(count_rows, dtype=jnp.int32))
    return (
        query_grad.reshape(-1, heads, HD),
        key_grad.reshape(-1, heads, HD),
        value_grad.reshape(-1, heads, HD),
    )


def local(
    activations,
    cotangent,
    lengths,
    positions,
    weights,
    first_moment,
    second_moment,
    vectors,
    vector_first,
    vector_second,
):
    columns = weights.shape[2]
    heads = columns // HD
    width = vectors.shape[1]
    offset = lax.axis_index("tp") * columns
    local_bias = lax.dynamic_slice_in_dim(vectors, offset, columns, 1)
    ids = picture_ids(lengths)
    total = ids.shape[0] * SEQ
    scale = HD ** (-0.5)
    cosine, sine = rotary_tables(positions)
    shard_low = weights.astype(jnp.bfloat16)
    block_w = lax.all_gather(shard_low, "fsdp", axis=0, tiled=True)
    inputs = activations.astype(jnp.float32)
    early_norm = layer_norm(inputs, vectors[0], vectors[1]).astype(jnp.bfloat16)
    early_rows = spread_rows(early_norm)
    query, keys, values = project_heads(early_rows, block_w, local_bias, cosine, sine)
    attended, logsums = attention_forward(query, keys, values, ids, scale)
    attended = attended.astype(jnp.bfloat16)
    middle = inputs + sum_branch(attended, block_w[:, 3, :], "tc,ic->ti") + vectors[4]
    later_norm = layer_norm(middle, vectors[2], vectors[3]).astype(jnp.bfloat16)
    later_rows = spread_rows(later_norm)
    upper = expand_hidden(later_rows, block_w[:, 4:8, :], local_bias[9:13])
    hidden = quick_gelu(upper).astype(jnp.bfloat16)
    final = middle + sum_branch(hidden, block_w[:, 8:12, :], "trc,irc->ti") + vectors[5]
    back_w = lax.all_gather(shard_low, "fsdp", axis=0, tiled=True)
    back_early = regather(early_norm)
    query, keys, values = project_heads(back_early, back_w, local_bias, cosine, sine)
    grad_out = cotangent.astype(jnp.float32)
    back_later = regather(later_norm)
    upper = expand_hidden(back_later, back_w[:, 4:8, :], local_bias[9:13])
    hidden = quick_gelu(upper).astype(jnp.bfloat16)
    returned_late = collect_back(cotangent)
    hidden_grad = jnp.einsum(
        "ti,irc->trc", returned_late, back_w[:, 8:12, :], preferred_element_type=jnp.float32
    )
    down_grad = jnp.einsum("ti,trc->irc", returned_late, hidden, preferred_element_type=jnp.float32)
    upper_grad = jax.vjp(quick_gelu, upper)[1](hidden_grad)[0].astype(jnp.bfloat16)
    lift_grad = jnp.einsum(
        "td,trc->drc", back_later, upper_grad, preferred_element_type=jnp.float32
    )
    later_grad = sum_inputs(upper_grad, back_w[:, 4:8, :], "trc,drc->td")
    ffn_grad = jnp.concatenate([lift_grad, down_grad], axis=1)
    ffn_sum = jnp.sum(upper_grad, axis=0, dtype=jnp.float32)
    ffn_bias = lax.dynamic_update_slice_in_dim(
        jnp.zeros((4, width), jnp.float32), ffn_sum, offset, 1
    )
    middle_part, gain_second, shift_second = jax.vjp(layer_norm, middle, vectors[2], vectors[3])[1](
        later_grad
    )
    middle_grad = grad_out + middle_part
    returned_early = collect_back(middle_grad.astype(jnp.bfloat16))
    attended_grad = jnp.einsum(
        "ti,ic->tc", returned_early, back_w[:, 3, :], preferred_element_type=jnp.float32
    ).astype(jnp.bfloat16)
    out_grad = jnp.einsum("ti,tc->ic", returned_early, attended, preferred_element_type=jnp.float32)
    query_grad, key_grad, value_grad = attention_backward(
        query, keys, values, attended_grad.reshape(total, heads, HD), ids, logsums, scale
    )
    heads_grad = jnp.stack(
        [
            unrotate(query_grad, cosine, sine).reshape(total, columns),
            unrotate(key_grad, cosine, sine).reshape(total, columns),
            value_grad.reshape(total, columns),
        ],
        axis=1,
    ).astype(jnp.bfloat16)
    project_grad = jnp.einsum(
        "td,tsc->dsc", back_early, heads_grad, preferred_element_type=jnp.float32
    )
    early_grad = sum_inputs(heads_grad, back_w[:, 0:3, :], "tsc,dsc->td")
    input_part, gain_first, shift_first = jax.vjp(layer_norm, inputs, vectors[0], vectors[1])[1](
        early_grad
    )
    input_grad = (middle_grad + input_part).astype(jnp.bfloat16)
    weight_grad = jnp.concatenate([project_grad, out_grad[:, None, :], ffn_grad], axis=1)
    owned_grad = lax.psum_scatter(
        weight_grad.astype(jnp.bfloat16), "fsdp", scatter_dimension=0, tiled=True
    ).astype(jnp.float32)
    whole_rows = jnp.stack(
        [
            gain_first,
            shift_first,
            gain_second,
            shift_second,
            jnp.sum(middle_grad, axis=0),
            jnp.sum(grad_out, axis=0),
        ]
    )
    heads_sum = jnp.sum(heads_grad, axis=0, dtype=jnp.float32)
    placed = lax.dynamic_update_slice_in_dim(
        jnp.zeros((3, width), jnp.float32), heads_sum, offset, 1
    )
    vector_grad = lax.psum(jnp.concatenate([whole_rows, placed, ffn_bias], axis=0), ("fsdp", "tp"))
    next_first, next_second, next_weights = adam_update(
        weights, owned_grad, first_moment, second_moment, rate_matrix, decay_matrix
    )
    next_vector_first, next_vector_second, next_vectors = adam_update(
        vectors, vector_grad, vector_first, vector_second, rate_vector, 0.0
    )
    return (
        final.astype(jnp.bfloat16),
        input_grad,
        next_first,
        next_second,
        next_weights,
        next_vector_first,
        next_vector_second,
        next_vectors,
    )


def solution(mesh):
    in_specs = (
        P(("fsdp", "tp"), None),
        P(("fsdp", "tp"), None),
        P("fsdp", None),
        P(None, "fsdp"),
        P("fsdp", None, "tp"),
        P("fsdp", None, "tp"),
        P("fsdp", None, "tp"),
        P(),
        P(),
        P(),
    )
    out_specs = (
        P(("fsdp", "tp"), None),
        P(("fsdp", "tp"), None),
        P("fsdp", None, "tp"),
        P("fsdp", None, "tp"),
        P("fsdp", None, "tp"),
        P(),
        P(),
        P(),
    )
    return jax.shard_map(local, mesh=mesh, in_specs=in_specs, out_specs=out_specs, check_vma=False)
```

profile of v0, /device:TPU:8, one launch (start us, length us, event | category | flops | bytes accessed | tf_op | source)
XLA Modules:
  0.0 2077.8 jit_solution(18189871414050176003)
XLA Ops:
  9.2 5.1 copy.68
  22.9 63.0 %all-gather.8.cloned.1.call-done = bf16[1280,12,160]{2,1,0:T(8,128)(2,1)} async-done(((bf16[320,12,160]{2,1,0:T(8,128)(2,1)}), bf16[1280,12,160]{2,1,0:T(8,128)(2,1)}) %all-gather.8.cloned.1.call-update) | async-done | bytes 4915216 | tf_op jit(solution)/shard_map/all_gather | solution.py:251
  85.9 4.0 slice.126
  92.6 4.1 slice.118
  96.7 5.0 copy.87
  101.6 136.1 %all-gather.6.cloned.1.call-done = bf16[4096,1280]{1,0:T(8,128)(2,1)} async-done(((bf16[512,1280]{1,0:T(8,128)(2,1)}), bf16[4096,1280]{1,0:T(8,128)(2,1)}) %all-gather.6.cloned.1.call-update) | async-done | bytes 10485776 | tf_op jit(solution)/shard_map/all_gather | solution.py:80
  237.7 8.3 fusion.90
  251.0 118.5 %while.46 = (s32[]{:T(128)}, bf16[8,512,2,80]{1,3,2,0:T(8,128)(2,1)}, f32[8,2,512]{2,1,0:T(2,128)}, s32[8]{0:T(128)S(1)}, bf16[4096,2,80]{0,2,1:T(8,128)(2,1)}, ...) while((s32[]{:T(128)}, ...), condition=%wide.region_7.8_spmd, body=%wide.region_4.7_spmd.sunk | while | flops 697302016 | bytes 31226460 | solution.py:167
  260.8 4.4 fusion.139
  275.5 4.4 fusion.139
  290.3 4.4 fusion.139
  305.1 4.4 fusion.139
  319.8 4.4 fusion.139
  334.6 4.4 fusion.139
  349.4 4.4 fusion.139
  364.2 4.4 fusion.139
  373.8 5.5 convolution_convert_fusion
  379.9 176.1 %reduce-scatter.8.cloned.1.call-done = bf16[512,1280]{1,0:T(8,128)(2,1)} async-done(((bf16[4096,1280]{1,0:T(8,128)(2,1)}), bf16[512,1280]{1,0:T(8,128)(2,1)}) %reduce-scatter.8.cloned.1.call-update) | async-done | bytes 1310736 | tf_op jit(solution)/shard_map/reduce_scatter | solution.py:96
  561.3 8.1 fusion.87
  569.4 5.0 copy.89
  574.4 5.0 copy.90
  579.4 128.2 %all-gather.12.cloned.1.call-done = bf16[4096,1280]{1,0:T(8,128)(2,1)} async-done(((bf16[512,1280]{1,0:T(8,128)(2,1)}), bf16[4096,1280]{1,0:T(8,128)(2,1)}) %all-gather.12.cloned.1.call-update) | async-done | bytes 10485776 | tf_op jit(solution)/shard_map/all_gather | solution.py:88
  707.7 12.5 fusion.92
  720.2 139.1 %all-gather.10.cloned.1.call-done = bf16[4096,1280]{1,0:T(8,128)(2,1)} async-done(((bf16[512,1280]{1,0:T(8,128)(2,1)}), bf16[4096,1280]{1,0:T(8,128)(2,1)}) %all-gather.10.cloned.1.call-update) | async-done | bytes 10485776 | tf_op jit(solution)/shard_map/all_gather | solution.py:80
  859.3 10.3 fusion.91
  869.7 6.3 convert_reduce_fusion
  878.3 11.0 bitcast_convert_fusion.1
  889.5 15.2 bitcast_convert_fusion.2
  904.7 161.5 %reduce-scatter.12.cloned.1.call-done = bf16[512,1280]{1,0:T(8,128)(2,1)} async-done(((bf16[4096,1280]{1,0:T(8,128)(2,1)}), bf16[512,1280]{1,0:T(8,128)(2,1)}) %reduce-scatter.12.cloned.1.call-update) | async-done | bytes 1310736 | tf_op jit(solution)/shard_map/reduce_scatter | solution.py:111
  1071.3 175.6 %reduce-scatter.10.cloned.1.call-done = bf16[512,1280]{1,0:T(8,128)(2,1)} async-done(((bf16[4096,1280]{1,0:T(8,128)(2,1)}), bf16[512,1280]{1,0:T(8,128)(2,1)}) %reduce-scatter.10.cloned.1.call-update) | async-done | bytes 1310736 | tf_op jit(solution)/shard_map/reduce_scatter | solution.py:96
  1246.9 5.0 fusion.84
  1254.8 10.8 fusion.94
  1267.0 14.7 fusion.58
  1281.7 122.8 %all-gather.14.cloned.1.call-done = bf16[4096,1280]{1,0:T(8,128)(2,1)} async-done(((bf16[512,1280]{1,0:T(8,128)(2,1)}), bf16[4096,1280]{1,0:T(8,128)(2,1)}) %all-gather.14.cloned.1.call-update) | async-done | bytes 10485776 | tf_op jit(solution)/shard_map/all_gather | solution.py:88
  1404.5 8.6 convolution_convert_fusion.1
  1413.1 237.9 %while.48 = (s32[]{:T(128)}, f32[2,2048,2,80]{3,2,1,0:T(2,128)}, f32[2,2048,2,80]{1,0,3,2:T(2,128)}, bf16[2,2048,2,80]{1,3,2,0:T(8,128)(2,1)}, s32[2]{0:T(128)S(...) while((s32[]{:T(128)}, f32[2,2048,2,80]{3,2,1,0:T(2,128)}, ...), condition=%wide.region_19.20_spmd, body=%wide.region_15.19_spmd.sunk | while | flops 1711946752 | bytes 102362016 | solution.py:221
  1418.8 82.9 %while.49 = (s32[]{:T(128)}, f32[2048,2,80]{0,2,1:T(8,128)S(1)}, f32[2048,2,80]{0,2,1:T(8,128)}, f32[4,512,2,80]{1,3,2,0:T(8,128)}, s32[4]{0:T(128)S(1)}, /*inde...) while((s32[]{:T(128)}, f32[2048,2,80]{0,2,1:T(8,128)S(1)}, ...), condition=%wide.region_18.18_spmd.clone, body=%wide.region_16.17_spmd.clone.sunk | while | flops 1711946752 | bytes 85830064 | solution.py:216
  1428.2 4.5 multiply_reduce_fusion.3
  1445.2 3.7 fusion.151
  1448.9 4.5 multiply_reduce_fusion.3
  1469.6 4.5 multiply_reduce_fusion.3
  1486.6 3.7 fusion.151
  1490.3 4.5 multiply_reduce_fusion.3
  1505.7 22.8 %dynamic_update_slice.56 = f32[2,2048,2,80]{1,0,3,2:T(2,128)} dynamic-update-slice(f32[2,2048,2,80]{1,0,3,2:T(2,128)} %get-tuple-element.967, f32[1,2048,2,80]{1,0,3,2:T(1,128)S(1)} %copy.113, s32[]{:T(128)S(6)} %copy.145, s32[]{:T(128)} %constant.265.clone.1..sunk.1, s32[]{:T(128)} %constant.265.clone.1..sunk.1, s32[]{:T(128)} %constant.265.clone.1..sunk.1) | dynamic-update-slice | bytes 2621444 | tf_op jit(solution)/shard_map/while/body/jit(dynamic_update_index_in_dim)/dynamic_update_slice | solution.py:221
  1537.5 82.9 %while.49 = (s32[]{:T(128)}, f32[2048,2,80]{0,2,1:T(8,128)S(1)}, f32[2048,2,80]{0,2,1:T(8,128)}, f32[4,512,2,80]{1,3,2,0:T(8,128)}, s32[4]{0:T(128)S(1)}, /*inde...) while((s32[]{:T(128)}, f32[2048,2,80]{0,2,1:T(8,128)S(1)}, ...), condition=%wide.region_18.18_spmd.clone, body=%wide.region_16.17_spmd.clone.sunk | while | flops 1711946752 | bytes 85830064 | solution.py:216
  1543.3 3.7 fusion.151
  1546.9 4.5 multiply_reduce_fusion.3
  1564.0 3.7 fusion.151
  1567.7 4.5 multiply_reduce_fusion.3
  1588.4 4.5 multiply_reduce_fusion.3
  1605.4 3.7 fusion.151
  1609.1 4.5 multiply_reduce_fusion.3
  1624.5 22.8 %dynamic_update_slice.56 = f32[2,2048,2,80]{1,0,3,2:T(2,128)} dynamic-update-slice(f32[2,2048,2,80]{1,0,3,2:T(2,128)} %get-tuple-element.967, f32[1,2048,2,80]{1,0,3,2:T(1,128)S(1)} %copy.113, s32[]{:T(128)S(6)} %copy.145, s32[]{:T(128)} %constant.265.clone.1..sunk.1, s32[]{:T(128)} %constant.265.clone.1..sunk.1, s32[]{:T(128)} %constant.265.clone.1..sunk.1) | dynamic-update-slice | bytes 2621444 | tf_op jit(solution)/shard_map/while/body/jit(dynamic_update_index_in_dim)/dynamic_update_slice | solution.py:221
  1659.2 9.8 fusion.89
  1669.0 6.1 copy.92
  1675.2 6.2 copy.91
  1686.1 9.8 fusion.93
  1701.7 7.9 copy.83
  1710.8 11.7 bitcast_convert_fusion
  1723.9 35.1 %reduce-scatter.16.cloned.1.call-done = bf16[320,1920]{1,0:T(8,128)(2,1)} async-done(((bf16[1280,1920]{1,0:T(8,128)(2,1)}), bf16[320,1920]{1,0:T(8,128)(2,1)}) %reduce-scatter.16.cloned.1.call-update) | async-done | bytes 1228816
  1761.3 8.7 multiply_subtract_fusion
  1770.0 169.2 %reduce-scatter.14.cloned.1.call-done = bf16[512,1280]{1,0:T(8,128)(2,1)} async-done(((bf16[4096,1280]{1,0:T(8,128)(2,1)}), bf16[512,1280]{1,0:T(8,128)(2,1)}) %reduce-scatter.14.cloned.1.call-update) | async-done | bytes 1310736 | tf_op jit(solution)/shard_map/reduce_scatter | solution.py:111
  1946.4 3.8 add_convert_fusion
  1950.2 119.2 %all-reduce.2.cloned.1.call-done = f32[13,1280]{1,0:T(8,128)} async-done(((f32[13,1280]{1,0:T(8,128)}), f32[13,1280]{1,0:T(8,128)}) %all-reduce.2.cloned.1.call-update) | async-done | bytes 66576 | tf_op jit(solution)/shard_map/psum | solution.py:332
  (365 shorter events, 253.1 us)
Async XLA Ops:
  7.2 78.7 %all-gather.8.cloned.1.call-start = ((), (), s32[]{:S(2)}) async-start(), calls=%async_computation.6 | async-start | bytes 13107200 | tf_op jit(solution)/shard_map/all_gather | solution.py:251
  9.2 7.0 copy-start
  14.4 223.3 %all-gather.6.cloned.1.call-start = ((), (), s32[]{:S(2)}) async-start(), calls=%async_computation.5 | async-start | bytes 11796480 | tf_op jit(solution)/shard_map/all_gather | solution.py:80
  16.2 2.4 copy-start.28
  16.5 2.2 copy-start.33
  16.5 2.4 copy-start.46
  16.5 3.8 copy-start.42
  17.0 3.1 copy-start.43
  17.0 3.0 copy-start.35
  18.6 537.3 %reduce-scatter.8.cloned.1.call-start = ((), (), s32[]{:S(2)}) async-start(), calls=%async_computation.7 | async-start | bytes 11796480 | tf_op jit(solution)/shard_map/reduce_scatter | solution.py:96
  22.9 226.0 %copy-start.15 = (f32[4096,40]{0,1:T(8,128)}, f32[4096,40]{0,1:T(8,128)S(1)}, u32[]{:S(2)}) copy-start(f32[4096,40]{0,1:T(8,128)S(1)} %get-tuple-element.583) | copy-start | bytes 1966084
  22.9 226.0 %copy-start.17 = (f32[4096,40]{0,1:T(8,128)}, f32[4096,40]{0,1:T(8,128)S(1)}, u32[]{:S(2)}) copy-start(f32[4096,40]{0,1:T(8,128)S(1)} %get-tuple-element.584) | copy-start | bytes 1966084
  92.6 280.1 %copy-start.21 = (bf16[1280,1,160]{0,2,1:T(8,128)(2,1)}, bf16[1280,1,160]{0,2,1:T(8,128)(2,1)S(1)}, u32[]{:S(2)}) copy-start(bf16[1280,1,160]{0,2,1:T(8,128)(2,1)S(1)} %copy.88) | copy-start | bytes 1228804
  369.6 3.1 copy-start.2
  369.6 3.1 copy-start.26
  379.2 328.4 %all-gather.12.cloned.1.call-start = ((), (), s32[]{:S(2)}) async-start(), calls=%async_computation.10 | async-start | bytes 11796480 | tf_op jit(solution)/shard_map/all_gather | solution.py:88
  379.8 479.5 %all-gather.10.cloned.1.call-start = ((), (), s32[]{:S(2)}) async-start(), calls=%async_computation.8 | async-start | bytes 11796480 | tf_op jit(solution)/shard_map/all_gather | solution.py:80
  560.5 505.7 %reduce-scatter.12.cloned.1.call-start = ((), (), s32[]{:S(2)}) async-start(), calls=%async_computation.11 | async-start | bytes 11796480 | tf_op jit(solution)/shard_map/reduce_scatter | solution.py:111
  859.3 10.3 copy-start.11
  869.7 6.4 copy-start.9
  869.7 8.6 copy-start.24
  876.0 2.3 copy-start.19
  889.4 357.5 %reduce-scatter.10.cloned.1.call-start = ((), (), s32[]{:S(2)}) async-start(), calls=%async_computation.9 | async-start | bytes 11796480 | tf_op jit(solution)/shard_map/reduce_scatter | solution.py:96
  904.6 499.9 %all-gather.14.cloned.1.call-start = ((), (), s32[]{:S(2)}) async-start(), calls=%async_computation.12 | async-start | bytes 11796480 | tf_op jit(solution)/shard_map/all_gather | solution.py:88
  1066.1 3.1 copy-start.7
  1069.2 177.7 %copy-start.37 = (f32[1280]{0:T(1024)S(1)}, f32[1280]{0:T(1024)}, u32[]{:S(2)}) copy-start(f32[1280]{0:T(1024)} %get-tuple-element.475) | copy-start | bytes 15364
  1254.7 504.2 %reduce-scatter.16.cloned.1.call-start = ((), (), s32[]{:S(2)}) async-start(), calls=%async_computation.15 | async-start | bytes 6144000
  1254.8 12.1 copy-start.10
  1267.0 137.5 %copy-start.22 = (bf16[1280,1,160]{0,2,1:T(8,128)(2,1)S(1)}, bf16[1280,1,160]{0,2,1:T(8,128)(2,1)}, u32[]{:S(2)}) copy-start(bf16[1280,1,160]{0,2,1:T(8,128)(2,1)} %copy-done.21) | copy-start | bytes 1228804
  1281.7 131.4 %copy-start.27 = (s32[2,2048]{1,0:T(2,128)S(1)}, s32[2,2048]{1,0:T(2,128)}, u32[]{:S(2)}) copy-start(s32[2,2048]{1,0:T(2,128)} %copy-done.26) | copy-start | bytes 49156
  1422.2 2.3 copy-start.4
  1428.2 4.6 copy-start.5
  1442.9 2.3 copy-start.4
  1448.9 4.6 copy-start.5
  1463.6 2.3 copy-start.4
  1469.6 4.6 copy-start.5
  1484.3 2.3 copy-start.4
  1490.3 4.6 copy-start.5
  1540.9 2.3 copy-start.4
  1546.9 4.6 copy-start.5
  1561.6 2.3 copy-start.4
  1567.7 4.6 copy-start.5
  1582.4 2.3 copy-start.4
  1588.4 4.6 copy-start.5
  1603.1 2.3 copy-start.4
  1609.1 4.6 copy-start.5
  1675.1 6.2 copy-start.16
  1685.3 10.7 slice-start
  1686.0 9.8 copy-start.20
  1686.1 10.0 slice-start.1
  1686.1 10.0 slice-start.2
  1697.2 1.9 copy-start.14
  1697.2 1.9 copy-start.23
  1709.5 229.7 %reduce-scatter.14.cloned.1.call-start = ((), (), s32[]{:S(2)}) async-start(), calls=%async_computation.13 | async-start | bytes 11796480 | tf_op jit(solution)/shard_map/reduce_scatter | solution.py:111
  1722.6 346.9 %all-reduce.2.cloned.1.call-start = ((), (), s32[]{:S(2)}) async-start(), calls=%async_computation.14 | async-start | bytes 163840 | tf_op jit(solution)/shard_map/psum | solution.py:332
  1761.3 178.0 %copy-start.1 = (bf16[512,1280]{1,0:T(8,128)(2,1)S(1)}, bf16[512,1280]{1,0:T(8,128)(2,1)}, u32[]{:S(2)}) copy-start(bf16[512,1280]{1,0:T(8,128)(2,1)} %param.16) | copy-start | bytes 3932164
  1761.3 178.0 %copy-start.29 = (f32[1280]{0:T(1024)S(1)}, f32[1280]{0:T(1024)}, u32[]{:S(2)}) copy-start(f32[1280]{0:T(1024)} %copy-done.28) | copy-start | bytes 15364
  1761.3 177.9 %copy-start.34 = (f32[512]{0:T(512)S(1)}, f32[512]{0:T(512)}, u32[]{:S(2)}) copy-start(f32[512]{0:T(512)} %copy-done.33) | copy-start | bytes 6148
  1770.0 171.4 %copy-start.44 = (f32[512]{0:T(512)S(1)}, f32[512]{0:T(512)}, u32[]{:S(2)}) copy-start(f32[512]{0:T(512)} %copy-done.43) | copy-start | bytes 6148
  1770.0 171.5 %copy-start.36 = (f32[512]{0:T(512)S(1)}, f32[512]{0:T(512)}, u32[]{:S(2)}) copy-start(f32[512]{0:T(512)} %copy-done.35) | copy-start | bytes 6148
  1939.2 2.3 copy-start.8
  1946.4 123.1 %copy-start.30 = (f32[13,1280]{1,0:T(8,128)S(1)}, f32[13,1280]{1,0:T(8,128)}, u32[]{:S(2)}) copy-start(f32[13,1280]{1,0:T(8,128)} %param.23) | copy-start | bytes 199684
  1946.4 123.0 %copy-start.31 = (f32[13,1280]{1,0:T(8,128)S(1)}, f32[13,1280]{1,0:T(8,128)}, u32[]{:S(2)}) copy-start(f32[13,1280]{1,0:T(8,128)} %param.25) | copy-start | bytes 199684
  1946.4 123.0 %copy-start.32 = (f32[13,1280]{1,0:T(8,128)S(1)}, f32[13,1280]{1,0:T(8,128)}, u32[]{:S(2)}) copy-start(f32[13,1280]{1,0:T(8,128)} %param.24) | copy-start | bytes 199684
  (11 other events, 12.8 us)
Sparse Core Ops, SparseCore 0:
  14.5 71.3 all-gather.7
  88.7 148.9 all-gather.5
  379.4 176.5 reduce-scatter.7
  558.0 149.5 all-gather.11
  710.3 149.0 all-gather.9
  889.5 176.5 reduce-scatter.11
  1069.7 177.1 reduce-scatter.9
  1254.9 149.5 all-gather.13
  1709.7 49.2 reduce-scatter.15
  1762.8 176.3 reduce-scatter.13
  1946.5 122.8 all-reduce.1
where the time goes:
time: 2090 us; the launch traced here: 2080 us
  waiting for transfers between devices  1430 us (68%)
  matrix products  298 us (14%)
  local copies, waits for them, and re-layouts  183 us (9%)
  other arithmetic  115 us (6%)
  loops' own time  39.6 us (2%)
    reduce_scatter x2, waiting for transfers between devices, sum_branch(): lax.psum_scatter(term(jnp.int32(0), left.shape[0] // lax.axis_size('tp')...  352 us
    reduce_scatter x2, waiting for transfers between devices, sum_inputs(): lax.psum_scatter(term(jnp.int32(0), left.shape[0] // lax.axis_size('tp')...  331 us
    all_gather x2, waiting for transfers between devices, spread_rows(): return lax.all_gather(normed, 'tp', axis=0, tiled=True)  275 us
    all_gather x2, waiting for transfers between devices, collect_back(): return lax.all_gather(grads, 'tp', axis=0, tiled=True)  251 us
    psum x1, waiting for transfers between devices, local(): lax.psum(jnp.concatenate([whole_rows, placed, ffn_bias], axis=0), ('fsdp'...  119 us
    all_gather x1, waiting for transfers between devices, local(): block_w = lax.all_gather(shard_low, 'fsdp', axis=0, tiled=True)  63 us
    dynamic_update_slice x8, local copies, waits for them, and re-layouts, attention_backward(): lax.map(row_grads, jnp.arange(count_rows, dtype=jnp.int32))  55.6 us
    unnamed x5, matrix products  51.8 us
  transfers between devices with their start and end apart: 11, of which 11 were waited for; matrix products, arithmetic and copies ran while one was open for 6% of the time, Pallas kernels for 0%

commit v1 on v0

v1 whole, which is shorter than its diff:
```python
import functools
import math

import jax
import jax.numpy as jnp
import numpy as np
from jax import lax
from jax.experimental import pallas as pl
from jax.experimental.pallas import tpu as pltpu
from jax.sharding import Mesh, PartitionSpec as P

HD = 80
LANES = 128
SEQ = 2048
STEP = 10
CHUNKS = 2

norm_eps = 1e-06
beta_first = 0.9
beta_second = 0.999
adam_eps = 1e-08
rate_matrix = 0.08
rate_vector = 0.6
decay_matrix = 0.05
gelu_slope = 1.702
masked_score = -1e30

LOW = jnp.bfloat16
FULL = jnp.float32
SQUARE = ("zl", "y")
LINE = ("zh", "zl")


def dot(a, b, dims):
    return lax.dot_general(a, b, (dims, ((), ())), preferred_element_type=FULL)


def nn(a, b):
    return dot(a, b, ((1,), (0,)))


def nt(a, b):
    return dot(a, b, ((1,), (1,)))


def tn(a, b):
    return dot(a, b, ((0,), (0,)))


def layer_norm(value, gain, shift):
    center = value - jnp.mean(value, axis=-1, keepdims=True)
    spread = jnp.mean(center * center, axis=-1, keepdims=True)
    return center * lax.rsqrt(spread + norm_eps) * gain + shift


def quick_gelu(value):
    return value * jax.nn.sigmoid(gelu_slope * value)


def adam_update(param, grad, first, second, rate, decay):
    first = beta_first * first + (1.0 - beta_first) * grad
    second = beta_second * second + (1.0 - beta_second) * grad * grad
    first_hat = first / (1.0 - beta_first**STEP)
    second_hat = second / (1.0 - beta_second**STEP)
    fresh = param - rate * (first_hat / (jnp.sqrt(second_hat) + adam_eps) + decay * param)
    return (first, second, fresh)


def swap(value, axis, far):
    return lax.ppermute(value, axis, [(i, i ^ far) for i in range(lax.axis_size(axis))])


def gather(value, axis):
    return [value] + [swap(value, axis, far) for far in range(1, lax.axis_size(axis))]


def settle(pieces, spot):
    bit = 1
    while bit < len(pieces):
        turned = (spot // bit) % 2 == 1
        pieces = [jnp.where(turned, pieces[i ^ bit], pieces[i]) for i in range(len(pieces))]
        bit *= 2
    return pieces


def scatter(value, axis, dim):
    spot = lax.axis_index(axis)

    def part(far):
        return lax.dynamic_index_in_dim(value, spot ^ far, dim, keepdims=False)

    total = part(0).astype(FULL)
    for far in range(1, lax.axis_size(axis)):
        total = total + swap(part(far).astype(LOW), axis, far).astype(FULL)
    return total


def scatter_near(pieces, axis):
    total = pieces[0].astype(FULL)
    for far in range(1, len(pieces)):
        total = total + swap(pieces[far].astype(LOW), axis, far).astype(FULL)
    return total


def leaves(things):
    return jax.tree.leaves(things)


def tie(value, *earlier):
    first = leaves(earlier)
    return pl.pallas_call(
        lambda *refs: None,
        in_specs=[pl.BlockSpec(memory_space=pl.ANY)] * (1 + len(first)),
        out_specs=pl.BlockSpec(memory_space=pl.ANY),
        out_shape=jax.ShapeDtypeStruct(value.shape, value.dtype),
        input_output_aliases={0: 0},
        name="tie",
    )(value, *first)


def sum_everywhere(value):
    for axis in ("c", "x", "y", "zl", "zh"):
        far = 1
        while far < lax.axis_size(axis):
            value = value + swap(value, axis, far)
            far *= 2
    return value


def project_kernel(heads, info_ref, rows_ref, w_ref, bias_ref, cos_ref, sin_ref, *refs):
    q_ref, k_ref, v_ref, kt_ref, vt_ref = refs[-5:]
    wide = heads * LANES
    cosine = cos_ref[...]
    sine = sin_ref[...]
    rows = rows_ref[...]
    factor = HD ** (-0.5) * math.log2(math.e)
    for slot in range(3):
        out = nn(rows, w_ref[:, slot * wide : (slot + 1) * wide])
        out = out + bias_ref[:, slot * wide : (slot + 1) * wide]
        for head in range(heads):
            lanes = slice(head * LANES, (head + 1) * LANES)
            value = out[:, lanes]
            if slot < 2:
                value = value * cosine + pltpu.roll(value, LANES // 2, 1) * sine
            if slot == 0:
                q_ref[:, lanes] = (value * factor).astype(LOW)
            elif slot == 1:
                k_ref[:, lanes] = value.astype(LOW)
                kt_ref[lanes, :] = value.T.astype(LOW)
            else:
                v_ref[:, lanes] = value.astype(LOW)
                vt_ref[lanes, :] = value.T.astype(LOW)


def project(info, rows, wide_w, wide_bias, cosine, sine, members, heads, earlier):
    total, width = rows.shape
    tile = total // (2 * members)
    wide = heads * LANES

    def place(g, info):
        return ((g % members) ^ info[0]) * 2 + g // members

    flat = pl.BlockSpec((tile, wide), lambda g, info: (place(g, info), 0))
    tall = pl.BlockSpec((wide, tile), lambda g, info: (0, place(g, info)))
    return pl.pallas_call(
        functools.partial(project_kernel, heads),
        grid_spec=pltpu.PrefetchScalarGridSpec(
            num_scalar_prefetch=1,
            grid=(2 * members,),
            in_specs=[
                pl.BlockSpec((tile, width), lambda g, info: (g, 0)),
                pl.BlockSpec((width, 3 * wide), lambda g, info: (0, 0)),
                pl.BlockSpec((1, 3 * wide), lambda g, info: (0, 0)),
                pl.BlockSpec((tile, LANES), lambda g, info: (g, 0)),
                pl.BlockSpec((tile, LANES), lambda g, info: (g, 0)),
            ]
            + [pl.BlockSpec(memory_space=pl.ANY)] * len(earlier),
            out_specs=[flat, flat, flat, tall, tall],
        ),
        out_shape=[jax.ShapeDtypeStruct((total, wide), LOW)] * 3
        + [jax.ShapeDtypeStruct((wide, total), LOW)] * 2,
        compiler_params=pltpu.CompilerParams(vmem_limit_bytes=48 << 20),
        cost_estimate=pl.CostEstimate(
            flops=2 * total * width * 3 * wide,
            bytes_accessed=2 * total * (width + 5 * wide) + 6 * width * wide,
            transcendentals=0,
        ),
        name="project",
    )(info, rows, wide_w, wide_bias, cosine, sine, *earlier)


def attend_kernel(heads, tile, info_ref, q_ref, k_ref, vt_ref, row_ids, column_ids, *refs):
    out_ref, lse_ref, acc_ref = refs[-3:]
    block = pl.program_id(0)
    first = info_ref[1 + block]
    last = info_ref[1 + pl.num_programs(0) + block]
    acc_ref[...] = jnp.zeros_like(acc_ref)
    mine = row_ids[0]

    def step(index, carry):
        start = pl.multiple_of(index * tile, tile)
        theirs = column_ids[pl.ds(start, tile), :]
        allowed = theirs == mine
        fresh = []
        for head in range(heads):
            lanes = slice(head * LANES, (head + 1) * LANES)
            top, summed = carry[head]
            scores = nt(k_ref[pl.ds(start, tile), lanes], q_ref[:, lanes])
            scores = jnp.where(allowed, scores, masked_score)
            higher = jnp.maximum(top, jnp.max(scores, axis=0, keepdims=True))
            shrink = jnp.exp2(top - higher)
            expo = jnp.exp2(scores - higher)
            summed = summed * shrink + jnp.sum(expo, axis=0, keepdims=True)
            part = nn(vt_ref[lanes, pl.ds(start, tile)], expo.astype(LOW))
            acc_ref[lanes, :] = acc_ref[lanes, :] * shrink + part
            fresh.append((higher, summed))
        return tuple(fresh)

    blank = (jnp.full((1, tile), masked_score, FULL), jnp.zeros((1, tile), FULL))
    done = lax.fori_loop(first, last, step, (blank,) * heads)
    for head in range(heads):
        lanes = slice(head * LANES, (head + 1) * LANES)
        top, summed = done[head]
        out_ref[:, lanes] = (acc_ref[lanes, :] / summed).T.astype(LOW)
        lse_ref[0, head : head + 1, :] = top + jnp.log2(summed)


def attend(info, query, keys, values_t, row_ids, column_ids, heads, group, earlier):
    total = query.shape[0]
    wide = heads * LANES
    blocks, _, tile = row_ids.shape

    return pl.pallas_call(
        functools.partial(attend_kernel, heads, tile),
        grid_spec=pltpu.PrefetchScalarGridSpec(
            num_scalar_prefetch=1,
            grid=(blocks,),
            in_specs=[
                pl.BlockSpec((tile, wide), lambda b, info: (b, group)),
                pl.BlockSpec((total, wide), lambda b, info: (0, group)),
                pl.BlockSpec((wide, total), lambda b, info: (group, 0)),
                pl.BlockSpec((1, 1, tile), lambda b, info: (b, 0, 0)),
                pl.BlockSpec((total, 1), lambda b, info: (0, 0)),
            ]
            + [pl.BlockSpec(memory_space=pl.ANY)] * len(earlier),
            out_specs=[
                pl.BlockSpec((tile, wide), lambda b, info: (b, 0)),
                pl.BlockSpec((1, heads, tile), lambda b, info: (b, 0, 0)),
            ],
            scratch_shapes=[pltpu.VMEM((wide, tile), FULL)],
        ),
        out_shape=[
            jax.ShapeDtypeStruct((total, wide), LOW),
            jax.ShapeDtypeStruct((blocks, heads, tile), FULL),
        ],
        compiler_params=pltpu.CompilerParams(vmem_limit_bytes=48 << 20),
        cost_estimate=pl.CostEstimate(
            flops=2 * total * total * wide, bytes_accessed=8 * total * wide, transcendentals=total * total * heads // 2
        ),
        name="attend",
    )(info, query, keys, values_t, row_ids, column_ids, *earlier)


def attend_back_kernel(
    heads,
    tile,
    members,
    info_ref,
    q_ref,
    k_ref,
    v_ref,
    kt_ref,
    do_ref,
    o_ref,
    lse_ref,
    row_ids,
    column_ids,
    cos_ref,
    sin_ref,
    *refs,
):
    out_ref, inner_ref, qt_ref, dk_ref, dv_ref = refs[-5:]
    block = pl.program_id(0)
    blocks = pl.num_programs(0)
    me = info_ref[0]
    first = info_ref[1 + block]
    last = info_ref[1 + blocks + block]
    wide = heads * LANES

    def place(b):
        return pl.multiple_of(b * tile, tile)

    def home(b):
        return pl.multiple_of(((b % 2) * members + ((b // 2) ^ me)) * tile, tile)

    def unrotate(value, b):
        where = pl.ds(home(b), tile)
        return value * cos_ref[where, :] - pltpu.roll(value, LANES // 2, 1) * sin_ref[where, :]

    @pl.when(block == 0)
    def _():
        qt_ref[...] = jnp.zeros_like(qt_ref)

        def fill(b, carry):
            where = pl.ds(place(b), tile)
            for head in range(heads):
                lanes = slice(head * LANES, (head + 1) * LANES)
                both = o_ref[where, lanes].astype(FULL) * do_ref[where, lanes].astype(FULL)
                inner_ref[b, head : head + 1, :] = jnp.sum(both.T, axis=0, keepdims=True)
            return carry

        lax.fori_loop(0, blocks, fill, 0)

    dk_ref[...] = jnp.zeros_like(dk_ref)
    dv_ref[...] = jnp.zeros_like(dv_ref)
    here = pl.ds(place(block), tile)
    theirs = column_ids[pl.ds(pl.multiple_of(block * tile, tile), tile), :]

    def step(index, carry):
        where = pl.ds(place(index), tile)
        allowed = theirs == row_ids[index]
        for head in range(heads):
            lanes = slice(head * LANES, (head + 1) * LANES)
            query = q_ref[where, lanes]
            grad = do_ref[where, lanes]
            scores = nt(k_ref[here, lanes], query)
            scores = jnp.where(allowed, scores, masked_score)
            probs = jnp.exp2(scores - lse_ref[index, head : head + 1, :])
            prob_grad = nt(v_ref[here, lanes], grad)
            score_grad = (probs * (prob_grad - inner_ref[index, head : head + 1, :])).astype(LOW)
            dv_ref[:, lanes] += nn(probs.astype(LOW), grad)
            dk_ref[:, lanes] += nn(score_grad, query)
            qt_ref[lanes, where] += nn(kt_ref[lanes, here], score_grad)
        return carry

    lax.fori_loop(first, last, step, 0)
    rows = pl.ds(home(block), tile)
    for head in range(heads):
        lanes = slice(head * LANES, (head + 1) * LANES)
        key_grad = unrotate(dk_ref[:, lanes] * math.log(2.0), block)
        out_ref[rows, wide + head * LANES : wide + (head + 1) * LANES] = key_grad.astype(LOW)
        out_ref[rows, 2 * wide + head * LANES : 2 * wide + (head + 1) * LANES] = dv_ref[:, lanes].astype(LOW)

    @pl.when(block == blocks - 1)
    def _():
        def spill(b, carry):
            for head in range(heads):
                lanes = slice(head * LANES, (head + 1) * LANES)
                query_grad = qt_ref[lanes, pl.ds(place(b), tile)].T * HD ** (-0.5)
                out_ref[pl.ds(home(b), tile), lanes] = unrotate(query_grad, b).astype(LOW)
            return carry

        lax.fori_loop(0, blocks, spill, 0)


def attend_back(info, query, keys, values, keys_t, grad, attended, logs, row_ids, column_ids, cosine, sine, members, heads, group, earlier):
    total = query.shape[0]
    wide = heads * LANES
    blocks, _, tile = row_ids.shape

    def whole(*shape):
        return pl.BlockSpec(shape, lambda b, info: (0,) * len(shape), pipeline_mode=pl.Buffered(1))

    flat = pl.BlockSpec((total, wide), lambda b, info: (0, group), pipeline_mode=pl.Buffered(1))
    tall = pl.BlockSpec((wide, total), lambda b, info: (group, 0), pipeline_mode=pl.Buffered(1))

    return pl.pallas_call(
        functools.partial(attend_back_kernel, heads, tile, members),
        grid_spec=pltpu.PrefetchScalarGridSpec(
            num_scalar_prefetch=1,
            grid=(blocks,),
            in_specs=[
                flat,
                flat,
                flat,
                tall,
                flat,
                whole(total, wide),
                whole(blocks, heads, tile),
                whole(blocks, 1, tile),
                whole(total, 1),
                whole(total, LANES),
                whole(total, LANES),
            ]
            + [pl.BlockSpec(memory_space=pl.ANY)] * len(earlier),
            out_specs=whole(total, 3 * wide),
            scratch_shapes=[
                pltpu.VMEM((blocks, heads, tile), FULL),
                pltpu.VMEM((wide, total), FULL),
                pltpu.VMEM((tile, wide), FULL),
                pltpu.VMEM((tile, wide), FULL),
            ],
        ),
        out_shape=jax.ShapeDtypeStruct((total, 3 * wide), LOW),
        compiler_params=pltpu.CompilerParams(vmem_limit_bytes=56 << 20),
        cost_estimate=pl.CostEstimate(
            flops=5 * total * total * wide, bytes_accessed=18 * total * wide, transcendentals=total * total * heads // 2
        ),
        name="attend_back",
    )(
        info, query, keys, values, keys_t, grad, attended, logs, row_ids, column_ids, cosine, sine, *earlier
    )


def spread_matrix(shards, slots, heads_each, turned):
    heads = shards * heads_each
    out = np.zeros((shards, slots, heads_each, HD, slots, heads, LANES), np.float32)
    half = HD // 2
    for shard in range(shards):
        for slot in range(slots):
            for head in range(heads_each):
                for j in range(HD):
                    lane = j
                    if turned and slot < 2 and j >= half:
                        lane = LANES // 2 + j - half
                    out[shard, slot, head, j, slot, shard * heads_each + head, lane] = 1.0
    return out.reshape(shards * slots * heads_each * HD, slots * heads * LANES)


def local(
    activations,
    cotangent,
    lengths,
    positions,
    weights,
    first_moment,
    second_moment,
    vectors,
    vector_first,
    vector_second,
):
    tokens, width = activations.shape
    depth, slots, columns = weights.shape
    half = tokens // 2
    shards = lax.axis_size("zh")
    ys = lax.axis_size("y")
    xs = lax.axis_size("x")
    members = 2 * ys
    heads_each = columns // HD
    heads = shards * heads_each
    x, c, zh, zl, y = (lax.axis_index(a) for a in ("x", "c", "zh", "zl", "y"))
    me = zl * ys + y
    members_of = shards * members
    four = 4 * columns
    everyone = ("zh", "zl", "y", "x", "c")

    inputs = activations.astype(FULL)
    early_norm = layer_norm(inputs, vectors[0], vectors[1]).astype(LOW)

    low = weights.astype(LOW)
    lift = jnp.concatenate([low[:, 4:8, :].reshape(depth, four), low[:, 3, :]], axis=1)
    down = low[:, 8:12, :].reshape(depth, four)
    lift_all = lax.all_gather(lift, everyone, axis=0, tiled=True)
    lift_all = lift_all.reshape(members_of, width, four + columns)
    down_w = lax.all_gather(down, everyone, axis=0, tiled=True)
    down_w = down_w.reshape(members_of, width, four)
    lift_w = lift_all[:, :, :four]
    out_w = jnp.concatenate(
        [lift_all[h * members + m, :, four:] for m in range(members) for h in range(shards)], axis=1
    )

    part = jnp.concatenate(gather(early_norm[:half], "y"), axis=0)
    rows_a = jnp.concatenate(gather(part, "zl"), axis=0)
    part = jnp.concatenate(gather(early_norm[half:], "zl"), axis=0).reshape(2, half, width)
    rows_b = jnp.stack(gather(part, "y"), axis=1).reshape(members * half, width)
    early_rows = jnp.concatenate([rows_a, rows_b], axis=0)

    qkv = low[:, 0:3, :].reshape(depth, 3 * columns)
    qkv = jnp.concatenate(settle(gather(qkv, "zh"), zh), axis=1)
    qkv = jnp.stack(settle(gather(qkv, "x"), x), axis=0)
    qkv = jnp.stack(settle(gather(qkv, "c"), c), axis=1).reshape(width, shards * 3 * columns)
    spread = spread_matrix(shards, 3, heads_each, True)
    spread_low = jnp.asarray(spread, LOW)
    wide_w = nn(qkv, spread_low).astype(LOW)
    shard_of = jnp.arange(shards) * members + me
    qkv_bias = jnp.take(vectors[6:9].reshape(3, -1, columns), shard_of, axis=1)
    qkv_bias = jnp.swapaxes(qkv_bias, 0, 1).reshape(1, -1)
    wide_bias = lax.dot(qkv_bias, jnp.asarray(spread), precision=lax.Precision.HIGHEST)

    counts = lax.dynamic_index_in_dim(lengths, zh, 0, keepdims=False)
    ends = jnp.cumsum(counts)
    spots = jnp.arange(SEQ, dtype=jnp.int32)
    ids = jnp.sum((spots[:, None] >= ends[None, :]).astype(jnp.int32), axis=1)
    blocks = 2 * members
    id_blocks = ids.reshape(blocks, half)
    low_spot = jnp.sum((ids[None, :] < id_blocks[:, :1]).astype(jnp.int32), axis=1)
    high_spot = jnp.sum((ids[None, :] <= id_blocks[:, -1:]).astype(jnp.int32), axis=1)
    info = jnp.concatenate(
        [me.reshape(1).astype(jnp.int32), low_spot // half, (high_spot + half - 1) // half]
    ).astype(jnp.int32)
    row_ids = ids.reshape(blocks, 1, half)
    column_ids = ids.reshape(SEQ, 1)

    spot = lax.dynamic_slice_in_dim(positions, zh * SEQ, SEQ, 1).reshape(2, members, 2, half)
    spot = jnp.take(spot, me ^ jnp.arange(members), axis=1)
    spot = jnp.swapaxes(spot, 1, 2).reshape(2, SEQ).astype(FULL)
    quarter = HD // 4
    freq = 10000.0 ** (-jnp.arange(quarter, dtype=FULL) * 4.0 / HD)
    angle = jnp.concatenate([spot[0][:, None] * freq, spot[1][:, None] * freq], axis=1)
    cosine, sine = jnp.cos(angle), jnp.sin(angle)
    gap = jnp.zeros((SEQ, LANES // 2 - HD // 2), FULL)
    cosine = jnp.concatenate([cosine, gap, cosine, gap], axis=1)
    sine = jnp.concatenate([-sine, gap, sine, gap], axis=1)

    query, keys, values, keys_t, values_t = project(
        info, early_rows, wide_w, wide_bias, cosine, sine, members, heads, []
    )
    groups = 2
    few = heads // groups
    attended_wide, logs = [], []
    for group in range(groups):
        some, log = attend(
            info, query, keys, values_t, row_ids, column_ids, few, group, logs[:1]
        )
        attended_wide.append(some)
        logs.append(log)

    squeeze = jnp.asarray(spread_matrix(shards, 1, heads_each, False).T, LOW)
    own = nn(attended_wide[0], squeeze[: few * LANES]) + nn(attended_wide[1], squeeze[few * LANES :])
    own = own.astype(LOW).reshape(members, tokens, shards * columns)
    own = lax.all_to_all(own, SQUARE, split_axis=0, concat_axis=0, tiled=True)
    attended = jnp.swapaxes(own, 0, 1).reshape(tokens, width)

    middle = inputs + nt(attended, out_w) + vectors[4]
    later_norm = layer_norm(middle, vectors[2], vectors[3]).astype(LOW)

    lift_bias = jnp.swapaxes(vectors[9:13].reshape(4, members_of, columns), 0, 1)
    lift_bias = lift_bias.reshape(members_of, 1, four)
    upper = jnp.einsum("nd,tdj->tnj", later_norm, lift_w, preferred_element_type=FULL) + lift_bias
    hidden = quick_gelu(upper).astype(LOW)

    mixed = jnp.einsum("tnj,tij->ni", hidden, down_w, preferred_element_type=FULL)
    block_output = (middle + mixed + vectors[5]).astype(LOW)

    def split(value):
        value = value.reshape(tokens, xs, 2, depth)
        parts = [value[:, :, i].reshape(tokens, xs * depth) for i in range(2)]
        return jnp.where(c == 0, parts[0], parts[1]), jnp.where(c == 0, parts[1], parts[0])

    def first_sum(left, right):
        mine, theirs = left
        theirs = jnp.einsum("ni,tnj->tij", theirs, right, preferred_element_type=FULL)
        theirs = swap(theirs.astype(LOW), "c", 1).astype(FULL)
        mine = jnp.einsum("ni,tnj->tij", mine, right, preferred_element_type=FULL)
        return (mine + theirs).astype(LOW)

    step = depth // CHUNKS

    def chunk(value, k):
        value = value.reshape(2 * shards, ys, xs, CHUNKS, step, value.shape[-1])
        return value[:, :, :, k]

    def over_plane(value, order):
        first = scatter(value, order[0], 1 if order[0] == "y" else 2).astype(LOW)
        last = scatter(first, order[1], 1).astype(LOW)
        return first, last

    cot_parts = split(cotangent)
    down_sum = first_sum(cot_parts, hidden)
    down_plane = [over_plane(chunk(down_sum, 0), "yx"), over_plane(chunk(down_sum, 1), "xy")]
    down_grad = jnp.concatenate([scatter(last, LINE, 0) for _, last in down_plane], axis=0)

    hidden_grad = jnp.einsum("ni,tij->tnj", cotangent, down_w, preferred_element_type=FULL)
    upper_grad = jax.vjp(quick_gelu, upper)[1](hidden_grad)[0].astype(LOW)
    lift_sum = first_sum(split(later_norm), upper_grad)
    lift_plane = [over_plane(chunk(lift_sum, 0), "xy"), over_plane(chunk(lift_sum, 1), "xy")]
    lift_grad = jnp.concatenate([scatter(last, LINE, 0) for _, last in lift_plane], axis=0)

    later_grad = jnp.einsum("tnj,tdj->nd", upper_grad, lift_w, preferred_element_type=FULL)

    cot_full = cotangent.astype(FULL)
    middle_part, gain_second, shift_second = jax.vjp(layer_norm, middle, vectors[2], vectors[3])[1](
        later_grad
    )
    middle_grad = cot_full + middle_part
    middle_low = tie(middle_grad.astype(LOW), [first for first, _ in down_plane])

    attended_grad = nn(middle_low, out_w).astype(LOW)
    row_grad = jnp.swapaxes(attended_grad.reshape(tokens, members, shards * columns), 0, 1)
    row_grad = lax.all_to_all(row_grad, SQUARE, split_axis=0, concat_axis=0, tiled=True)
    row_grad = nt(row_grad.reshape(SEQ, shards * columns), squeeze).astype(LOW)

    mine, theirs = split(middle_low)
    out_sum = (tn(mine, attended) + swap(tn(theirs, attended).astype(LOW), "c", 1).astype(FULL)).astype(LOW)
    out_sum = scatter(out_sum.reshape(xs, depth, width), "x", 0).astype(LOW)
    out_sum = out_sum.reshape(depth, 2, ys, shards, columns)
    out_sum = jnp.moveaxis(out_sum, (3, 1, 2), (0, 1, 2)).reshape(2 * shards, ys, depth, columns)
    out_sum = scatter(out_sum, "y", 1).astype(LOW)
    out_grad = scatter(out_sum, LINE, 0)

    heads_grad = []
    waits = [
        leaves((lift_plane[0][0], [last for _, last in down_plane])),
        leaves((lift_plane[1][0], down_grad)),
    ]
    for group in range(groups):
        heads_grad.append(
            attend_back(
                info,
                query,
                keys,
                values,
                keys_t,
                row_grad,
                attended_wide[group],
                logs[group],
                row_ids,
                column_ids,
                cosine,
                sine,
                members,
                few,
                group,
                waits[group] + heads_grad[:1],
            )
        )
    pack = spread_low.reshape(-1, 3, groups, few * LANES)
    pack = [pack[:, :, group].reshape(-1, 3 * few * LANES) for group in range(groups)]
    heads_grad = (nt(heads_grad[0], pack[0]) + nt(heads_grad[1], pack[1])).astype(LOW)
    heads_grad = tie(heads_grad, [last for _, last in lift_plane])

    partial = nt(heads_grad, qkv).astype(LOW).reshape(2, 2, ys, half, width)
    some = scatter_near([partial[0, l] for l in range(2)], "zl")
    some_a = scatter_near([some[j] for j in range(ys)], "y")
    some = scatter_near([partial[1, :, j] for j in range(ys)], "y")
    some_b = scatter_near([some[l] for l in range(2)], "zl")
    early_grad = jnp.concatenate([some_a, some_b], axis=0)

    qkv_grad = tn(early_rows, heads_grad).astype(LOW).reshape(xs, 2, depth, shards * 3 * columns)
    qkv_grad = scatter(qkv_grad, "c", 1).astype(LOW)
    qkv_grad = scatter(qkv_grad, "x", 0).astype(LOW)
    qkv_grad = jnp.swapaxes(qkv_grad.reshape(depth, shards, 3 * columns), 0, 1)
    qkv_grad = scatter(qkv_grad, "zh", 0)

    input_part, gain_first, shift_first = jax.vjp(layer_norm, inputs, vectors[0], vectors[1])[1](
        early_grad
    )
    input_grad = (middle_grad + input_part).astype(LOW)

    owned = jnp.concatenate([qkv_grad, out_grad, lift_grad, down_grad], axis=1)
    owned = owned.reshape(depth, slots, columns)

    ffn_sum = jnp.sum(upper_grad, axis=1, dtype=FULL).reshape(members_of, 4, columns)
    ffn_bias = jnp.swapaxes(ffn_sum, 0, 1).reshape(4, width)
    ready = jnp.stack(
        [gain_second, shift_second, jnp.sum(middle_grad, axis=0), jnp.sum(cot_full, axis=0)]
    )
    ready = sum_everywhere(jnp.concatenate([ready, ffn_bias], axis=0))
    heads_sum = jnp.sum(heads_grad, axis=0, dtype=FULL).reshape(shards, 3, columns)
    placed = jnp.where(
        (jnp.arange(members) == me)[None, None, :, None],
        jnp.swapaxes(heads_sum, 0, 1)[:, :, None, :],
        0.0,
    ).reshape(3, width)
    late = sum_everywhere(jnp.concatenate([jnp.stack([gain_first, shift_first]), placed], axis=0))
    vector_grad = jnp.concatenate([late[0:2], ready[0:4], late[2:5], ready[4:8]], axis=0)

    next_first, next_second, next_weights = adam_update(
        weights, owned, first_moment, second_moment, rate_matrix, decay_matrix
    )
    next_vector_first, next_vector_second, next_vectors = adam_update(
        vectors, vector_grad, vector_first, vector_second, rate_vector, 0.0
    )
    return (
        block_output,
        input_grad,
        next_first,
        next_second,
        next_weights,
        next_vector_first,
        next_vector_second,
        next_vectors,
    )


def solution(mesh):
    fsdp = mesh.shape["fsdp"]
    tp = mesh.shape["tp"]
    outer = ("x", "c")
    inner = ("zh", "zl", "y")

    def run(*args):
        rows = args[2].shape[0] // fsdp
        fine = Mesh(
            mesh.devices.reshape(fsdp // 2, 2, rows, 2, tp // (2 * rows)), outer + inner
        )
        patches = P(outer + inner, None)
        matrix = P(outer, None, inner)
        in_specs = (
            patches,
            patches,
            P(outer, None),
            P(None, outer),
            matrix,
            matrix,
            matrix,
            P(),
            P(),
            P(),
        )
        out_specs = (patches, patches, matrix, matrix, matrix, P(), P(), P())
        return jax.shard_map(
            local, mesh=fine, in_specs=in_specs, out_specs=out_specs, check_vma=False
        )(*args)

    return run
```

time: 2090 us -> 804 us (0.38)
  waiting for transfers between devices: 1430 us -> 260 us
  matrix products: 298 us -> 134 us
  Pallas kernels: 0 us -> 142 us
  local copies, waits for them, and re-layouts: 183 us -> 104 us
  starting transfers between devices: 0.63 us -> 72.3 us
  other arithmetic: 115 us -> 71.4 us
  loops' own time: 39.6 us -> 0 us
    reduce_scatter x4 -> x0, waiting for transfers between devices: 682 us -> none  [the longest x2 352 us: sum_branch(): lax.psum_scatter(term(jnp.int32(0), left.shape[0] // lax.axis_size('tp')...]
    all_gather x5 -> x2, waiting for transfers between devices: 589 us -> 17.1 us  [the longest x1 17.1 us: local(): down_w = lax.all_gather(down, everyone, axis=0, tiled=True)]
    ppermute x0 -> x52, waiting for transfers between devices: none -> 235 us  [swap(): lax.ppermute(value, axis, [(i, i ^ far) for i in range(lax.axis_size(axis...]
    pallas_call x0 -> x7, Pallas kernels: none -> 142 us  [the longest x2 68.3 us: attend_back(): pl.pallas_call(functools.partial(attend_back_kernel, heads, tile, members...]
    psum x1 -> x0, waiting for transfers between devices: 119 us -> none  [local(): lax.psum(jnp.concatenate([whole_rows, placed, ffn_bias], axis=0), ('fsdp'...]
    dot_general x63 -> x21, matrix products: 247 us -> 134 us  [the longest x12 51.2 us: dot(): return lax.dot_general(a, b, (dims, ((), ())), preferred_element_type=FULL)]
    ppermute x0 -> x52, starting transfers between devices: none -> 61.1 us  [swap(): lax.ppermute(value, axis, [(i, i ^ far) for i in range(lax.axis_size(axis...]
    dynamic_update_slice x10 -> x0, local copies, waits for them, and re-layouts: 56.2 us -> none  [the longest x8 55.6 us: attention_backward(): lax.map(row_grads, jnp.arange(count_rows, dtype=jnp.int32))]
  transfers between devices with their start and end apart: 11 -> 56, of which waited for: 11 -> 28; matrix products, arithmetic and copies ran while one was open for 6% -> 36% of each run, Pallas kernels for 0% -> 18%
where the time goes in v1:
time: 804 us; the launch traced here: 800 us
  waiting for transfers between devices  260 us (32%)
  Pallas kernels  142 us (18%)
  matrix products  134 us (17%)
  local copies, waits for them, and re-layouts  104 us (13%)
  starting transfers between devices  72.3 us (9%)
  other arithmetic  71.4 us (9%)
  between operations  15.8 us (2%)
    ppermute x52, waiting for transfers between devices, swap(): lax.ppermute(value, axis, [(i, i ^ far) for i in range(lax.axis_size(axis...  235 us
    pallas_call x2, Pallas kernels, attend_back(): pl.pallas_call(functools.partial(attend_back_kernel, heads, tile, members...  68.3 us
    ppermute x52, starting transfers between devices, swap(): lax.ppermute(value, axis, [(i, i ^ far) for i in range(lax.axis_size(axis...  61.1 us
    pallas_call x2, Pallas kernels, attend(): pl.pallas_call(functools.partial(attend_kernel, heads, tile), grid_spec=p...  59.2 us
    dot_general x12, matrix products, dot(): return lax.dot_general(a, b, (dims, ((), ())), preferred_element_type=FULL)  51.2 us
    unnamed x174, local copies, waits for them, and re-layouts  17.7 us
    all_gather x1, waiting for transfers between devices, local(): down_w = lax.all_gather(down, everyone, axis=0, tiled=True)  17.1 us
  transfers between devices with their start and end apart: 56, of which 28 were waited for; matrix products, arithmetic and copies ran while one was open for 36% of the time, Pallas kernels for 18%

profile of v1, /device:TPU:8, one launch (start us, length us, event | category | flops | bytes accessed | tf_op | source)
XLA Modules:
  0.0 800.2 jit_solution(13251334254176402218)
XLA Ops:
  22.0 2.7 collective-permute-start.4
  31.7 5.6 fusion.91.bias_ref
  37.3 19.5 %collective-permute-done.4 = bf16[320,480]{1,0:T(8,128)(2,1)S(1)} collective-permute-done((bf16[320,480]{1,0:T(8,128)(2,1)S(1)}, bf16[320,480]{1,0:T(8,128)(2,1)S(1)}, u32[]{:S(2)}, u32[]{:S(2)}) %collective-permute-start.4) | collective-permute-done | bytes 307232 | tf_op jit(solution)/shard_map/ppermute | solution.py:70
  66.1 19.2 %collective-permute-done.5 = bf16[320,960]{1,0:T(8,128)(2,1)S(1)} collective-permute-done((bf16[320,960]{1,0:T(8,128)(2,1)S(1)}, bf16[320,960]{1,0:T(8,128)(2,1)S(1)}, u32[]{:S(2)}, u32[]{:S(2)}) %collective-permute-start.5) | collective-permute-done | bytes 614432 | tf_op jit(solution)/shard_map/ppermute | solution.py:70
  88.2 10.1 %collective-permute-done.3 = bf16[2,256,1280]{2,1,0:T(8,128)(2,1)} collective-permute-done((bf16[2,256,1280]{2,1,0:T(8,128)(2,1)}, bf16[2,256,1280]{2,1,0:T(8,128)(2,1)}, u32[]{:S(2)}, u32[]{:S(2)}) %collective-permute-start.3) | collective-permute-done | bytes 1310752 | tf_op jit(solution)/shard_map/ppermute | solution.py:70
  100.4 13.1 %collective-permute-done.1 = bf16[512,1280]{1,0:T(8,128)(2,1)} collective-permute-done((bf16[512,1280]{1,0:T(8,128)(2,1)}, bf16[512,1280]{1,0:T(8,128)(2,1)}, u32[]{:S(2)}, u32[]{:S(2)}) %collective-permute-start.1) | collective-permute-done | bytes 1310752 | tf_op jit(solution)/shard_map/ppermute | solution.py:70
  113.6 5.0 pad_maximum_fusion.rows_ref
  123.3 5.8 convolution_convert_fusion.w_ref
  129.2 14.9 %project.1 = (bf16[2048,512]{1,0:T(8,128)(2,1)S(1)}, bf16[2048,512]{1,0:T(8,128)(2,1)}, bf16[2048,512]{1,0:T(8,128)(2,1)}, bf16[512,2048]{1,0:T(8,128)(2,1)}, bf16[512,2048]{1,0:T(8,128)(2,1)}) custom-call(s32[17]{0:T(128)S(1)} %pad_add_fusion.info_ref, bf16[2048,1280]{1,0:T(8,128)(2,1)} %pad_maximum_fusion.rows_ref, ...), custom_call_target="tpu_custom_call" | custom-call | flops 8053063680 | bytes 19660800 | tf_op jit(solution)/shard_map/project/pallas_call | solution.py:165
  144.0 29.6 %attend.2 = (bf16[2048,256]{1,0:T(8,128)(2,1)S(1)}, f32[8,2,256]{2,1,0:T(2,128)S(1)}) custom-call(s32[17]{0:T(128)S(1)} %pad_add_fusion.info_ref, bf16[2048,512]{1,0:T(8,128)(2,1)S(1)} %get-tuple-element.17.q_ref, bf16[2048,512]{1,0:T(8,128)(2,1)} %get-tuple-element.18.k_ref, bf16[512,2048]{1,0:T(8,128)(2,1)} %get-tuple-element.19.vt_ref, ...), custom_call_target="tpu_custom_call" | custom-call | flops 2147483648 | bytes 4194304 | tf_op jit(solution)/shard_map/attend/pallas_call | solution.py:233
  173.7 29.6 %attend.3 = (bf16[2048,256]{1,0:T(8,128)(2,1)S(1)}, f32[8,2,256]{2,1,0:T(2,128)S(1)}) custom-call(s32[17]{0:T(128)S(1)} %pad_add_fusion.info_ref, bf16[2048,512]{1,0:T(8,128)(2,1)S(1)} %get-tuple-element.17.q_ref, bf16[2048,512]{1,0:T(8,128)(2,1)} %get-tuple-element.18.k_ref, bf16[512,2048]{1,0:T(8,128)(2,1)} %get-tuple-element.19.vt_ref, ...), custom_call_target="tpu_custom_call" | custom-call | flops 2147483648 | bytes 4194304 | tf_op jit(solution)/shard_map/attend/pallas_call | solution.py:233
  206.3 5.4 all-to-all-start
  214.5 4.7 slice_bitcast_fusion.6
  219.3 8.1 %concatenate.61 = bf16[1280,1280]{1,0:T(8,128)(2,1)} concatenate(bf16[1280,160]{1,0:T(8,128)(2,1)} %get-tuple-element.62, bf16[1280,160]{1,0:T(8,128)(2,1)} %get-tuple-element.61, bf16[1280,160]{1,0:T(8,128)(2,1)} %get-tuple-element.60, bf16[1280,160]{1,0:T(8,128)(2,1)} %get-tuple-element.59, bf16[1280,160]{1,0:T(8,128)(2,1)} %get-tuple-element.58, ...), dimensions={1} | concatenate | bytes 6553600 | tf_op jit(solution)/shard_map/concatenate | solution.py:458
  227.4 7.6 all-to-all-done
  235.0 4.4 fusion.90
  244.3 13.8 %fusion.14 = (bf16[8,512,640]{2,1,0:T(8,128)(2,1)S(1)}, f32[8,640,512]{1,2,0:T(8,128)}) fusion(f32[8,640]{1,0:T(8,128)S(1)} %add.452, bf16[8,1280,800]{2,1,0:T(8,128)(2,1)} %bitcast.376, bf16[512,1280]{1,0:T(8,128)(2,1)} %add_convert_fusion.2), kind=kOutput, calls=%fused_computation.24 | convolution fusion | flops 6729236480 | bytes 30167040 | tf_op jit(solution)/shard_map/nd,tdj->tnj/dot_general | solution.py:529
  258.1 5.5 convert_bitcast_fusion.1
  264.6 17.1 %all-gather.5.cloned.1.call-done = bf16[10240,640]{1,0:T(8,128)(2,1)} async-done(((bf16[320,640]{1,0:T(8,128)(2,1)}), bf16[10240,640]{1,0:T(8,128)(2,1)}) %all-gather.5.cloned.1.call-update) | async-done | bytes 13107216 | tf_op jit(solution)/shard_map/all_gather | solution.py:455
  281.7 14.7 %convert_reduce_fusion = (f32[8,640]{1,0:T(8,128)S(1)}, bf16[8,512,640]{2,1,0:T(8,128)(2,1)S(1)}) fusion(f32[8,640,512]{1,2,0:T(8,128)} %get-tuple-element.126, f32[8,640]{1,0:T(8,128)S(1)} %add.452, bf16[8,1280,640]{2,1,0:T(8,128)(2,1)} %bitcast.393, bf16[512,1280]{1,0:T(8,128)(2,1)S(1)} %copy-done.24), kind=kOutput, calls=%fused_computation.23 | convolution fusion | flops 6750202880 | bytes 30187520 | tf_op jit(solution)/shard_map/ni,tij->tnj/dot_general | solution.py:563
  296.4 5.5 convert_bitcast_fusion
  302.2 10.3 %multiply_reduce_fusion = (f32[1280]{0:T(1024)S(1)}, f32[512]{0:T(512)S(1)}, f32[1280]{0:T(1024)S(1)}, f32[512,1280]{1,0:T(8,128)S(1)}) fusion(f32[512,1280]{1,0:T(8,128)S(1)} %copy-done.17, f32[512]{0:T(512)S(1)} %fusion.69, f32[512]{0:T(512)S(1)} %broadcast_multiply_fusion.2, f32[1280]{0:T(1024)S(1)} %get-tuple-element.35, ...), kind=kOutput, calls=%fused_computation.82 | convolution fusion | flops 6716126208 | bytes 23614464 | tf_op jit(solution)/shard_map/tnj,tdj->nd/dot_general | solution.py:569
  313.4 13.6 %fusion.29 = bf16[512,1280]{1,0:T(8,128)(2,1)} fusion(f32[512,1280]{1,0:T(8,128)S(1)} %copy-done.17, bf16[8,512,640]{2,1,0:T(8,128)(2,1)} %copy-done.79, bf16[8,1280,640]{2,1,0:T(8,128)(2,1)} %bitcast.394, f32[1280]{0:T(1024)S(1)} %copy-done.71), kind=kOutput, calls=%fused_computation.62 | convolution fusion | flops 6712852480 | bytes 22287360 | tf_op jit(solution)/shard_map/tnj,tij->ni/dot_general | solution.py:532
  327.1 7.7 fusion.1
  343.6 5.8 fusion
  357.8 3.4 constant_dynamic-slice_fusion.7
  363.1 13.7 %collective-permute-done.8 = bf16[4,2,160,640]{3,2,0,1:T(8,128)(2,1)} collective-permute-done((bf16[4,2,160,640]{3,2,0,1:T(8,128)(2,1)}, bf16[4,2,160,640]{3,2,0,1:T(8,128)(2,1)}, u32[]{:S(2)}, u32[]{:S(2)}) %collective-permute-start.8) | collective-permute-done | bytes 1638432 | tf_op jit(solution)/shard_map/ppermute | solution.py:70
  388.9 5.2 convolution_convert_fusion.5
  396.5 5.7 all-to-all-start.1
  402.2 14.8 %collective-permute-done.14 = bf16[4,2,160,640]{3,2,0,1:T(8,128)(2,1)} collective-permute-done((bf16[4,2,160,640]{3,2,0,1:T(8,128)(2,1)}, bf16[4,2,160,640]{3,2,0,1:T(8,128)(2,1)}, u32[]{:S(2)}, u32[]{:S(2)}) %collective-permute-start.14) | collective-permute-done | bytes 1638432 | tf_op jit(solution)/shard_map/ppermute | solution.py:70
  423.7 28.5 %collective-permute-done.11 = bf16[4,2,160,640]{3,2,0,1:T(8,128)(2,1)} collective-permute-done((bf16[4,2,160,640]{3,2,0,1:T(8,128)(2,1)}, bf16[4,2,160,640]{3,2,0,1:T(8,128)(2,1)}, u32[]{:S(2)}, u32[]{:S(2)}) %collective-permute-start.11) | collective-permute-done | bytes 1638432 | tf_op jit(solution)/shard_map/ppermute | solution.py:70
  462.0 6.7 collective-permute-done.12
  470.2 6.5 collective-permute-done.21
  478.2 13.2 %collective-permute-done.22 = bf16[4,160,640]{2,1,0:T(8,128)(2,1)S(1)} collective-permute-done((bf16[4,160,640]{2,1,0:T(8,128)(2,1)S(1)}, bf16[4,160,640]{2,1,0:T(8,128)(2,1)S(1)}, u32[]{:S(2)}, u32[]{:S(2)}) %collective-permute-start.22) | collective-permute-done | bytes 819232 | tf_op jit(solution)/shard_map/ppermute | solution.py:70
  496.8 15.8 %collective-permute-done.17 = bf16[160,640]{1,0:T(8,128)(2,1)S(1)} collective-permute-done((bf16[160,640]{1,0:T(8,128)(2,1)S(1)}, bf16[160,640]{1,0:T(8,128)(2,1)S(1)}, u32[]{:S(2)}, u32[]{:S(2)}) %collective-permute-start.17) | collective-permute-done | bytes 204832 | tf_op jit(solution)/shard_map/ppermute | solution.py:70
  512.6 2.5 collective-permute-done.16
  515.2 3.3 collective-permute-start.39
  520.2 5.2 collective-permute-done.41
  525.4 7.3 collective-permute-done.40
  532.7 5.5 collective-permute-start.36
  552.2 2.6 convolution_convert_fusion.4.do_ref
  554.9 34.0 %attend_back.2.refs_2_ = bf16[2048,768]{1,0:T(8,128)(2,1)} custom-call(s32[17]{0:T(128)} %copy-done.11, bf16[2048,512]{1,0:T(8,128)(2,1)} %copy-done.5, bf16[2048,512]{1,0:T(8,128)(2,1)} %get-tuple-element.18.k_ref, bf16[2048,512]{1,0:T(8,128)(2,1)} %get-tuple-element.23.v_ref, bf16[512,2048]{1,0:T(8,128)(2,1)} %get-tuple-element.24.kt_ref, ...), custom_call_target="tpu_custom_call" | custom-call | flops 5368709120 | bytes 9437184 | tf_op jit(solution)/shard_map/attend_back/pallas_call | solution.py:367
  588.9 34.3 %attend_back.3 = bf16[2048,768]{1,0:T(8,128)(2,1)} custom-call(s32[17]{0:T(128)} %copy-done.11, bf16[2048,512]{1,0:T(8,128)(2,1)} %copy-done.5, bf16[2048,512]{1,0:T(8,128)(2,1)} %get-tuple-element.18.k_ref, bf16[2048,512]{1,0:T(8,128)(2,1)} %get-tuple-element.23.v_ref, bf16[512,2048]{1,0:T(8,128)(2,1)} %get-tuple-element.24.kt_ref, ...), custom_call_target="tpu_custom_call" | custom-call | flops 5368709120 | bytes 9437184 | tf_op jit(solution)/shard_map/attend_back/pallas_call | solution.py:367
  623.2 5.3 fusion.93
  628.6 4.8 convolution_add_fusion
  633.4 6.3 copy.337.refs_0_
  639.7 8.6 %convolution_convert_fusion.1 = bf16[2048,1280]{1,0:T(8,128)(2,1)S(1)} fusion(bf16[2048,960]{1,0:T(8,128)(2,1)} %tie.3, bf16[1280,960]{1,0:T(8,128)(2,1)} %bitcast.371), kind=kOutput, calls=%fused_computation.27 | convolution fusion | flops 5035786240 | bytes 11632640 | tf_op jit(solution)/shard_map/dot_general | solution.py:35
  656.2 8.6 %convolution_convert_fusion.2 = bf16[1280,960]{0,1:T(8,128)(2,1)} fusion(bf16[2048,960]{1,0:T(8,128)(2,1)S(1)} %copy-done.15, bf16[1024,1280]{1,0:T(8,128)(2,1)S(1)} %bitcast.354, bf16[512,1280]{1,0:T(8,128)(2,1)} %collective-permute-done.1, bf16[256,1280]{1,0:T(8,128)(2,1)} %collective-permute-done, bf16[256,1280]{1,0:T(8,128)(2,1)S(1)} %copy-done.40), kind=kOutput, calls=%fused_computation.42 | convolution fusion | flops 5055365120 | bytes 11632640 | tf_op jit(solution)/shard_map/dot_general | solution.py:35
  664.7 4.4 copy.340
  671.5 2.9 convert_reduce_fusion.1
  676.8 2.7 fusion.40
  679.6 2.9 copy.345
  685.3 13.2 %collective-permute-done.32 = bf16[4,320,160]{1,2,0:T(8,128)(2,1)S(1)} collective-permute-done((bf16[4,320,160]{1,2,0:T(8,128)(2,1)}, bf16[4,320,160]{1,2,0:T(8,128)(2,1)S(1)}, u32[]{:S(2)}, u32[]{:S(2)}) %collective-permute-start.32) | collective-permute-done | bytes 409632 | tf_op jit(solution)/shard_map/ppermute | solution.py:70
  701.8 4.9 collective-permute-start.35
  708.2 3.1 convert_add_fusion.8
  716.8 15.9 %collective-permute-done.26 = bf16[256,1280]{1,0:T(8,128)(2,1)S(1)} collective-permute-done((bf16[256,1280]{1,0:T(8,128)(2,1)S(1)}, bf16[256,1280]{1,0:T(8,128)(2,1)S(1)}, u32[]{:S(2)}, u32[]{:S(2)}) %collective-permute-start.26) | collective-permute-done | bytes 655392 | tf_op jit(solution)/shard_map/ppermute | solution.py:70
  738.4 2.7 convert_reduce_fusion.3
  741.2 8.3 %collective-permute-done.43 = f32[5,1280]{1,0:T(8,128)} collective-permute-done((f32[5,1280]{1,0:T(8,128)S(1)}, f32[5,1280]{1,0:T(8,128)}, u32[]{:S(2)}, u32[]{:S(2)}) %collective-permute-start.43) | collective-permute-done | bytes 25632 | tf_op jit(solution)/shard_map/ppermute | solution.py:70
  757.8 3.5 collective-permute-start.29
  762.2 3.3 collective-permute-done.49
  767.4 8.9 %collective-permute-done.46 = f32[5,1280]{1,0:T(8,128)S(1)} collective-permute-done((f32[5,1280]{1,0:T(8,128)S(1)}, f32[5,1280]{1,0:T(8,128)S(1)}, u32[]{:S(2)}, u32[]{:S(2)}) %collective-permute-start.46) | collective-permute-done | bytes 25632 | tf_op jit(solution)/shard_map/ppermute | solution.py:70
  776.4 3.5 collective-permute-start.51
  782.3 3.5 copy.348
  785.9 6.5 multiply_subtract_fusion
  (440 shorter events, 172.8 us)
Async XLA Ops:
  7.2 207.3 %all-gather.3.cloned.1.call-start = ((), (), s32[]{:S(2)}) async-start(), calls=%async_computation.2 | async-start | bytes 18923520 | tf_op jit(solution)/shard_map/all_gather | solution.py:453
  15.8 265.9 %all-gather.5.cloned.1.call-start = ((), (), s32[]{:S(2)}) async-start(), calls=%async_computation.3 | async-start | bytes 13516800 | tf_op jit(solution)/shard_map/all_gather | solution.py:455
  19.7 38.9 %collective-permute-start.2 = (bf16[256,1280]{1,0:T(8,128)(2,1)}, bf16[256,1280]{1,0:T(8,128)(2,1)}, u32[]{:S(2)}, u32[]{:S(2)}) collective-permute-start(bf16[256,1280]{1,0:T(8,128)(2,1)} %get-tuple-element.93), channel_id=1, source_target_pairs={{0,2},{2,0},{1,3},{3,1},{4,6},{6,4},{5,7},{7,5},{8,10},{10,8},{9,1... | collective-permute-start | bytes 1966088 | tf_op jit(solution)/shard_map/ppermute | solution.py:70
  19.8 42.8 %collective-permute-start = (bf16[256,1280]{1,0:T(8,128)(2,1)S(1)}, bf16[256,1280]{1,0:T(8,128)(2,1)}, u32[]{:S(2)}, u32[]{:S(2)}) collective-permute-start(bf16[256,1280]{1,0:T(8,128)(2,1)S(1)} %get-tuple-element.92), channel_id=1, source_target_pairs={{0,1},{1,0},{2,3},{3,2},{4,5},{5,4},{6,7},{7,6},{8,9},{9,8},{10,11... | collective-permute-start | bytes 1966088 | tf_op jit(solution)/shard_map/ppermute | solution.py:70
  22.0 34.8 %collective-permute-start.4 = (bf16[320,480]{1,0:T(8,128)(2,1)S(1)}, bf16[320,480]{1,0:T(8,128)(2,1)S(1)}, u32[]{:S(2)}, u32[]{:S(2)}) collective-permute-start(bf16[320,480]{1,0:T(8,128)(2,1)S(1)} %copy.299), channel_id=1, source_target_pairs={{0,4},{4,0},{1,5},{5,1},{2,6},{6,2},{3,7},{7,3},{8,12},{12,8},{9,1... | collective-permute-start | bytes 921608 | tf_op jit(solution)/shard_map/ppermute | solution.py:70
  25.1 148.6 %copy-start.8 = (s32[2048]{0:T(1024)}, s32[2048]{0:T(1024)S(1)}, u32[]{:S(2)}) copy-start(s32[2048]{0:T(1024)S(1)} %convert_reduce_fusion.4) | copy-start | bytes 24580
  57.1 28.2 %collective-permute-start.5 = (bf16[320,960]{1,0:T(8,128)(2,1)S(1)}, bf16[320,960]{1,0:T(8,128)(2,1)S(1)}, u32[]{:S(2)}, u32[]{:S(2)}) collective-permute-start(bf16[320,960]{1,0:T(8,128)(2,1)S(1)} %pad_maximum_fusion.13), channel_id=1, source_target_pairs={{0,16},{16,0},{1,17},{17,1},{2,18},{18,2},{3,19},{19,3},{4,20},{20... | collective-permute-start | bytes 1843208 | tf_op jit(solution)/shard_map/ppermute | solution.py:70
  61.1 37.2 %collective-permute-start.3 = (bf16[2,256,1280]{2,1,0:T(8,128)(2,1)}, bf16[2,256,1280]{2,1,0:T(8,128)(2,1)}, u32[]{:S(2)}, u32[]{:S(2)}) collective-permute-start(bf16[2,256,1280]{2,1,0:T(8,128)(2,1)} %bitcast.3), channel_id=1, source_target_pairs={{0,1},{1,0},{2,3},{3,2},{4,5},{5,4},{6,7},{7,6},{8,9},{9,8},{10,11... | collective-permute-start | bytes 3932168 | tf_op jit(solution)/shard_map/ppermute | solution.py:70
  64.8 48.7 %collective-permute-start.1 = (bf16[512,1280]{1,0:T(8,128)(2,1)}, bf16[512,1280]{1,0:T(8,128)(2,1)}, u32[]{:S(2)}, u32[]{:S(2)}) collective-permute-start(bf16[512,1280]{1,0:T(8,128)(2,1)} %pad_maximum_fusion.8), channel_id=1, source_target_pairs={{0,2},{2,0},{1,3},{3,1},{4,6},{6,4},{5,7},{7,5},{8,10},{10,8},{9,1... | collective-permute-start | bytes 3932168 | tf_op jit(solution)/shard_map/ppermute | solution.py:70
  66.1 63.1 %copy-start.3 = (f32[2048,128]{1,0:T(8,128)}, f32[2048,128]{1,0:T(8,128)S(1)}, u32[]{:S(2)}) copy-start(f32[2048,128]{1,0:T(8,128)S(1)} %get-tuple-element.94.sin_ref) | copy-start | bytes 3145732
  66.1 63.1 %copy-start.4 = (f32[2048,128]{1,0:T(8,128)}, f32[2048,128]{1,0:T(8,128)S(1)}, u32[]{:S(2)}) copy-start(f32[2048,128]{1,0:T(8,128)S(1)} %get-tuple-element.95.cos_ref) | copy-start | bytes 3145732
  87.7 30.8 %collective-permute-start.6 = (bf16[2,320,960]{2,1,0:T(8,128)(2,1)}, bf16[2,320,960]{2,1,0:T(8,128)(2,1)}, u32[]{:S(2)}, u32[]{:S(2)}) collective-permute-start(bf16[2,320,960]{2,1,0:T(8,128)(2,1)} %pad_maximum_fusion.10), channel_id=1, source_target_pairs={{0,8},{8,0},{1,9},{9,1},{2,10},{10,2},{3,11},{11,3},{4,12},{12,4},... | collective-permute-start | bytes 3686408 | tf_op jit(solution)/shard_map/ppermute | solution.py:70
  88.1 85.6 %copy-start.2 = (s32[2048,1]{1,0:T(8,128)}, s32[2048,1]{1,0:T(8,128)S(1)}, u32[]{:S(2)}) copy-start(s32[2048,1]{1,0:T(8,128)S(1)} %copy.310.column_ids) | copy-start | bytes 24580
  88.2 85.5 %copy-start.11 = (s32[17]{0:T(128)}, s32[17]{0:T(128)S(1)}, u32[]{:S(2)}) copy-start(s32[17]{0:T(128)S(1)} %pad_add_fusion.info_ref) | copy-start | bytes 208
  206.3 28.6 %all-to-all-start = ((bf16[4,512,320]{1,2,0:T(8,128)(2,1)}), bf16[4,512,320]{1,2,0:T(8,128)(2,1)}, u32[]{:S(2)}, u32[]{:S(2)}) async-start(bf16[4,512,320]{1,2,0:T(8,128)(2,1)} %bitcast.345), calls=%async_computation | async-start | bytes 2621440 | tf_op jit(solution)/shard_map/all_to_all | solution.py:521
  263.6 63.4 %collective-permute-start.7 = (bf16[8,640,640]{2,1,0:T(8,128)(2,1)}, bf16[8,640,640]{2,1,0:T(8,128)(2,1)}, u32[]{:S(2)}, u32[]{:S(2)}) collective-permute-start(bf16[8,640,640]{2,1,0:T(8,128)(2,1)} %convert_bitcast_fusion.1), channel_id=1, source_target_pairs={{0,8},{8,0},{1,9},{9,1},{2,10},{10,2},{3,11},{11,3},{4,12},{12,4},... | collective-permute-start | bytes 19660808 | tf_op jit(solution)/shard_map/ppermute | solution.py:70
  301.9 41.6 %collective-permute-start.10 = (bf16[8,640,640]{2,1,0:T(8,128)(2,1)}, bf16[8,640,640]{2,1,0:T(8,128)(2,1)}, u32[]{:S(2)}, u32[]{:S(2)}) collective-permute-start(bf16[8,640,640]{2,1,0:T(8,128)(2,1)} %convert_bitcast_fusion), channel_id=1, source_target_pairs={{0,8},{8,0},{1,9},{9,1},{2,10},{10,2},{3,11},{11,3},{4,12},{12,4},... | collective-permute-start | bytes 19660808 | tf_op jit(solution)/shard_map/ppermute | solution.py:70
  338.6 38.3 %collective-permute-start.8 = (bf16[4,2,160,640]{3,2,0,1:T(8,128)(2,1)}, bf16[4,2,160,640]{3,2,0,1:T(8,128)(2,1)}, u32[]{:S(2)}, u32[]{:S(2)}) collective-permute-start(bf16[4,2,160,640]{3,2,0,1:T(8,128)(2,1)} %bitcast.344), channel_id=1, source_target_pairs={{0,1},{1,0},{2,3},{3,2},{4,5},{5,4},{6,7},{7,6},{8,9},{9,8},{10,11... | collective-permute-start | bytes 4915208 | tf_op jit(solution)/shard_map/ppermute | solution.py:70
  343.0 39.0 %collective-permute-start.9 = (bf16[4,2,160,640]{3,2,0,1:T(8,128)(2,1)}, bf16[4,2,160,640]{3,2,0,1:T(8,128)(2,1)}, u32[]{:S(2)}, u32[]{:S(2)}) collective-permute-start(bf16[4,2,160,640]{3,2,0,1:T(8,128)(2,1)} %bitcast.343), channel_id=1, source_target_pairs={{0,16},{16,0},{1,17},{17,1},{2,18},{18,2},{3,19},{19,3},{4,20},{20... | collective-permute-start | bytes 4915208 | tf_op jit(solution)/shard_map/ppermute | solution.py:70
  354.7 62.4 %collective-permute-start.14 = (bf16[4,2,160,640]{3,2,0,1:T(8,128)(2,1)}, bf16[4,2,160,640]{3,2,0,1:T(8,128)(2,1)}, u32[]{:S(2)}, u32[]{:S(2)}) collective-permute-start(bf16[4,2,160,640]{3,2,0,1:T(8,128)(2,1)} %bitcast.341), channel_id=1, source_target_pairs={{0,16},{16,0},{1,17},{17,1},{2,18},{18,2},{3,19},{19,3},{4,20},{20... | collective-permute-start | bytes 4915208 | tf_op jit(solution)/shard_map/ppermute | solution.py:70
  362.6 89.6 %collective-permute-start.11 = (bf16[4,2,160,640]{3,2,0,1:T(8,128)(2,1)}, bf16[4,2,160,640]{3,2,0,1:T(8,128)(2,1)}, u32[]{:S(2)}, u32[]{:S(2)}) collective-permute-start(bf16[4,2,160,640]{3,2,0,1:T(8,128)(2,1)} %bitcast.342), channel_id=1, source_target_pairs={{0,16},{16,0},{1,17},{17,1},{2,18},{18,2},{3,19},{19,3},{4,20},{20... | collective-permute-start | bytes 4915208 | tf_op jit(solution)/shard_map/ppermute | solution.py:70
  396.5 154.2 %all-to-all-start.1 = ((bf16[4,512,320]{1,2,0:T(8,128)(2,1)}), bf16[4,512,320]{1,2,0:T(8,128)(2,1)}, u32[]{:S(2)}, u32[]{:S(2)}) async-start(bf16[4,512,320]{1,2,0:T(8,128)(2,1)} %bitcast.363), calls=%async_computation.1 | async-start | bytes 2621440 | tf_op jit(solution)/shard_map/all_to_all | solution.py:580
  421.5 38.8 %collective-permute-start.13 = (bf16[4,160,640]{2,1,0:T(8,128)(2,1)S(1)}, bf16[4,160,640]{2,1,0:T(8,128)(2,1)S(1)}, u32[]{:S(2)}, u32[]{:S(2)}) collective-permute-start(bf16[4,160,640]{2,1,0:T(8,128)(2,1)S(1)} %dynamic-slice_bitcast_fusion.4), channel_id=1, source_target_pairs={{0,1},{1,0},{2,3},{3,2},{4,5},{5,4},{6,7},{7,6},{8,9},{9,8},{10,11... | collective-permute-start | bytes 2457608 | tf_op jit(solution)/shard_map/ppermute | solution.py:70
  422.2 46.4 %collective-permute-start.12 = (bf16[4,160,640]{2,1,0:T(8,128)(2,1)S(1)}, bf16[4,160,640]{2,1,0:T(8,128)(2,1)S(1)}, u32[]{:S(2)}, u32[]{:S(2)}) collective-permute-start(bf16[4,160,640]{2,1,0:T(8,128)(2,1)S(1)} %dynamic-slice_bitcast_fusion.5), channel_id=1, source_target_pairs={{0,16},{16,0},{1,17},{17,1},{2,18},{18,2},{3,19},{19,3},{4,20},{20... | collective-permute-start | bytes 2457608 | tf_op jit(solution)/shard_map/ppermute | solution.py:70
  455.5 21.2 %collective-permute-start.21 = (bf16[4,160,640]{2,1,0:T(8,128)(2,1)S(1)}, bf16[4,160,640]{2,1,0:T(8,128)(2,1)S(1)}, u32[]{:S(2)}, u32[]{:S(2)}) collective-permute-start(bf16[4,160,640]{2,1,0:T(8,128)(2,1)S(1)} %dynamic-slice_bitcast_fusion.3), channel_id=1, source_target_pairs={{0,1},{1,0},{2,3},{3,2},{4,5},{5,4},{6,7},{7,6},{8,9},{9,8},{10,11... | collective-permute-start | bytes 2457608 | tf_op jit(solution)/shard_map/ppermute | solution.py:70
  456.2 35.2 %collective-permute-start.22 = (bf16[4,160,640]{2,1,0:T(8,128)(2,1)S(1)}, bf16[4,160,640]{2,1,0:T(8,128)(2,1)S(1)}, u32[]{:S(2)}, u32[]{:S(2)}) collective-permute-start(bf16[4,160,640]{2,1,0:T(8,128)(2,1)S(1)} %dynamic-slice_bitcast_fusion.2), channel_id=1, source_target_pairs={{0,1},{1,0},{2,3},{3,2},{4,5},{5,4},{6,7},{7,6},{8,9},{9,8},{10,11... | collective-permute-start | bytes 2457608 | tf_op jit(solution)/shard_map/ppermute | solution.py:70
  460.2 85.3 %collective-permute-start.30 = (bf16[640,1280]{1,0:T(8,128)(2,1)S(1)}, bf16[640,1280]{1,0:T(8,128)(2,1)S(1)}, u32[]{:S(2)}, u32[]{:S(2)}) collective-permute-start(bf16[640,1280]{1,0:T(8,128)(2,1)S(1)} %convolution_convert_fusion.3), channel_id=1, source_target_pairs={{0,8},{8,0},{1,9},{9,1},{2,10},{10,2},{3,11},{11,3},{4,12},{12,4},... | collective-permute-start | bytes 4915208 | tf_op jit(solution)/shard_map/ppermute | solution.py:70
  460.6 32.5 %collective-permute-start.20 = (bf16[160,640]{1,0:T(8,128)(2,1)S(1)}, bf16[160,640]{1,0:T(8,128)(2,1)S(1)}, u32[]{:S(2)}, u32[]{:S(2)}) collective-permute-start(bf16[160,640]{1,0:T(8,128)(2,1)S(1)} %get-tuple-element.106), channel_id=1, source_target_pairs={{0,6},{2,4},{4,2},{6,0},{1,7},{3,5},{5,3},{7,1},{8,14},{10,12},{12... | collective-permute-start | bytes 614408 | tf_op jit(solution)/shard_map/ppermute | solution.py:70
  468.6 26.8 %collective-permute-start.19 = (bf16[160,640]{1,0:T(8,128)(2,1)S(1)}, bf16[160,640]{1,0:T(8,128)(2,1)S(1)}, u32[]{:S(2)}, u32[]{:S(2)}) collective-permute-start(bf16[160,640]{1,0:T(8,128)(2,1)S(1)} %get-tuple-element.107), channel_id=1, source_target_pairs={{0,4},{2,6},{4,0},{6,2},{1,5},{3,7},{5,1},{7,3},{8,12},{10,14},{12... | collective-permute-start | bytes 614408 | tf_op jit(solution)/shard_map/ppermute | solution.py:70
  470.1 49.0 %copy-start.34 = (bf16[4,160,640]{2,1,0:T(8,128)(2,1)}, bf16[4,160,640]{2,1,0:T(8,128)(2,1)S(1)}, u32[]{:S(2)}) copy-start(bf16[4,160,640]{2,1,0:T(8,128)(2,1)S(1)} %fusion.44.refs_1_) | copy-start | bytes 2457604
  476.7 18.7 %collective-permute-start.18 = (bf16[160,640]{1,0:T(8,128)(2,1)S(1)}, bf16[160,640]{1,0:T(8,128)(2,1)S(1)}, u32[]{:S(2)}, u32[]{:S(2)}) collective-permute-start(bf16[160,640]{1,0:T(8,128)(2,1)S(1)} %get-tuple-element.105), channel_id=1, source_target_pairs={{0,2},{2,0},{4,6},{6,4},{1,3},{3,1},{5,7},{7,5},{8,10},{10,8},{12,... | collective-permute-start | bytes 614408 | tf_op jit(solution)/shard_map/ppermute | solution.py:70
  478.2 66.4 %copy-start.30 = (bf16[4,160,640]{2,1,0:T(8,128)(2,1)}, bf16[4,160,640]{2,1,0:T(8,128)(2,1)S(1)}, u32[]{:S(2)}) copy-start(bf16[4,160,640]{2,1,0:T(8,128)(2,1)S(1)} %fusion.42.refs_1_) | copy-start | bytes 2457604
  491.4 21.2 %collective-permute-start.17 = (bf16[160,640]{1,0:T(8,128)(2,1)S(1)}, bf16[160,640]{1,0:T(8,128)(2,1)S(1)}, u32[]{:S(2)}, u32[]{:S(2)}) collective-permute-start(bf16[160,640]{1,0:T(8,128)(2,1)S(1)} %get-tuple-element.103), channel_id=1, source_target_pairs={{0,6},{2,4},{4,2},{6,0},{1,7},{3,5},{5,3},{7,1},{8,14},{10,12},{12... | collective-permute-start | bytes 614408 | tf_op jit(solution)/shard_map/ppermute | solution.py:70
  492.9 45.3 %copy-start.31 = (bf16[4,160,640]{2,1,0:T(8,128)(2,1)}, bf16[4,160,640]{2,1,0:T(8,128)(2,1)S(1)}, u32[]{:S(2)}) copy-start(bf16[4,160,640]{2,1,0:T(8,128)(2,1)S(1)} %fusion.41.refs_2_) | copy-start | bytes 2457604
  493.1 22.1 %collective-permute-start.16 = (bf16[160,640]{1,0:T(8,128)(2,1)S(1)}, bf16[160,640]{1,0:T(8,128)(2,1)S(1)}, u32[]{:S(2)}, u32[]{:S(2)}) collective-permute-start(bf16[160,640]{1,0:T(8,128)(2,1)S(1)} %get-tuple-element.104), channel_id=1, source_target_pairs={{0,4},{2,6},{4,0},{6,2},{1,5},{3,7},{5,1},{7,3},{8,12},{10,14},{12... | collective-permute-start | bytes 614408 | tf_op jit(solution)/shard_map/ppermute | solution.py:70
  495.4 23.0 %collective-permute-start.15 = (bf16[160,640]{1,0:T(8,128)(2,1)S(1)}, bf16[160,640]{1,0:T(8,128)(2,1)S(1)}, u32[]{:S(2)}, u32[]{:S(2)}) collective-permute-start(bf16[160,640]{1,0:T(8,128)(2,1)S(1)} %get-tuple-element.102), channel_id=1, source_target_pairs={{0,2},{2,0},{4,6},{6,4},{1,3},{3,1},{5,7},{7,5},{8,10},{10,8},{12,... | collective-permute-start | bytes 614408 | tf_op jit(solution)/shard_map/ppermute | solution.py:70
  495.4 30.0 %collective-permute-start.41 = (bf16[160,640]{1,0:T(8,128)(2,1)S(1)}, bf16[160,640]{1,0:T(8,128)(2,1)S(1)}, u32[]{:S(2)}, u32[]{:S(2)}) collective-permute-start(bf16[160,640]{1,0:T(8,128)(2,1)S(1)} %get-tuple-element.100), channel_id=1, source_target_pairs={{0,6},{2,4},{4,2},{6,0},{1,7},{3,5},{5,3},{7,1},{8,14},{10,12},{12... | collective-permute-start | bytes 614408 | tf_op jit(solution)/shard_map/ppermute | solution.py:70
  512.6 20.1 %collective-permute-start.40 = (bf16[160,640]{1,0:T(8,128)(2,1)S(1)}, bf16[160,640]{1,0:T(8,128)(2,1)S(1)}, u32[]{:S(2)}, u32[]{:S(2)}) collective-permute-start(bf16[160,640]{1,0:T(8,128)(2,1)S(1)} %get-tuple-element.101), channel_id=1, source_target_pairs={{0,4},{2,6},{4,0},{6,2},{1,5},{3,7},{5,1},{7,3},{8,12},{10,14},{12... | collective-permute-start | bytes 614408 | tf_op jit(solution)/shard_map/ppermute | solution.py:70
  515.2 23.1 %collective-permute-start.39 = (bf16[160,640]{1,0:T(8,128)(2,1)S(1)}, bf16[160,640]{1,0:T(8,128)(2,1)S(1)}, u32[]{:S(2)}, u32[]{:S(2)}) collective-permute-start(bf16[160,640]{1,0:T(8,128)(2,1)S(1)} %get-tuple-element.99), channel_id=1, source_target_pairs={{0,2},{2,0},{4,6},{6,4},{1,3},{3,1},{5,7},{7,5},{8,10},{10,8},{12,... | collective-permute-start | bytes 614408 | tf_op jit(solution)/shard_map/ppermute | solution.py:70
  518.5 22.7 %collective-permute-start.38 = (bf16[160,640]{1,0:T(8,128)(2,1)S(1)}, bf16[160,640]{1,0:T(8,128)(2,1)S(1)}, u32[]{:S(2)}, u32[]{:S(2)}) collective-permute-start(bf16[160,640]{1,0:T(8,128)(2,1)S(1)} %get-tuple-element.97), channel_id=1, source_target_pairs={{0,6},{2,4},{4,2},{6,0},{1,7},{3,5},{5,3},{7,1},{8,14},{10,12},{12... | collective-permute-start | bytes 614408 | tf_op jit(solution)/shard_map/ppermute | solution.py:70
  525.4 17.3 %collective-permute-start.37 = (bf16[160,640]{1,0:T(8,128)(2,1)S(1)}, bf16[160,640]{1,0:T(8,128)(2,1)S(1)}, u32[]{:S(2)}, u32[]{:S(2)}) collective-permute-start(bf16[160,640]{1,0:T(8,128)(2,1)S(1)} %get-tuple-element.98), channel_id=1, source_target_pairs={{0,4},{2,6},{4,0},{6,2},{1,5},{3,7},{5,1},{7,3},{8,12},{10,14},{12... | collective-permute-start | bytes 614408 | tf_op jit(solution)/shard_map/ppermute | solution.py:70
  532.7 11.9 %collective-permute-start.36 = (bf16[160,640]{1,0:T(8,128)(2,1)S(1)}, bf16[160,640]{1,0:T(8,128)(2,1)S(1)}, u32[]{:S(2)}, u32[]{:S(2)}) collective-permute-start(bf16[160,640]{1,0:T(8,128)(2,1)S(1)} %get-tuple-element.96), channel_id=1, source_target_pairs={{0,2},{2,0},{4,6},{6,4},{1,3},{3,1},{5,7},{7,5},{8,10},{10,8},{12,... | collective-permute-start | bytes 614408 | tf_op jit(solution)/shard_map/ppermute | solution.py:70
  548.9 125.8 %collective-permute-start.31 = (bf16[320,1280]{1,0:T(8,128)(2,1)}, bf16[320,1280]{1,0:T(8,128)(2,1)}, u32[]{:S(2)}, u32[]{:S(2)}) collective-permute-start(bf16[320,1280]{1,0:T(8,128)(2,1)} %get-tuple-element.81), channel_id=1, source_target_pairs={{0,16},{16,0},{1,17},{17,1},{2,18},{18,2},{3,19},{19,3},{4,20},{20... | collective-permute-start | bytes 2457608 | tf_op jit(solution)/shard_map/ppermute | solution.py:70
  652.3 54.5 %collective-permute-start.23 = (bf16[2,256,1280]{2,1,0:T(8,128)(2,1)}, bf16[2,256,1280]{2,1,0:T(8,128)(2,1)}, u32[]{:S(2)}, u32[]{:S(2)}) collective-permute-start(bf16[2,256,1280]{2,1,0:T(8,128)(2,1)} %slice_bitcast_fusion.4), channel_id=1, source_target_pairs={{0,2},{2,0},{1,3},{3,1},{4,6},{6,4},{5,7},{7,5},{8,10},{10,8},{9,1... | collective-permute-start | bytes 3932168 | tf_op jit(solution)/shard_map/ppermute | solution.py:70
  654.8 53.4 %collective-permute-start.25 = (bf16[2,256,1280]{2,1,0:T(8,128)(2,1)}, bf16[2,256,1280]{2,1,0:T(8,128)(2,1)}, u32[]{:S(2)}, u32[]{:S(2)}) collective-permute-start(bf16[2,256,1280]{2,1,0:T(8,128)(2,1)} %slice_bitcast_fusion.1), channel_id=1, source_target_pairs={{0,1},{1,0},{2,3},{3,2},{4,5},{5,4},{6,7},{7,6},{8,9},{9,8},{10,11... | collective-permute-start | bytes 3932168 | tf_op jit(solution)/shard_map/ppermute | solution.py:70
  671.5 40.5 %collective-permute-start.27 = (bf16[2,320,960]{2,1,0:T(8,128)(2,1)}, bf16[2,320,960]{2,1,0:T(8,128)(2,1)}, u32[]{:S(2)}, u32[]{:S(2)}) collective-permute-start(bf16[2,320,960]{2,1,0:T(8,128)(2,1)} %dynamic-slice_bitcast_fusion), channel_id=1, source_target_pairs={{0,8},{8,0},{1,9},{9,1},{2,10},{10,2},{3,11},{11,3},{4,12},{12,4},... | collective-permute-start | bytes 3686408 | tf_op jit(solution)/shard_map/ppermute | solution.py:70
  684.6 13.8 %collective-permute-start.32 = (bf16[4,320,160]{1,2,0:T(8,128)(2,1)}, bf16[4,320,160]{1,2,0:T(8,128)(2,1)S(1)}, u32[]{:S(2)}, u32[]{:S(2)}) collective-permute-start(bf16[4,320,160]{1,2,0:T(8,128)(2,1)} %bitcast.386), channel_id=1, source_target_pairs={{0,1},{1,0},{2,3},{3,2},{4,5},{5,4},{6,7},{7,6},{8,9},{9,8},{10,11... | collective-permute-start | bytes 1228808 | tf_op jit(solution)/shard_map/ppermute | solution.py:70
  701.8 63.9 %collective-permute-start.35 = (bf16[320,160]{1,0:T(8,128)(2,1)}, bf16[320,160]{1,0:T(8,128)(2,1)S(1)}, u32[]{:S(2)}, u32[]{:S(2)}) collective-permute-start(bf16[320,160]{1,0:T(8,128)(2,1)} %get-tuple-element.109), channel_id=1, source_target_pairs={{0,6},{2,4},{4,2},{6,0},{1,7},{3,5},{5,3},{7,1},{8,14},{10,12},{12... | collective-permute-start | bytes 307208 | tf_op jit(solution)/shard_map/ppermute | solution.py:70
  706.7 59.5 %collective-permute-start.34 = (bf16[320,160]{1,0:T(8,128)(2,1)}, bf16[320,160]{1,0:T(8,128)(2,1)}, u32[]{:S(2)}, u32[]{:S(2)}) collective-permute-start(bf16[320,160]{1,0:T(8,128)(2,1)} %get-tuple-element.110), channel_id=1, source_target_pairs={{0,4},{2,6},{4,0},{6,2},{1,5},{3,7},{5,1},{7,3},{8,12},{10,14},{12... | collective-permute-start | bytes 307208 | tf_op jit(solution)/shard_map/ppermute | solution.py:70
  706.7 59.5 %collective-permute-start.33 = (bf16[320,160]{1,0:T(8,128)(2,1)}, bf16[320,160]{1,0:T(8,128)(2,1)}, u32[]{:S(2)}, u32[]{:S(2)}) collective-permute-start(bf16[320,160]{1,0:T(8,128)(2,1)} %get-tuple-element.108), channel_id=1, source_target_pairs={{0,2},{2,0},{4,6},{6,4},{1,3},{3,1},{5,7},{7,5},{8,10},{10,8},{12,... | collective-permute-start | bytes 307208 | tf_op jit(solution)/shard_map/ppermute | solution.py:70
  711.4 21.4 %collective-permute-start.26 = (bf16[256,1280]{1,0:T(8,128)(2,1)S(1)}, bf16[256,1280]{1,0:T(8,128)(2,1)S(1)}, u32[]{:S(2)}, u32[]{:S(2)}) collective-permute-start(bf16[256,1280]{1,0:T(8,128)(2,1)S(1)} %fusion.54), channel_id=1, source_target_pairs={{0,2},{2,0},{1,3},{3,1},{4,6},{6,4},{5,7},{7,5},{8,10},{10,8},{9,1... | collective-permute-start | bytes 1966088 | tf_op jit(solution)/shard_map/ppermute | solution.py:70
  712.1 20.9 %collective-permute-start.24 = (bf16[256,1280]{1,0:T(8,128)(2,1)S(1)}, bf16[256,1280]{1,0:T(8,128)(2,1)S(1)}, u32[]{:S(2)}, u32[]{:S(2)}) collective-permute-start(bf16[256,1280]{1,0:T(8,128)(2,1)S(1)} %fusion.53), channel_id=1, source_target_pairs={{0,1},{1,0},{2,3},{3,2},{4,5},{5,4},{6,7},{7,6},{8,9},{9,8},{10,11... | collective-permute-start | bytes 1966088 | tf_op jit(solution)/shard_map/ppermute | solution.py:70
  732.8 17.5 %collective-permute-start.28 = (bf16[320,960]{1,0:T(8,128)(2,1)}, bf16[320,960]{1,0:T(8,128)(2,1)}, u32[]{:S(2)}, u32[]{:S(2)}) collective-permute-start(bf16[320,960]{1,0:T(8,128)(2,1)} %dynamic-slice_bitcast_fusion.6), channel_id=1, source_target_pairs={{0,16},{16,0},{1,17},{17,1},{2,18},{18,2},{3,19},{19,3},{4,20},{20... | collective-permute-start | bytes 1843208 | tf_op jit(solution)/shard_map/ppermute | solution.py:70
  735.0 1.3 collective-permute-start.42
  736.3 13.1 %collective-permute-start.43 = (f32[5,1280]{1,0:T(8,128)S(1)}, f32[5,1280]{1,0:T(8,128)}, u32[]{:S(2)}, u32[]{:S(2)}) collective-permute-start(f32[5,1280]{1,0:T(8,128)S(1)} %fusion.73), channel_id=1, source_target_pairs={{0,16},{16,0},{1,17},{17,1},{2,18},{18,2},{3,19},{19,3},{4,20},{20... | collective-permute-start | bytes 76808 | tf_op jit(solution)/shard_map/ppermute | solution.py:70
  749.5 4.3 collective-permute-start.47
  750.3 4.1 collective-permute-start.44
  753.8 4.1 collective-permute-start.48
  754.3 7.0 collective-permute-start.45
  757.8 22.1 %collective-permute-start.29 = (bf16[320,480]{1,0:T(8,128)(2,1)S(1)}, bf16[320,480]{1,0:T(8,128)(2,1)S(1)}, u32[]{:S(2)}, u32[]{:S(2)}) collective-permute-start(bf16[320,480]{1,0:T(8,128)(2,1)S(1)} %bitcast.387), channel_id=1, source_target_pairs={{0,4},{4,0},{1,5},{5,1},{2,6},{6,2},{3,7},{7,3},{8,12},{12,8},{9,1... | collective-permute-start | bytes 921608 | tf_op jit(solution)/shard_map/ppermute | solution.py:70
  761.4 4.1 collective-permute-start.49
  765.4 10.9 %collective-permute-start.46 = (f32[5,1280]{1,0:T(8,128)S(1)}, f32[5,1280]{1,0:T(8,128)S(1)}, u32[]{:S(2)}, u32[]{:S(2)}) collective-permute-start(f32[5,1280]{1,0:T(8,128)S(1)} %add.519), channel_id=1, source_target_pairs={{0,4},{4,0},{1,5},{5,1},{2,6},{6,2},{3,7},{7,3},{8,12},{12,8},{9,1... | collective-permute-start | bytes 76808 | tf_op jit(solution)/shard_map/ppermute | solution.py:70
  765.8 10.6 %collective-permute-start.50 = (f32[8,1280]{1,0:T(8,128)S(1)}, f32[8,1280]{1,0:T(8,128)S(1)}, u32[]{:S(2)}, u32[]{:S(2)}) collective-permute-start(f32[8,1280]{1,0:T(8,128)S(1)} %add.523), channel_id=1, source_target_pairs={{0,2},{2,0},{1,3},{3,1},{4,6},{6,4},{5,7},{7,5},{8,10},{10,8},{9,1... | collective-permute-start | bytes 122888 | tf_op jit(solution)/shard_map/ppermute | solution.py:70
  776.4 16.1 %collective-permute-start.51 = (f32[8,1280]{1,0:T(8,128)S(1)}, f32[8,1280]{1,0:T(8,128)S(1)}, u32[]{:S(2)}, u32[]{:S(2)}) collective-permute-start(f32[8,1280]{1,0:T(8,128)S(1)} %add.524), channel_id=1, source_target_pairs={{0,4},{4,0},{1,5},{5,1},{2,6},{6,2},{3,7},{7,3},{8,12},{12,8},{9,1... | collective-permute-start | bytes 122888 | tf_op jit(solution)/shard_map/ppermute | solution.py:70
  (75 other events, 699.0 us)
Sparse Core Ops, SparseCore 0:
  15.9 155.8 all-gather.2
  174.6 107.0 all-gather.4

commit v2 on v1

--- a/solution.py
+++ b/solution.py
@@ -189,7 +189,7 @@
     )(info, rows, wide_w, wide_bias, cosine, sine, *earlier)
 
 
-def attend_kernel(heads, tile, info_ref, q_ref, k_ref, vt_ref, row_ids, column_ids, *refs):
+def attend_kernel(heads, tile, info_ref, q_ref, k_ref, vt_ref, row_ids, column_ids, pack_ref, *refs):
     out_ref, lse_ref, acc_ref = refs[-3:]
     block = pl.program_id(0)
     first = info_ref[1 + block]
@@ -221,11 +221,12 @@
     for head in range(heads):
         lanes = slice(head * LANES, (head + 1) * LANES)
         top, summed = done[head]
-        out_ref[:, lanes] = (acc_ref[lanes, :] / summed).T.astype(LOW)
+        acc_ref[lanes, :] = acc_ref[lanes, :] / summed
         lse_ref[0, head : head + 1, :] = top + jnp.log2(summed)
-
-
-def attend(info, query, keys, values_t, row_ids, column_ids, heads, group, earlier):
+    out_ref[...] = tn(acc_ref[...].astype(LOW), pack_ref[...]).astype(LOW)
+
+
+def attend(info, query, keys, values_t, row_ids, column_ids, pack, heads, group, earlier):
     total = query.shape[0]
     wide = heads * LANES
     blocks, _, tile = row_ids.shape
@@ -241,16 +242,17 @@
                 pl.BlockSpec((wide, total), lambda b, info: (group, 0)),
                 pl.BlockSpec((1, 1, tile), lambda b, info: (b, 0, 0)),
                 pl.BlockSpec((total, 1), lambda b, info: (0, 0)),
+                pl.BlockSpec(pack.shape, lambda b, info: (0, 0)),
             ]
             + [pl.BlockSpec(memory_space=pl.ANY)] * len(earlier),
             out_specs=[
-                pl.BlockSpec((tile, wide), lambda b, info: (b, 0)),
+                pl.BlockSpec((tile, heads * HD), lambda b, info: (b, 0)),
                 pl.BlockSpec((1, heads, tile), lambda b, info: (b, 0, 0)),
             ],
             scratch_shapes=[pltpu.VMEM((wide, tile), FULL)],
         ),
         out_shape=[
-            jax.ShapeDtypeStruct((total, wide), LOW),
+            jax.ShapeDtypeStruct((total, heads * HD), LOW),
             jax.ShapeDtypeStruct((blocks, heads, tile), FULL),
         ],
         compiler_params=pltpu.CompilerParams(vmem_limit_bytes=48 << 20),
@@ -258,7 +260,7 @@
             flops=2 * total * total * wide, bytes_accessed=8 * total * wide, transcendentals=total * total * heads // 2
         ),
         name="attend",
-    )(info, query, keys, values_t, row_ids, column_ids, *earlier)
+    )(info, query, keys, values_t, row_ids, column_ids, pack, *earlier)
 
 
 def attend_back_kernel(
@@ -270,16 +272,18 @@
     k_ref,
     v_ref,
     kt_ref,
-    do_ref,
+    grad_ref,
     o_ref,
     lse_ref,
     row_ids,
     column_ids,
     cos_ref,
     sin_ref,
+    pack_ref,
+    spread_ref,
     *refs,
 ):
-    out_ref, inner_ref, qt_ref, dk_ref, dv_ref = refs[-5:]
+    out_ref, inner_ref, do_ref, qt_ref, dk_ref, dv_ref = refs[-6:]
     block = pl.program_id(0)
     blocks = pl.num_programs(0)
     me = info_ref[0]
@@ -301,12 +305,22 @@
     def _():
         qt_ref[...] = jnp.zeros_like(qt_ref)
 
+        lane = lax.broadcasted_iota(jnp.int32, (8, heads * HD), 1)
+        head = lax.broadcasted_iota(jnp.int32, (8, heads * HD), 0)
+        pick = ((lane >= head * HD) & (lane < (head + 1) * HD)).astype(FULL)
+
         def fill(b, carry):
             where = pl.ds(place(b), tile)
-            for head in range(heads):
-                lanes = slice(head * LANES, (head + 1) * LANES)
-                both = o_ref[where, lanes].astype(FULL) * do_ref[where, lanes].astype(FULL)
-                inner_ref[b, head : head + 1, :] = jnp.sum(both.T, axis=0, keepdims=True)
+            grad = grad_ref[where, :]
+            do_ref[where, :] = nt(grad, pack_ref[...]).astype(LOW)
+            both = o_ref[where, :].astype(FULL) * grad.astype(FULL)
+            inner_ref[b] = lax.dot_general(
+                pick,
+                both,
+                (((1,), (1,)), ((), ())),
+                precision=lax.Precision.HIGHEST,
+                preferred_element_type=FULL,
+            )
             return carry
 
         lax.fori_loop(0, blocks, fill, 0)
@@ -337,23 +351,27 @@
     rows = pl.ds(home(block), tile)
     for head in range(heads):
         lanes = slice(head * LANES, (head + 1) * LANES)
-        key_grad = unrotate(dk_ref[:, lanes] * math.log(2.0), block)
-        out_ref[rows, wide + head * LANES : wide + (head + 1) * LANES] = key_grad.astype(LOW)
-        out_ref[rows, 2 * wide + head * LANES : 2 * wide + (head + 1) * LANES] = dv_ref[:, lanes].astype(LOW)
+        dk_ref[:, lanes] = unrotate(dk_ref[:, lanes] * math.log(2.0), block)
+    key_part = nt(dk_ref[...].astype(LOW), spread_ref[:, wide : 2 * wide])
+    value_part = nt(dv_ref[...].astype(LOW), spread_ref[:, 2 * wide :])
+    out_ref[rows, :] = (key_part + value_part).astype(LOW)
 
     @pl.when(block == blocks - 1)
     def _():
         def spill(b, carry):
+            rows = pl.ds(home(b), tile)
             for head in range(heads):
                 lanes = slice(head * LANES, (head + 1) * LANES)
                 query_grad = qt_ref[lanes, pl.ds(place(b), tile)].T * HD ** (-0.5)
-                out_ref[pl.ds(home(b), tile), lanes] = unrotate(query_grad, b).astype(LOW)
+                dk_ref[:, lanes] = unrotate(query_grad, b)
+            query_part = nt(dk_ref[...].astype(LOW), spread_ref[:, :wide])
+            out_ref[rows, :] = (out_ref[rows, :].astype(FULL) + query_part).astype(LOW)
             return carry
 
         lax.fori_loop(0, blocks, spill, 0)
 
 
-def attend_back(info, query, keys, values, keys_t, grad, attended, logs, row_ids, column_ids, cosine, sine, members, heads, group, earlier):
+def attend_back(info, query, keys, values, keys_t, grad, attended, logs, row_ids, column_ids, cosine, sine, pack, spread, members, heads, group, earlier):
     total = query.shape[0]
     wide = heads * LANES
     blocks, _, tile = row_ids.shape
@@ -374,31 +392,48 @@
                 flat,
                 flat,
                 tall,
-                flat,
-                whole(total, wide),
+                whole(total, heads * HD),
+                whole(total, heads * HD),
                 whole(blocks, heads, tile),
                 whole(blocks, 1, tile),
                 whole(total, 1),
                 whole(total, LANES),
                 whole(total, LANES),
+                whole(*pack.shape),
+                whole(*spread.shape),
             ]
             + [pl.BlockSpec(memory_space=pl.ANY)] * len(earlier),
-            out_specs=whole(total, 3 * wide),
+            out_specs=whole(total, 3 * heads * HD),
             scratch_shapes=[
-                pltpu.VMEM((blocks, heads, tile), FULL),
+                pltpu.VMEM((blocks, 8, tile), FULL),
+                pltpu.VMEM((total, wide), LOW),
                 pltpu.VMEM((wide, total), FULL),
                 pltpu.VMEM((tile, wide), FULL),
                 pltpu.VMEM((tile, wide), FULL),
             ],
         ),
-        out_shape=jax.ShapeDtypeStruct((total, 3 * wide), LOW),
+        out_shape=jax.ShapeDtypeStruct((total, 3 * heads * HD), LOW),
         compiler_params=pltpu.CompilerParams(vmem_limit_bytes=56 << 20),
         cost_estimate=pl.CostEstimate(
             flops=5 * total * total * wide, bytes_accessed=18 * total * wide, transcendentals=total * total * heads // 2
         ),
         name="attend_back",
     )(
-        info, query, keys, values, keys_t, grad, attended, logs, row_ids, column_ids, cosine, sine, *earlier
+        info,
+        query,
+        keys,
+        values,
+        keys_t,
+        grad,
+        attended,
+        logs,
+        row_ids,
+        column_ids,
+        cosine,
+        sine,
+        pack,
+        spread,
+        *earlier,
     )
 
 
@@ -455,9 +490,7 @@
     down_w = lax.all_gather(down, everyone, axis=0, tiled=True)
     down_w = down_w.reshape(members_of, width, four)
     lift_w = lift_all[:, :, :four]
-    out_w = jnp.concatenate(
-        [lift_all[h * members + m, :, four:] for m in range(members) for h in range(shards)], axis=1
-    )
+    out_w = lift_all[:, :, four:]
 
     part = jnp.concatenate(gather(early_norm[:half], "y"), axis=0)
     rows_a = jnp.concatenate(gather(part, "zl"), axis=0)
@@ -505,23 +538,21 @@
     query, keys, values, keys_t, values_t = project(
         info, early_rows, wide_w, wide_bias, cosine, sine, members, heads, []
     )
-    groups = 2
-    few = heads // groups
-    attended_wide, logs = [], []
-    for group in range(groups):
+    pack = jnp.asarray(spread_matrix(1, 1, heads_each, False).T, LOW)
+    spread_one = jnp.asarray(spread_matrix(1, 3, heads_each, True), LOW)
+    own, logs, attended = [], [], []
+    for group in range(shards):
         some, log = attend(
-            info, query, keys, values_t, row_ids, column_ids, few, group, logs[:1]
+            info, query, keys, values_t, row_ids, column_ids, pack, heads_each, group, logs[-1:]
         )
-        attended_wide.append(some)
+        own.append(some)
         logs.append(log)
-
-    squeeze = jnp.asarray(spread_matrix(shards, 1, heads_each, False).T, LOW)
-    own = nn(attended_wide[0], squeeze[: few * LANES]) + nn(attended_wide[1], squeeze[few * LANES :])
-    own = own.astype(LOW).reshape(members, tokens, shards * columns)
-    own = lax.all_to_all(own, SQUARE, split_axis=0, concat_axis=0, tiled=True)
-    attended = jnp.swapaxes(own, 0, 1).reshape(tokens, width)
-
-    middle = inputs + nt(attended, out_w) + vectors[4]
+        some = some.reshape(members, tokens, columns)
+        attended.append(lax.all_to_all(some, SQUARE, split_axis=0, concat_axis=0, tiled=True))
+
+    attended = jnp.concatenate(attended, axis=0)
+    branch = jnp.einsum("tnc,tic->ni", attended, out_w, preferred_element_type=FULL)
+    middle = inputs + branch + vectors[4]
     later_norm = layer_norm(middle, vectors[2], vectors[3]).astype(LOW)
 
     lift_bias = jnp.swapaxes(vectors[9:13].reshape(4, members_of, columns), 0, 1)
@@ -562,10 +593,7 @@
 
     hidden_grad = jnp.einsum("ni,tij->tnj", cotangent, down_w, preferred_element_type=FULL)
     upper_grad = jax.vjp(quick_gelu, upper)[1](hidden_grad)[0].astype(LOW)
-    lift_sum = first_sum(split(later_norm), upper_grad)
-    lift_plane = [over_plane(chunk(lift_sum, 0), "xy"), over_plane(chunk(lift_sum, 1), "xy")]
-    lift_grad = jnp.concatenate([scatter(last, LINE, 0) for _, last in lift_plane], axis=0)
-
+    upper_grad = tie(upper_grad, down_sum)
     later_grad = jnp.einsum("tnj,tdj->nd", upper_grad, lift_w, preferred_element_type=FULL)
 
     cot_full = cotangent.astype(FULL)
@@ -573,27 +601,29 @@
         later_grad
     )
     middle_grad = cot_full + middle_part
-    middle_low = tie(middle_grad.astype(LOW), [first for first, _ in down_plane])
-
-    attended_grad = nn(middle_low, out_w).astype(LOW)
-    row_grad = jnp.swapaxes(attended_grad.reshape(tokens, members, shards * columns), 0, 1)
-    row_grad = lax.all_to_all(row_grad, SQUARE, split_axis=0, concat_axis=0, tiled=True)
-    row_grad = nt(row_grad.reshape(SEQ, shards * columns), squeeze).astype(LOW)
-
-    mine, theirs = split(middle_low)
-    out_sum = (tn(mine, attended) + swap(tn(theirs, attended).astype(LOW), "c", 1).astype(FULL)).astype(LOW)
-    out_sum = scatter(out_sum.reshape(xs, depth, width), "x", 0).astype(LOW)
-    out_sum = out_sum.reshape(depth, 2, ys, shards, columns)
-    out_sum = jnp.moveaxis(out_sum, (3, 1, 2), (0, 1, 2)).reshape(2 * shards, ys, depth, columns)
-    out_sum = scatter(out_sum, "y", 1).astype(LOW)
-    out_grad = scatter(out_sum, LINE, 0)
+    middle_low = middle_grad.astype(LOW)
+
+    lift_sum = first_sum(split(later_norm), upper_grad)
+    lift_plane = [over_plane(chunk(lift_sum, 0), "xy"), over_plane(chunk(lift_sum, 1), "yx")]
+    lift_grad = jnp.concatenate([scatter(last, LINE, 0) for _, last in lift_plane], axis=0)
+
+    attended_grad = jnp.einsum("ni,tic->tnc", middle_low, out_w, preferred_element_type=FULL)
+    attended_grad = attended_grad.astype(LOW).reshape(shards, members, tokens, columns)
+    row_grad = [
+        lax.all_to_all(attended_grad[g], SQUARE, split_axis=0, concat_axis=0, tiled=True)
+        for g in range(shards)
+    ]
+    out_grad = jnp.einsum("ni,tnc->tic", middle_low, attended, preferred_element_type=FULL)
+    out_grad = out_grad.astype(LOW).reshape(members_of * width, columns)
+    out_grad = lax.psum_scatter(out_grad, everyone, scatter_dimension=0, tiled=True).astype(FULL)
 
     heads_grad = []
     waits = [
-        leaves((lift_plane[0][0], [last for _, last in down_plane])),
-        leaves((lift_plane[1][0], down_grad)),
+        leaves([first for first, _ in down_plane]),
+        leaves(([last for _, last in down_plane], [first for first, _ in lift_plane])),
     ]
-    for group in range(groups):
+    waits += [[]] * (shards - 2)
+    for group in range(shards):
         heads_grad.append(
             attend_back(
                 info,
@@ -601,35 +631,35 @@
                 keys,
                 values,
                 keys_t,
-                row_grad,
-                attended_wide[group],
+                row_grad[group].reshape(SEQ, columns),
+                own[group],
                 logs[group],
                 row_ids,
                 column_ids,
                 cosine,
                 sine,
+                pack,
+                spread_one,
                 members,
-                few,
+                heads_each,
                 group,
-                waits[group] + heads_grad[:1],
+                waits[group] + heads_grad[-1:],
             )
         )
-    pack = spread_low.reshape(-1, 3, groups, few * LANES)
-    pack = [pack[:, :, group].reshape(-1, 3 * few * LANES) for group in range(groups)]
-    heads_grad = (nt(heads_grad[0], pack[0]) + nt(heads_grad[1], pack[1])).astype(LOW)
-    heads_grad = tie(heads_grad, [last for _, last in lift_plane])
-
-    partial = nt(heads_grad, qkv).astype(LOW).reshape(2, 2, ys, half, width)
+    qkv = tie(qkv, heads_grad[-1], [last for _, last in lift_plane], down_grad)
+    three = 3 * columns
+    partial = sum(nt(some, qkv[:, g * three : (g + 1) * three]) for g, some in enumerate(heads_grad))
+    partial = partial.astype(LOW).reshape(2, 2, ys, half, width)
     some = scatter_near([partial[0, l] for l in range(2)], "zl")
     some_a = scatter_near([some[j] for j in range(ys)], "y")
     some = scatter_near([partial[1, :, j] for j in range(ys)], "y")
     some_b = scatter_near([some[l] for l in range(2)], "zl")
     early_grad = jnp.concatenate([some_a, some_b], axis=0)
 
-    qkv_grad = tn(early_rows, heads_grad).astype(LOW).reshape(xs, 2, depth, shards * 3 * columns)
-    qkv_grad = scatter(qkv_grad, "c", 1).astype(LOW)
-    qkv_grad = scatter(qkv_grad, "x", 0).astype(LOW)
-    qkv_grad = jnp.swapaxes(qkv_grad.reshape(depth, shards, 3 * columns), 0, 1)
+    qkv_grad = jnp.stack([tn(early_rows, some).astype(LOW) for some in heads_grad], axis=0)
+    qkv_grad = qkv_grad.reshape(shards, xs, 2, depth, three)
+    qkv_grad = scatter(qkv_grad, "c", 2).astype(LOW)
+    qkv_grad = scatter(qkv_grad, "x", 1).astype(LOW)
     qkv_grad = scatter(qkv_grad, "zh", 0)
 
     input_part, gain_first, shift_first = jax.vjp(layer_norm, inputs, vectors[0], vectors[1])[1](
@@ -645,15 +675,17 @@
     ready = jnp.stack(
         [gain_second, shift_second, jnp.sum(middle_grad, axis=0), jnp.sum(cot_full, axis=0)]
     )
-    ready = sum_everywhere(jnp.concatenate([ready, ffn_bias], axis=0))
-    heads_sum = jnp.sum(heads_grad, axis=0, dtype=FULL).reshape(shards, 3, columns)
+    heads_sum = jnp.stack([jnp.sum(some, axis=0, dtype=FULL) for some in heads_grad])
+    heads_sum = heads_sum.reshape(shards, 3, columns)
     placed = jnp.where(
         (jnp.arange(members) == me)[None, None, :, None],
         jnp.swapaxes(heads_sum, 0, 1)[:, :, None, :],
         0.0,
     ).reshape(3, width)
-    late = sum_everywhere(jnp.concatenate([jnp.stack([gain_first, shift_first]), placed], axis=0))
-    vector_grad = jnp.concatenate([late[0:2], ready[0:4], late[2:5], ready[4:8]], axis=0)
+    vector_grad = jnp.concatenate(
+        [jnp.stack([gain_first, shift_first]), ready, placed, ffn_bias], axis=0
+    )
+    vector_grad = sum_everywhere(vector_grad)
 
     next_first, next_second, next_weights = adam_update(
         weights, owned, first_moment, second_moment, rate_matrix, decay_matrix

time: 804 us -> 735 us (0.914)
  waiting for transfers between devices: 260 us -> 151 us
  starting transfers between devices: 72.3 us -> 121 us
  Pallas kernels: 142 us -> 132 us
    ppermute x52 -> x41, waiting for transfers between devices: 235 us -> 118 us  [swap(): lax.ppermute(value, axis, [(i, i ^ far) for i in range(lax.axis_size(axis...]
    ppermute x52 -> x41, starting transfers between devices: 61.1 us -> 100 us  [swap(): lax.ppermute(value, axis, [(i, i ^ far) for i in range(lax.axis_size(axis...]
    dot_general x12 -> x5, matrix products: 51.2 us -> 33 us  [dot(): return lax.dot_general(a, b, (dims, ((), ())), preferred_element_type=FULL)]
    dot_general x0 -> x3, matrix products: none -> 15.9 us  [the longest x1 6.08 us: local(): jnp.einsum('tnc,tic->ni', attended, out_w, preferred_element_type=FULL)]
    pallas_call x2, Pallas kernels: 59.2 us -> 49.4 us  [attend(): pl.pallas_call(functools.partial(attend_kernel, heads, tile), grid_spec=p...]
    all_to_all x2 -> x4, starting transfers between devices: 11.1 us -> 20.3 us  [the longest x2 11 us: local(): lax.all_to_all(some, SQUARE, split_axis=0, concat_axis=0, tiled=True)]
    all_to_all x2 -> x4, waiting for transfers between devices: 7.56 us -> 15.9 us  [the longest x2 8.84 us: local(): lax.all_to_all(attended_grad[g], SQUARE, split_axis=0, concat_axis=0, til...]
    unnamed x174 -> x177, local copies, waits for them, and re-layouts: 17.7 us -> 20.4 us
  transfers between devices with their start and end apart: 56 -> 48, of which waited for: 28 -> 17; matrix products, arithmetic and copies ran while one was open for 36% -> 36% of each run, Pallas kernels for 18% -> 18%
where the time goes in v2:
time: 735 us; the launch traced here: 729 us
  waiting for transfers between devices  151 us (21%)
  matrix products  139 us (19%)
  Pallas kernels  132 us (18%)
  starting transfers between devices  121 us (16%)
  local copies, waits for them, and re-layouts  96.1 us (13%)
  other arithmetic  74.6 us (10%)
  between operations  15.3 us (2%)
    ppermute x41, waiting for transfers between devices, swap(): lax.ppermute(value, axis, [(i, i ^ far) for i in range(lax.axis_size(axis...  118 us
    ppermute x41, starting transfers between devices, swap(): lax.ppermute(value, axis, [(i, i ^ far) for i in range(lax.axis_size(axis...  100 us
    pallas_call x2, Pallas kernels, attend_back(): pl.pallas_call(functools.partial(attend_back_kernel, heads, tile, members...  68.3 us
    pallas_call x2, Pallas kernels, attend(): pl.pallas_call(functools.partial(attend_kernel, heads, tile), grid_spec=p...  49.4 us
    dot_general x5, matrix products, dot(): return lax.dot_general(a, b, (dims, ((), ())), preferred_element_type=FULL)  33 us
    unnamed x177, local copies, waits for them, and re-layouts  20.4 us
    all_gather x1, waiting for transfers between devices, local(): down_w = lax.all_gather(down, everyone, axis=0, tiled=True)  16.9 us
    dot_general x1, matrix products, local(): jnp.einsum('ni,tij->tnj', cotangent, down_w, preferred_element_type=FULL)  16.8 us
  transfers between devices with their start and end apart: 48, of which 17 were waited for; matrix products, arithmetic and copies ran while one was open for 36% of the time, Pallas kernels for 18%

profile of v2, /device:TPU:8, one launch (start us, length us, event | category | flops | bytes accessed | tf_op | source)
XLA Modules:
  0.0 729.2 jit_solution(1145343416777948880)
XLA Ops:
  18.4 2.7 collective-permute-start.4
  27.8 5.6 fusion.111.bias_ref
  33.5 20.9 %collective-permute-done.4 = bf16[320,480]{0,1:T(8,128)(2,1)} collective-permute-done((bf16[320,480]{0,1:T(8,128)(2,1)S(1)}, bf16[320,480]{0,1:T(8,128)(2,1)}, u32[]{:S(2)}, u32[]{:S(2)}) %collective-permute-start.4) | collective-permute-done | bytes 307232 | tf_op jit(solution)/shard_map/ppermute | solution.py:70
  67.9 21.6 %collective-permute-done.5 = bf16[320,960]{1,0:T(8,128)(2,1)} collective-permute-done((bf16[320,960]{1,0:T(8,128)(2,1)}, bf16[320,960]{1,0:T(8,128)(2,1)}, u32[]{:S(2)}, u32[]{:S(2)}) %collective-permute-start.5) | collective-permute-done | bytes 614432 | tf_op jit(solution)/shard_map/ppermute | solution.py:70
  100.8 9.8 %collective-permute-done.1 = bf16[512,1280]{1,0:T(8,128)(2,1)} collective-permute-done((bf16[512,1280]{1,0:T(8,128)(2,1)}, bf16[512,1280]{1,0:T(8,128)(2,1)}, u32[]{:S(2)}, u32[]{:S(2)}) %collective-permute-start.1) | collective-permute-done | bytes 1310752 | tf_op jit(solution)/shard_map/ppermute | solution.py:70
  110.6 4.1 pad_maximum_fusion.rows_ref
  114.7 2.8 copy.372
  121.9 4.7 copy.374
  126.6 8.7 %convolution_convert_fusion.w_ref = bf16[1280,1536]{1,0:T(8,128)(2,1)} fusion(bf16[1280,960]{1,0:T(8,128)(2,1)} %bitcast.319, bf16[960,1536]{1,0:T(8,128)(2,1)} %constant.297.clone), kind=kOutput, calls=%fused_computation.26 | convolution fusion | flops 3776839680 | bytes 9338880 | tf_op jit(solution)/shard_map/dot_general | solution.py:35
  135.3 14.7 %project.1 = (bf16[2048,512]{1,0:T(8,128)(2,1)S(1)}, bf16[2048,512]{1,0:T(8,128)(2,1)}, bf16[2048,512]{1,0:T(8,128)(2,1)}, bf16[512,2048]{1,0:T(8,128)(2,1)}, bf16[512,2048]{1,0:T(8,128)(2,1)}) custom-call(s32[17]{0:T(128)S(1)} %pad_add_fusion.info_ref, bf16[2048,1280]{1,0:T(8,128)(2,1)} %pad_maximum_fusion.rows_ref, ...), custom_call_target="tpu_custom_call" | custom-call | flops 8053063680 | bytes 19660800 | tf_op jit(solution)/shard_map/project/pallas_call | solution.py:165
  150.0 24.8 %attend.2 = (bf16[2048,160]{1,0:T(8,128)(2,1)S(1)}, f32[8,2,256]{2,1,0:T(2,128)S(1)}) custom-call(s32[17]{0:T(128)S(1)} %pad_add_fusion.info_ref, bf16[2048,512]{1,0:T(8,128)(2,1)S(1)} %get-tuple-element.17.q_ref, bf16[2048,512]{1,0:T(8,128)(2,1)} %get-tuple-element.18.k_ref, bf16[512,2048]{1,0:T(8,128)(2,1)} %get-tuple-element.19.vt_ref, ...), custom_call_target="tpu_custom_call" | custom-call | flops 2147483648 | bytes 4194304 | tf_op jit(solution)/shard_map/attend/pallas_call | solution.py:234
  178.1 6.4 all-to-all-start
  184.5 24.6 %attend.3 = (bf16[2048,160]{1,0:T(8,128)(2,1)S(1)}, f32[8,2,256]{2,1,0:T(2,128)S(1)}) custom-call(s32[17]{0:T(128)S(1)} %pad_add_fusion.info_ref, bf16[2048,512]{1,0:T(8,128)(2,1)S(1)} %copy-done.6, bf16[2048,512]{1,0:T(8,128)(2,1)} %get-tuple-element.18.k_ref, bf16[512,2048]{1,0:T(8,128)(2,1)} %get-tuple-element.19.vt_ref, s32[8,1,256]{2,1,0:T(1,128)S(1)} %bitcast.308, ...), custom_call_target="tpu_custom_call" | custom-call | flops 2147483648 | bytes 4194304 | tf_op jit(solution)/shard_map/attend/pallas_call | solution.py:234
  212.3 4.6 all-to-all-start.1
  218.6 2.6 broadcast_select_fusion.3
  223.2 7.1 all-to-all-done.1
  231.1 6.1 fusion.110
  239.2 13.5 %fusion.14 = (bf16[8,512,640]{2,1,0:T(8,128)(2,1)S(1)}, f32[8,640,512]{1,2,0:T(8,128)}) fusion(f32[8,640]{1,0:T(8,128)S(1)} %add.405, bf16[8,1280,800]{2,1,0:T(8,128)(2,1)} %bitcast.348, bf16[512,1280]{1,0:T(8,128)(2,1)S(1)} %add_convert_fusion.2), kind=kOutput, calls=%fused_computation.25 | convolution fusion | flops 6729236480 | bytes 30167040 | tf_op jit(solution)/shard_map/nd,tdj->tnj/dot_general | solution.py:560
  252.7 5.4 convert_bitcast_fusion.1
  260.4 2.7 broadcast_select_fusion.1
  263.0 16.9 %all-gather.5.cloned.1.call-done = bf16[10240,640]{1,0:T(8,128)(2,1)} async-done(((bf16[320,640]{1,0:T(8,128)(2,1)}), bf16[10240,640]{1,0:T(8,128)(2,1)}) %all-gather.5.cloned.1.call-update) | async-done | bytes 13107216 | tf_op jit(solution)/shard_map/all_gather | solution.py:490
  280.0 16.8 %fusion.9.refs_0_ = bf16[8,512,640]{2,1,0:T(8,128)(2,1)} fusion(f32[8,640,512]{1,2,0:T(8,128)} %get-tuple-element.111, f32[8,640]{1,0:T(8,128)S(1)} %add.405, bf16[8,1280,640]{2,1,0:T(8,128)(2,1)} %bitcast.351, bf16[512,1280]{1,0:T(8,128)(2,1)S(1)} %copy-done.45), kind=kOutput, calls=%fused_computation.14 | convolution fusion | flops 6744965120 | bytes 30167040 | tf_op jit(solution)/shard_map/ni,tij->tnj/dot_general | solution.py:594
  296.8 7.3 %fusion.1.refs_1_ = bf16[8,640,640]{2,1,0:T(8,128)(2,1)} fusion(bf16[8,640,640]{2,1,0:T(8,128)(2,1)} %collective-permute-done.7, bf16[512,640,1]{0,1,2:T(8,128)(2,1)S(1)} %bitcast.338, bf16[8,512,640]{2,1,0:T(8,128)(2,1)S(1)} %bitcast.354), kind=kOutput, calls=%fused_computation.6 | convolution fusion | flops 3365273600 | bytes 19005440 | tf_op jit(solution)/shard_map/ni,tnj->tij/dot_general | solution.py:575
  305.8 11.8 %multiply_reduce_fusion = (f32[1280]{0:T(1024)S(1)}, f32[512]{0:T(512)S(1)}, f32[1280]{0:T(1024)S(1)}, f32[512,1280]{1,0:T(8,128)S(1)}) fusion(f32[512,1280]{1,0:T(8,128)S(1)} %copy-done.18, f32[512]{0:T(512)S(1)} %fusion.91, f32[512]{0:T(512)S(1)} %broadcast_multiply_fusion.2, f32[1280]{0:T(1024)S(1)} %get-tuple-element.35, bf16[8,512,640]{2,1,0:T(8,128)(2,1)} %tie.2, ...), kind=kOutput, calls=%fused_computation.88 | convolution fusion | flops 6716126208 | bytes 23614464 | tf_op jit(solution)/shard_map/tnj,tdj->nd/dot_general | solution.py:597
  319.0 6.0 fusion.58
  326.1 4.7 all-to-all-start.2
  330.8 9.2 %convert_bitcast_fusion = bf16[8,640,640]{2,1,0:T(8,128)(2,1)} fusion(bf16[512,640,1]{0,1,2:T(8,128)(2,1)} %bitcast.339, bf16[8,512,640]{2,1,0:T(8,128)(2,1)} %tie.2), kind=kOutput, calls=%fused_computation.27 | convolution fusion | flops 3358720000 | bytes 12451840 | tf_op jit(solution)/shard_map/ni,tnj->tij/dot_general | solution.py:573
  348.3 4.7 all-to-all-start.3
  353.0 14.2 %fusion.41 = bf16[512,1280]{1,0:T(8,128)(2,1)} fusion(f32[512,1280]{1,0:T(8,128)S(1)} %copy-done.18, bf16[8,512,640]{2,1,0:T(8,128)(2,1)} %copy-done.75, bf16[8,1280,640]{2,1,0:T(8,128)(2,1)} %bitcast.352, f32[1280]{0:T(1024)S(1)} %copy-done.72), kind=kOutput, calls=%fused_computation.64 | convolution fusion | flops 6712852480 | bytes 22287360 | tf_op jit(solution)/shard_map/tnj,tij->ni/dot_general | solution.py:563
  367.2 3.8 fusion.23
  371.0 4.8 copy.422
  375.9 3.3 convert_reduce_fusion
  380.6 8.8 %all-to-all-done.3 = bf16[4,512,160]{1,2,0:T(8,128)(2,1)} async-done(((bf16[4,512,160]{1,2,0:T(8,128)(2,1)}), bf16[4,512,160]{1,2,0:T(8,128)(2,1)}, u32[]{:S(2)}, u32[]{:S(2)}) %all-to-all-start.3) | async-done | bytes 655392 | tf_op jit(solution)/shard_map/all_to_all | solution.py:613
  402.9 34.3 %attend_back.2.refs_4_ = bf16[2048,480]{1,0:T(8,128)(2,1)} custom-call(s32[17]{0:T(128)} %copy-done.13, bf16[2048,512]{1,0:T(8,128)(2,1)} %copy-done.5, bf16[2048,512]{1,0:T(8,128)(2,1)} %get-tuple-element.18.k_ref, bf16[2048,512]{1,0:T(8,128)(2,1)} %get-tuple-element.23.v_ref, bf16[512,2048]{1,0:T(8,128)(2,1)} %get-tuple-element.24.kt_ref, ...), custom_call_target="tpu_custom_call" | custom-call | flops 5368709120 | bytes 9437184 | tf_op jit(solution)/shard_map/attend_back/pallas_call | solution.py:385
  437.2 4.5 convolution_convert_fusion.3
  441.7 6.0 fusion
  453.1 7.2 collective-permute-start.13
  467.4 14.6 %collective-permute-start.22 = (bf16[160,640]{1,0:T(8,128)(2,1)S(1)}, bf16[160,640]{1,0:T(8,128)(2,1)S(1)}, u32[]{:S(2)}, u32[]{:S(2)}) collective-permute-start(bf16[160,640]{1,0:T(8,128)(2,1)S(1)} %get-tuple-element.98), channel_id=1, source_target_pairs={{0,6},{2,4},{4,2},{6,0},{1,7},{3,5},{5,3},{7,1},{8,14},{10,12},{12... | collective-permute-start | bytes 614408 | tf_op jit(solution)/shard_map/ppermute | solution.py:70
  485.8 13.7 %collective-permute-done.22 = bf16[160,640]{1,0:T(8,128)(2,1)S(1)} collective-permute-done((bf16[160,640]{1,0:T(8,128)(2,1)S(1)}, bf16[160,640]{1,0:T(8,128)(2,1)S(1)}, u32[]{:S(2)}, u32[]{:S(2)}) %collective-permute-start.22) | collective-permute-done | bytes 204832 | tf_op jit(solution)/shard_map/ppermute | solution.py:70
  499.5 5.9 collective-permute-start.19
  505.4 7.3 %collective-permute-done.21 = bf16[160,640]{1,0:T(8,128)(2,1)S(1)} collective-permute-done((bf16[160,640]{1,0:T(8,128)(2,1)S(1)}, bf16[160,640]{1,0:T(8,128)(2,1)S(1)}, u32[]{:S(2)}, u32[]{:S(2)}) %collective-permute-start.21) | collective-permute-done | bytes 204832 | tf_op jit(solution)/shard_map/ppermute | solution.py:70
  512.7 3.9 collective-permute-start.18
  518.6 3.9 collective-permute-done.18
  531.0 34.1 %attend_back.3.refs_1_ = bf16[2048,480]{1,0:T(8,128)(2,1)} custom-call(s32[17]{0:T(128)} %copy-done.13, bf16[2048,512]{1,0:T(8,128)(2,1)} %copy-done.5, bf16[2048,512]{1,0:T(8,128)(2,1)} %get-tuple-element.18.k_ref, bf16[2048,512]{1,0:T(8,128)(2,1)} %get-tuple-element.23.v_ref, bf16[512,2048]{1,0:T(8,128)(2,1)} %get-tuple-element.24.kt_ref, ...), custom_call_target="tpu_custom_call" | custom-call | flops 5368709120 | bytes 9437184 | tf_op jit(solution)/shard_map/attend_back/pallas_call | solution.py:385
  565.1 7.0 convolution_convert_fusion.2
  572.0 2.6 copy.419
  574.7 3.1 fusion.62
  585.0 7.0 fusion.66
  592.0 5.8 add_convert_fusion
  603.7 13.3 %collective-permute-start.35 = (bf16[160,640]{1,0:T(8,128)(2,1)S(1)}, bf16[160,640]{1,0:T(8,128)(2,1)S(1)}, u32[]{:S(2)}, u32[]{:S(2)}) collective-permute-start(bf16[160,640]{1,0:T(8,128)(2,1)S(1)} %get-tuple-element.92), channel_id=1, source_target_pairs={{0,6},{2,4},{4,2},{6,0},{1,7},{3,5},{5,3},{7,1},{8,14},{10,12},{12... | collective-permute-start | bytes 614408 | tf_op jit(solution)/shard_map/ppermute | solution.py:70
  621.2 15.3 %collective-permute-done.23 = bf16[2,256,1280]{2,1,0:T(8,128)(2,1)} collective-permute-done((bf16[2,256,1280]{2,1,0:T(8,128)(2,1)}, bf16[2,256,1280]{2,1,0:T(8,128)(2,1)}, u32[]{:S(2)}, u32[]{:S(2)}) %collective-permute-start.23) | collective-permute-done | bytes 1310752 | tf_op jit(solution)/shard_map/ppermute | solution.py:70
  636.5 5.3 collective-permute-start.28
  644.2 6.9 collective-permute-start.26
  651.2 8.2 %collective-permute-start.32 = (bf16[160,640]{1,0:T(8,128)(2,1)}, bf16[160,640]{1,0:T(8,128)(2,1)}, u32[]{:S(2)}, u32[]{:S(2)}) collective-permute-start(bf16[160,640]{1,0:T(8,128)(2,1)} %get-tuple-element.89), channel_id=1, source_target_pairs={{0,6},{2,4},{4,2},{6,0},{1,7},{3,5},{5,3},{7,1},{8,14},{10,12},{12... | collective-permute-start | bytes 614408 | tf_op jit(solution)/shard_map/ppermute | solution.py:70
  661.4 7.9 %collective-permute-done.26 = bf16[256,1280]{1,0:T(8,128)(2,1)S(1)} collective-permute-done((bf16[256,1280]{1,0:T(8,128)(2,1)S(1)}, bf16[256,1280]{1,0:T(8,128)(2,1)S(1)}, u32[]{:S(2)}, u32[]{:S(2)}) %collective-permute-start.26) | collective-permute-done | bytes 655392 | tf_op jit(solution)/shard_map/ppermute | solution.py:70
  669.5 5.4 collective-permute-done.24
  677.9 2.7 convert_reduce_fusion.4
  680.9 10.5 %collective-permute-start.29 = (bf16[320,480]{1,0:T(8,128)(2,1)S(1)}, bf16[320,480]{1,0:T(8,128)(2,1)S(1)}, u32[]{:S(2)}, u32[]{:S(2)}) collective-permute-start(bf16[320,480]{1,0:T(8,128)(2,1)S(1)} %dynamic-slice_bitcast_fusion.5), channel_id=1, source_target_pairs={{0,4},{4,0},{1,5},{5,1},{2,6},{6,2},{3,7},{7,3},{8,12},{12,8},{9,1... | collective-permute-start | bytes 921608 | tf_op jit(solution)/shard_map/ppermute | solution.py:70
  696.5 4.4 collective-permute-done.38
  700.9 4.2 collective-permute-done.29
  705.2 2.9 concatenate.61
  708.1 3.5 copy.423
  711.6 3.5 collective-permute-start.40
  715.1 6.5 multiply_subtract_fusion
  (410 shorter events, 147.2 us)
Async XLA Ops:
  7.2 223.9 %all-gather.3.cloned.1.call-start = ((), (), s32[]{:S(2)}) async-start(), calls=%async_computation.5 | async-start | bytes 18923520 | tf_op jit(solution)/shard_map/all_gather | solution.py:488
  11.3 268.6 %all-gather.5.cloned.1.call-start = ((), (), s32[]{:S(2)}) async-start(), calls=%async_computation.6 | async-start | bytes 13516800 | tf_op jit(solution)/shard_map/all_gather | solution.py:490
  16.3 48.0 %copy-start.41 = (bf16[256,1280]{1,0:T(8,128)(2,1)}, bf16[256,1280]{1,0:T(8,128)(2,1)S(1)}, u32[]{:S(2)}) copy-start(bf16[256,1280]{1,0:T(8,128)(2,1)S(1)} %get-tuple-element.84) | copy-start | bytes 1966084
  16.3 44.1 %collective-permute-start.2 = (bf16[256,1280]{1,0:T(8,128)(2,1)}, bf16[256,1280]{1,0:T(8,128)(2,1)}, u32[]{:S(2)}, u32[]{:S(2)}) collective-permute-start(bf16[256,1280]{1,0:T(8,128)(2,1)} %get-tuple-element.85), channel_id=1, source_target_pairs={{0,2},{2,0},{1,3},{3,1},{4,6},{6,4},{5,7},{7,5},{8,10},{10,8},{9,1... | collective-permute-start | bytes 1966088 | tf_op jit(solution)/shard_map/ppermute | solution.py:70
  16.4 47.9 %collective-permute-start = (bf16[256,1280]{1,0:T(8,128)(2,1)S(1)}, bf16[256,1280]{1,0:T(8,128)(2,1)}, u32[]{:S(2)}, u32[]{:S(2)}) collective-permute-start(bf16[256,1280]{1,0:T(8,128)(2,1)S(1)} %get-tuple-element.84), channel_id=1, source_target_pairs={{0,1},{1,0},{2,3},{3,2},{4,5},{5,4},{6,7},{7,6},{8,9},{9,8},{10,11... | collective-permute-start | bytes 1966088 | tf_op jit(solution)/shard_map/ppermute | solution.py:70
  18.4 35.9 %collective-permute-start.4 = (bf16[320,480]{0,1:T(8,128)(2,1)S(1)}, bf16[320,480]{0,1:T(8,128)(2,1)}, u32[]{:S(2)}, u32[]{:S(2)}) collective-permute-start(bf16[320,480]{0,1:T(8,128)(2,1)S(1)} %bitcast.336), channel_id=1, source_target_pairs={{0,4},{4,0},{1,5},{5,1},{2,6},{6,2},{3,7},{7,3},{8,12},{12,8},{9,1... | collective-permute-start | bytes 921608 | tf_op jit(solution)/shard_map/ppermute | solution.py:70
  21.5 163.0 %copy-start.10 = (s32[2048]{0:T(1024)}, s32[2048]{0:T(1024)S(1)}, u32[]{:S(2)}) copy-start(s32[2048]{0:T(1024)S(1)} %convert_reduce_fusion.5) | copy-start | bytes 24580
  27.8 26.5 %copy-start.56 = (bf16[320,3,160]{0,2,1:T(8,128)(2,1)S(1)}, bf16[320,3,160]{0,2,1:T(8,128)(2,1)}, u32[]{:S(2)}) copy-start(bf16[320,3,160]{0,2,1:T(8,128)(2,1)} %copy-done.55) | copy-start | bytes 921604
  58.9 30.5 %collective-permute-start.5 = (bf16[320,960]{1,0:T(8,128)(2,1)}, bf16[320,960]{1,0:T(8,128)(2,1)}, u32[]{:S(2)}, u32[]{:S(2)}) collective-permute-start(bf16[320,960]{1,0:T(8,128)(2,1)} %copy.368), channel_id=1, source_target_pairs={{0,16},{16,0},{1,17},{17,1},{2,18},{18,2},{3,19},{19,3},{4,20},{20... | collective-permute-start | bytes 1843208 | tf_op jit(solution)/shard_map/ppermute | solution.py:70
  62.8 35.7 %collective-permute-start.3 = (bf16[2,256,1280]{2,1,0:T(8,128)(2,1)}, bf16[2,256,1280]{2,1,0:T(8,128)(2,1)}, u32[]{:S(2)}, u32[]{:S(2)}) collective-permute-start(bf16[2,256,1280]{2,1,0:T(8,128)(2,1)} %bitcast.4), channel_id=1, source_target_pairs={{0,1},{1,0},{2,3},{3,2},{4,5},{5,4},{6,7},{7,6},{8,9},{9,8},{10,11... | collective-permute-start | bytes 3932168 | tf_op jit(solution)/shard_map/ppermute | solution.py:70
  66.6 44.0 %collective-permute-start.1 = (bf16[512,1280]{1,0:T(8,128)(2,1)}, bf16[512,1280]{1,0:T(8,128)(2,1)}, u32[]{:S(2)}, u32[]{:S(2)}) collective-permute-start(bf16[512,1280]{1,0:T(8,128)(2,1)} %pad_maximum_fusion.9), channel_id=1, source_target_pairs={{0,2},{2,0},{1,3},{3,1},{4,6},{6,4},{5,7},{7,5},{8,10},{10,8},{9,1... | collective-permute-start | bytes 3932168 | tf_op jit(solution)/shard_map/ppermute | solution.py:70
  67.8 67.5 %copy-start.3 = (f32[2048,128]{1,0:T(8,128)}, f32[2048,128]{1,0:T(8,128)S(1)}, u32[]{:S(2)}) copy-start(f32[2048,128]{1,0:T(8,128)S(1)} %get-tuple-element.86.sin_ref) | copy-start | bytes 3145732
  67.8 67.5 %copy-start.4 = (f32[2048,128]{1,0:T(8,128)}, f32[2048,128]{1,0:T(8,128)S(1)}, u32[]{:S(2)}) copy-start(f32[2048,128]{1,0:T(8,128)S(1)} %get-tuple-element.87.cos_ref) | copy-start | bytes 3145732
  98.0 16.6 %collective-permute-start.6 = (bf16[2,320,960]{2,1,0:T(8,128)(2,1)}, bf16[2,320,960]{2,1,0:T(8,128)(2,1)}, u32[]{:S(2)}, u32[]{:S(2)}) collective-permute-start(bf16[2,320,960]{2,1,0:T(8,128)(2,1)} %copy.371), channel_id=1, source_target_pairs={{0,8},{8,0},{1,9},{9,1},{2,10},{10,2},{3,11},{11,3},{4,12},{12,4},... | collective-permute-start | bytes 3686408 | tf_op jit(solution)/shard_map/ppermute | solution.py:70
  98.4 86.0 %copy-start.2 = (s32[2048,1]{1,0:T(8,128)}, s32[2048,1]{1,0:T(8,128)S(1)}, u32[]{:S(2)}) copy-start(s32[2048,1]{1,0:T(8,128)S(1)} %copy.382.column_ids) | copy-start | bytes 24580
  98.5 86.0 %copy-start.13 = (s32[17]{0:T(128)}, s32[17]{0:T(128)S(1)}, u32[]{:S(2)}) copy-start(s32[17]{0:T(128)S(1)} %pad_add_fusion.info_ref) | copy-start | bytes 208
  150.0 24.8 %copy-start.5 = (bf16[2048,512]{1,0:T(8,128)(2,1)}, bf16[2048,512]{1,0:T(8,128)(2,1)S(1)}, u32[]{:S(2)}) copy-start(bf16[2048,512]{1,0:T(8,128)(2,1)S(1)} %get-tuple-element.17.q_ref) | copy-start | bytes 6291460
  175.8 33.3 %copy-start.12 = (f32[8,2,256]{2,1,0:T(2,128)}, f32[8,2,256]{2,1,0:T(2,128)S(1)}, u32[]{:S(2)}) copy-start(f32[8,2,256]{2,1,0:T(2,128)S(1)} %get-tuple-element.21.refs_0_.lse_ref) | copy-start | bytes 49156
  178.1 34.2 %all-to-all-start = ((bf16[4,512,160]{1,2,0:T(8,128)(2,1)}), bf16[4,512,160]{1,2,0:T(8,128)(2,1)}, u32[]{:S(2)}, u32[]{:S(2)}) async-start(bf16[4,512,160]{1,2,0:T(8,128)(2,1)} %copy.383), calls=%async_computation | async-start | bytes 1310720 | tf_op jit(solution)/shard_map/all_to_all | solution.py:551
  212.3 17.9 %all-to-all-start.1 = ((bf16[4,512,160]{1,2,0:T(8,128)(2,1)}), bf16[4,512,160]{1,2,0:T(8,128)(2,1)S(1)}, u32[]{:S(2)}, u32[]{:S(2)}) async-start(bf16[4,512,160]{1,2,0:T(8,128)(2,1)} %copy.385), calls=%async_computation.1 | async-start | bytes 1310720 | tf_op jit(solution)/shard_map/all_to_all | solution.py:551
  258.1 38.6 %collective-permute-start.7 = (bf16[8,640,640]{2,1,0:T(8,128)(2,1)}, bf16[8,640,640]{2,1,0:T(8,128)(2,1)}, u32[]{:S(2)}, u32[]{:S(2)}) collective-permute-start(bf16[8,640,640]{2,1,0:T(8,128)(2,1)} %convert_bitcast_fusion.1), channel_id=1, source_target_pairs={{0,8},{8,0},{1,9},{9,1},{2,10},{10,2},{3,11},{11,3},{4,12},{12,4},... | collective-permute-start | bytes 19660808 | tf_op jit(solution)/shard_map/ppermute | solution.py:70
  260.4 36.4 %slice-start.6 = ((s8[5242880]{0:T(1024)(128)(4,1)}), s8[1048576]{0:T(1024)(128)(4,1)S(1)}, s32[]{:S(2)}) async-start(s8[5242880]{0:T(1024)(128)(4,1)} %bitcast.353), calls=%async_computation.14 | async-start | bytes 2097152
  326.1 22.2 %all-to-all-start.2 = ((bf16[4,512,160]{1,2,0:T(8,128)(2,1)}), bf16[4,512,160]{1,2,0:T(8,128)(2,1)S(1)}, u32[]{:S(2)}, u32[]{:S(2)}) async-start(bf16[4,512,160]{1,2,0:T(8,128)(2,1)} %get-tuple-element.81), calls=%async_computation.2 | async-start | bytes 1310720 | tf_op jit(solution)/shard_map/all_to_all | solution.py:613
  340.0 101.7 %collective-permute-start.12 = (bf16[8,640,640]{2,1,0:T(8,128)(2,1)}, bf16[8,640,640]{2,1,0:T(8,128)(2,1)}, u32[]{:S(2)}, u32[]{:S(2)}) collective-permute-start(bf16[8,640,640]{2,1,0:T(8,128)(2,1)} %convert_bitcast_fusion), channel_id=1, source_target_pairs={{0,8},{8,0},{1,9},{9,1},{2,10},{10,2},{3,11},{11,3},{4,12},{12,4},... | collective-permute-start | bytes 19660808 | tf_op jit(solution)/shard_map/ppermute | solution.py:70
  343.9 47.7 %collective-permute-start.8 = (bf16[4,2,160,640]{3,2,0,1:T(8,128)(2,1)}, bf16[4,2,160,640]{3,2,0,1:T(8,128)(2,1)}, u32[]{:S(2)}, u32[]{:S(2)}) collective-permute-start(bf16[4,2,160,640]{3,2,0,1:T(8,128)(2,1)} %bitcast.300), channel_id=1, source_target_pairs={{0,1},{1,0},{2,3},{3,2},{4,5},{5,4},{6,7},{7,6},{8,9},{9,8},{10,11... | collective-permute-start | bytes 4915208 | tf_op jit(solution)/shard_map/ppermute | solution.py:70
  348.3 46.6 %collective-permute-start.9 = (bf16[4,2,160,640]{3,2,0,1:T(8,128)(2,1)}, bf16[4,2,160,640]{3,2,0,1:T(8,128)(2,1)}, u32[]{:S(2)}, u32[]{:S(2)}) collective-permute-start(bf16[4,2,160,640]{3,2,0,1:T(8,128)(2,1)} %bitcast.299), channel_id=1, source_target_pairs={{0,16},{16,0},{1,17},{17,1},{2,18},{18,2},{3,19},{19,3},{4,20},{20... | collective-permute-start | bytes 4915208 | tf_op jit(solution)/shard_map/ppermute | solution.py:70
  348.3 41.2 %all-to-all-start.3 = ((bf16[4,512,160]{1,2,0:T(8,128)(2,1)}), bf16[4,512,160]{1,2,0:T(8,128)(2,1)}, u32[]{:S(2)}, u32[]{:S(2)}) async-start(bf16[4,512,160]{1,2,0:T(8,128)(2,1)} %get-tuple-element.80), calls=%async_computation.3 | async-start | bytes 1310720 | tf_op jit(solution)/shard_map/all_to_all | solution.py:613
  353.0 352.2 %reduce-scatter.2.cloned.1.call-start = ((), (), s32[]{:S(2)}) async-start(), calls=%async_computation.7 | async-start | bytes 5406720 | tf_op jit(solution)/shard_map/reduce_scatter | solution.py:618
  398.0 39.1 %slice-start.4 = ((s8[5242880]{0:T(1024)(128)(4,1)}), s8[4194304]{0:T(1024)(128)(4,1)S(1)}, s32[]{:S(2)}) async-start(s8[5242880]{0:T(1024)(128)(4,1)} %bitcast.325), calls=%async_computation.12 | async-start | bytes 8388608
  400.4 82.5 %collective-permute-start.10 = (bf16[4,160,640]{2,1,0:T(8,128)(2,1)}, bf16[4,160,640]{2,1,0:T(8,128)(2,1)}, u32[]{:S(2)}, u32[]{:S(2)}) collective-permute-start(bf16[4,160,640]{2,1,0:T(8,128)(2,1)} %dynamic-slice_bitcast_fusion.3), channel_id=1, source_target_pairs={{0,16},{16,0},{1,17},{17,1},{2,18},{18,2},{3,19},{19,3},{4,20},{20... | collective-permute-start | bytes 2457608 | tf_op jit(solution)/shard_map/ppermute | solution.py:70
  401.4 63.8 %collective-permute-start.11 = (bf16[4,160,640]{2,1,0:T(8,128)(2,1)}, bf16[4,160,640]{2,1,0:T(8,128)(2,1)}, u32[]{:S(2)}, u32[]{:S(2)}) collective-permute-start(bf16[4,160,640]{2,1,0:T(8,128)(2,1)} %dynamic-slice_bitcast_fusion.2), channel_id=1, source_target_pairs={{0,1},{1,0},{2,3},{3,2},{4,5},{5,4},{6,7},{7,6},{8,9},{9,8},{10,11... | collective-permute-start | bytes 2457608 | tf_op jit(solution)/shard_map/ppermute | solution.py:70
  402.9 34.3 %slice-start.5 = ((s8[5242880]{0:T(1024)(128)(4,1)}), s8[1048576]{0:T(1024)(128)(4,1)S(1)}, s32[]{:S(2)}) async-start(s8[5242880]{0:T(1024)(128)(4,1)} %bitcast.325), calls=%async_computation.13 | async-start | bytes 2097152
  402.9 38.8 %slice-start.2 = ((s8[5242880]{0:T(1024)(128)(4,1)}), s8[1048576]{0:T(1024)(128)(4,1)S(1)}, s32[]{:S(2)}) async-start(s8[5242880]{0:T(1024)(128)(4,1)} %bitcast.315), calls=%async_computation.10 | async-start | bytes 2097152
  453.1 71.0 %collective-permute-start.13 = (bf16[4,2,160,640]{3,2,0,1:T(8,128)(2,1)}, bf16[4,2,160,640]{3,2,0,1:T(8,128)(2,1)}, u32[]{:S(2)}, u32[]{:S(2)}) collective-permute-start(bf16[4,2,160,640]{3,2,0,1:T(8,128)(2,1)} %bitcast.298), channel_id=1, source_target_pairs={{0,16},{16,0},{1,17},{17,1},{2,18},{18,2},{3,19},{19,3},{4,20},{20... | collective-permute-start | bytes 4915208 | tf_op jit(solution)/shard_map/ppermute | solution.py:70
  464.7 63.6 %collective-permute-start.14 = (bf16[4,2,160,640]{3,2,0,1:T(8,128)(2,1)S(1)}, bf16[4,2,160,640]{3,2,0,1:T(8,128)(2,1)S(1)}, u32[]{:S(2)}, u32[]{:S(2)}) collective-permute-start(bf16[4,2,160,640]{3,2,0,1:T(8,128)(2,1)S(1)} %bitcast.335), channel_id=1, source_target_pairs={{0,1},{1,0},{2,3},{3,2},{4,5},{5,4},{6,7},{7,6},{8,9},{9,8},{10,11... | collective-permute-start | bytes 4915208 | tf_op jit(solution)/shard_map/ppermute | solution.py:70
  467.3 49.5 %copy-start.34 = (bf16[4,160,640]{2,1,0:T(8,128)(2,1)}, bf16[4,160,640]{2,1,0:T(8,128)(2,1)S(1)}, u32[]{:S(2)}) copy-start(bf16[4,160,640]{2,1,0:T(8,128)(2,1)S(1)} %fusion.53.refs_1_) | copy-start | bytes 2457604
  467.4 32.1 %collective-permute-start.22 = (bf16[160,640]{1,0:T(8,128)(2,1)S(1)}, bf16[160,640]{1,0:T(8,128)(2,1)S(1)}, u32[]{:S(2)}, u32[]{:S(2)}) collective-permute-start(bf16[160,640]{1,0:T(8,128)(2,1)S(1)} %get-tuple-element.98), channel_id=1, source_target_pairs={{0,6},{2,4},{4,2},{6,0},{1,7},{3,5},{5,3},{7,1},{8,14},{10,12},{12... | collective-permute-start | bytes 614408 | tf_op jit(solution)/shard_map/ppermute | solution.py:70
  481.9 30.8 %collective-permute-start.21 = (bf16[160,640]{1,0:T(8,128)(2,1)S(1)}, bf16[160,640]{1,0:T(8,128)(2,1)S(1)}, u32[]{:S(2)}, u32[]{:S(2)}) collective-permute-start(bf16[160,640]{1,0:T(8,128)(2,1)S(1)} %get-tuple-element.99), channel_id=1, source_target_pairs={{0,4},{2,6},{4,0},{6,2},{1,5},{3,7},{5,1},{7,3},{8,12},{10,14},{12... | collective-permute-start | bytes 614408 | tf_op jit(solution)/shard_map/ppermute | solution.py:70
  482.9 33.7 %collective-permute-start.20 = (bf16[160,640]{1,0:T(8,128)(2,1)S(1)}, bf16[160,640]{1,0:T(8,128)(2,1)S(1)}, u32[]{:S(2)}, u32[]{:S(2)}) collective-permute-start(bf16[160,640]{1,0:T(8,128)(2,1)S(1)} %get-tuple-element.97), channel_id=1, source_target_pairs={{0,2},{2,0},{4,6},{6,4},{1,3},{3,1},{5,7},{7,5},{8,10},{10,8},{12,... | collective-permute-start | bytes 614408 | tf_op jit(solution)/shard_map/ppermute | solution.py:70
  485.7 38.5 %copy-start.35 = (bf16[4,160,640]{2,1,0:T(8,128)(2,1)}, bf16[4,160,640]{2,1,0:T(8,128)(2,1)S(1)}, u32[]{:S(2)}) copy-start(bf16[4,160,640]{2,1,0:T(8,128)(2,1)S(1)} %fusion.54.refs_0_) | copy-start | bytes 2457604
  485.7 38.5 %copy-start.38 = (bf16[4,2,1,1,160,640]{5,4,3,2,1,0:T(8,128)(2,1)S(1)}, bf16[4,2,1,1,160,640]{5,4,3,2,1,0:T(8,128)(2,1)}, u32[]{:S(2)}) copy-start(bf16[4,2,1,1,160,640]{5,4,3,2,1,0:T(8,128)(2,1)} %get-tuple-element.64) | copy-start | bytes 4915204
  499.5 19.1 %collective-permute-start.19 = (bf16[160,640]{1,0:T(8,128)(2,1)S(1)}, bf16[160,640]{1,0:T(8,128)(2,1)S(1)}, u32[]{:S(2)}, u32[]{:S(2)}) collective-permute-start(bf16[160,640]{1,0:T(8,128)(2,1)S(1)} %get-tuple-element.95), channel_id=1, source_target_pairs={{0,6},{2,4},{4,2},{6,0},{1,7},{3,5},{5,3},{7,1},{8,14},{10,12},{12... | collective-permute-start | bytes 614408 | tf_op jit(solution)/shard_map/ppermute | solution.py:70
  512.7 9.7 %collective-permute-start.18 = (bf16[160,640]{1,0:T(8,128)(2,1)S(1)}, bf16[160,640]{1,0:T(8,128)(2,1)S(1)}, u32[]{:S(2)}, u32[]{:S(2)}) collective-permute-start(bf16[160,640]{1,0:T(8,128)(2,1)S(1)} %get-tuple-element.96), channel_id=1, source_target_pairs={{0,4},{2,6},{4,0},{6,2},{1,5},{3,7},{5,1},{7,3},{8,12},{10,14},{12... | collective-permute-start | bytes 614408 | tf_op jit(solution)/shard_map/ppermute | solution.py:70
  516.6 6.4 collective-permute-start.17
  531.0 47.9 %collective-permute-start.15 = (bf16[4,160,640]{2,1,0:T(8,128)(2,1)}, bf16[4,160,640]{2,1,0:T(8,128)(2,1)}, u32[]{:S(2)}, u32[]{:S(2)}) collective-permute-start(bf16[4,160,640]{2,1,0:T(8,128)(2,1)} %dynamic-slice_bitcast_fusion.1), channel_id=1, source_target_pairs={{0,1},{1,0},{2,3},{3,2},{4,5},{5,4},{6,7},{7,6},{8,9},{9,8},{10,11... | collective-permute-start | bytes 2457608 | tf_op jit(solution)/shard_map/ppermute | solution.py:70
  531.0 50.1 %collective-permute-start.16 = (bf16[4,160,640]{2,1,0:T(8,128)(2,1)}, bf16[4,160,640]{2,1,0:T(8,128)(2,1)}, u32[]{:S(2)}, u32[]{:S(2)}) collective-permute-start(bf16[4,160,640]{2,1,0:T(8,128)(2,1)} %dynamic-slice_bitcast_fusion), channel_id=1, source_target_pairs={{0,16},{16,0},{1,17},{17,1},{2,18},{18,2},{3,19},{19,3},{4,20},{20... | collective-permute-start | bytes 2457608 | tf_op jit(solution)/shard_map/ppermute | solution.py:70
  578.9 38.9 %collective-permute-start.27 = (bf16[2,2,320,480]{3,2,0,1:T(8,128)(2,1)}, bf16[2,2,320,480]{3,2,0,1:T(8,128)(2,1)}, u32[]{:S(2)}, u32[]{:S(2)}) collective-permute-start(bf16[2,2,320,480]{3,2,0,1:T(8,128)(2,1)} %bitcast.301), channel_id=1, source_target_pairs={{0,8},{8,0},{1,9},{9,1},{2,10},{10,2},{3,11},{11,3},{4,12},{12,4},... | collective-permute-start | bytes 3686408 | tf_op jit(solution)/shard_map/ppermute | solution.py:70
  601.0 35.6 %collective-permute-start.23 = (bf16[2,256,1280]{2,1,0:T(8,128)(2,1)}, bf16[2,256,1280]{2,1,0:T(8,128)(2,1)}, u32[]{:S(2)}, u32[]{:S(2)}) collective-permute-start(bf16[2,256,1280]{2,1,0:T(8,128)(2,1)} %slice_bitcast_fusion.4), channel_id=1, source_target_pairs={{0,2},{2,0},{1,3},{3,1},{4,6},{6,4},{5,7},{7,5},{8,10},{10,8},{9,1... | collective-permute-start | bytes 3932168 | tf_op jit(solution)/shard_map/ppermute | solution.py:70
  602.8 39.1 %collective-permute-start.25 = (bf16[2,256,1280]{2,1,0:T(8,128)(2,1)}, bf16[2,256,1280]{2,1,0:T(8,128)(2,1)}, u32[]{:S(2)}, u32[]{:S(2)}) collective-permute-start(bf16[2,256,1280]{2,1,0:T(8,128)(2,1)} %slice_bitcast_fusion.1), channel_id=1, source_target_pairs={{0,1},{1,0},{2,3},{3,2},{4,5},{5,4},{6,7},{7,6},{8,9},{9,8},{10,11... | collective-permute-start | bytes 3932168 | tf_op jit(solution)/shard_map/ppermute | solution.py:70
  603.7 47.5 %collective-permute-start.35 = (bf16[160,640]{1,0:T(8,128)(2,1)S(1)}, bf16[160,640]{1,0:T(8,128)(2,1)S(1)}, u32[]{:S(2)}, u32[]{:S(2)}) collective-permute-start(bf16[160,640]{1,0:T(8,128)(2,1)S(1)} %get-tuple-element.92), channel_id=1, source_target_pairs={{0,6},{2,4},{4,2},{6,0},{1,7},{3,5},{5,3},{7,1},{8,14},{10,12},{12... | collective-permute-start | bytes 614408 | tf_op jit(solution)/shard_map/ppermute | solution.py:70
  617.0 42.4 %collective-permute-start.34 = (bf16[160,640]{1,0:T(8,128)(2,1)S(1)}, bf16[160,640]{1,0:T(8,128)(2,1)S(1)}, u32[]{:S(2)}, u32[]{:S(2)}) collective-permute-start(bf16[160,640]{1,0:T(8,128)(2,1)S(1)} %get-tuple-element.93), channel_id=1, source_target_pairs={{0,4},{2,6},{4,0},{6,2},{1,5},{3,7},{5,1},{7,3},{8,12},{10,14},{12... | collective-permute-start | bytes 614408 | tf_op jit(solution)/shard_map/ppermute | solution.py:70
  617.8 41.6 %collective-permute-start.33 = (bf16[160,640]{1,0:T(8,128)(2,1)S(1)}, bf16[160,640]{1,0:T(8,128)(2,1)S(1)}, u32[]{:S(2)}, u32[]{:S(2)}) collective-permute-start(bf16[160,640]{1,0:T(8,128)(2,1)S(1)} %get-tuple-element.91), channel_id=1, source_target_pairs={{0,2},{2,0},{4,6},{6,4},{1,3},{3,1},{5,7},{7,5},{8,10},{10,8},{12,... | collective-permute-start | bytes 614408 | tf_op jit(solution)/shard_map/ppermute | solution.py:70
  636.5 23.1 %collective-permute-start.28 = (bf16[2,320,480]{2,1,0:T(8,128)(2,1)S(1)}, bf16[2,320,480]{2,1,0:T(8,128)(2,1)S(1)}, u32[]{:S(2)}, u32[]{:S(2)}) collective-permute-start(bf16[2,320,480]{2,1,0:T(8,128)(2,1)S(1)} %dynamic-slice_bitcast_fusion.4), channel_id=1, source_target_pairs={{0,16},{16,0},{1,17},{17,1},{2,18},{18,2},{3,19},{19,3},{4,20},{20... | collective-permute-start | bytes 1843208 | tf_op jit(solution)/shard_map/ppermute | solution.py:70
  644.2 25.2 %collective-permute-start.26 = (bf16[256,1280]{1,0:T(8,128)(2,1)S(1)}, bf16[256,1280]{1,0:T(8,128)(2,1)S(1)}, u32[]{:S(2)}, u32[]{:S(2)}) collective-permute-start(bf16[256,1280]{1,0:T(8,128)(2,1)S(1)} %fusion.76), channel_id=1, source_target_pairs={{0,2},{2,0},{1,3},{3,1},{4,6},{6,4},{5,7},{7,5},{8,10},{10,8},{9,1... | collective-permute-start | bytes 1966088 | tf_op jit(solution)/shard_map/ppermute | solution.py:70
  651.2 42.3 %collective-permute-start.32 = (bf16[160,640]{1,0:T(8,128)(2,1)}, bf16[160,640]{1,0:T(8,128)(2,1)}, u32[]{:S(2)}, u32[]{:S(2)}) collective-permute-start(bf16[160,640]{1,0:T(8,128)(2,1)} %get-tuple-element.89), channel_id=1, source_target_pairs={{0,6},{2,4},{4,2},{6,0},{1,7},{3,5},{5,3},{7,1},{8,14},{10,12},{12... | collective-permute-start | bytes 614408 | tf_op jit(solution)/shard_map/ppermute | solution.py:70
  659.4 34.1 %collective-permute-start.31 = (bf16[160,640]{1,0:T(8,128)(2,1)S(1)}, bf16[160,640]{1,0:T(8,128)(2,1)}, u32[]{:S(2)}, u32[]{:S(2)}) collective-permute-start(bf16[160,640]{1,0:T(8,128)(2,1)S(1)} %get-tuple-element.90), channel_id=1, source_target_pairs={{0,4},{2,6},{4,0},{6,2},{1,5},{3,7},{5,1},{7,3},{8,12},{10,14},{12... | collective-permute-start | bytes 614408 | tf_op jit(solution)/shard_map/ppermute | solution.py:70
  659.4 15.5 %collective-permute-start.24 = (bf16[256,1280]{1,0:T(8,128)(2,1)S(1)}, bf16[256,1280]{1,0:T(8,128)(2,1)S(1)}, u32[]{:S(2)}, u32[]{:S(2)}) collective-permute-start(bf16[256,1280]{1,0:T(8,128)(2,1)S(1)} %fusion.75), channel_id=1, source_target_pairs={{0,1},{1,0},{2,3},{3,2},{4,5},{5,4},{6,7},{7,6},{8,9},{9,8},{10,11... | collective-permute-start | bytes 1966088 | tf_op jit(solution)/shard_map/ppermute | solution.py:70
  659.6 33.9 %collective-permute-start.30 = (bf16[160,640]{1,0:T(8,128)(2,1)S(1)}, bf16[160,640]{1,0:T(8,128)(2,1)}, u32[]{:S(2)}, u32[]{:S(2)}) collective-permute-start(bf16[160,640]{1,0:T(8,128)(2,1)S(1)} %get-tuple-element.88), channel_id=1, source_target_pairs={{0,2},{2,0},{4,6},{6,4},{1,3},{3,1},{5,7},{7,5},{8,10},{10,8},{12,... | collective-permute-start | bytes 614408 | tf_op jit(solution)/shard_map/ppermute | solution.py:70
  680.8 10.6 %collective-permute-start.36 = (f32[13,1280]{1,0:T(8,128)S(1)}, f32[13,1280]{1,0:T(8,128)S(1)}, u32[]{:S(2)}, u32[]{:S(2)}) collective-permute-start(f32[13,1280]{1,0:T(8,128)S(1)} %concatenate.62), channel_id=1, source_target_pairs={{0,8},{8,0},{1,9},{9,1},{2,10},{10,2},{3,11},{11,3},{4,12},{12,4},... | collective-permute-start | bytes 199688 | tf_op jit(solution)/shard_map/ppermute | solution.py:70
  680.9 24.2 %collective-permute-start.29 = (bf16[320,480]{1,0:T(8,128)(2,1)S(1)}, bf16[320,480]{1,0:T(8,128)(2,1)S(1)}, u32[]{:S(2)}, u32[]{:S(2)}) collective-permute-start(bf16[320,480]{1,0:T(8,128)(2,1)S(1)} %dynamic-slice_bitcast_fusion.5), channel_id=1, source_target_pairs={{0,4},{4,0},{1,5},{5,1},{2,6},{6,2},{3,7},{7,3},{8,12},{12,8},{9,1... | collective-permute-start | bytes 921608 | tf_op jit(solution)/shard_map/ppermute | solution.py:70
  691.4 4.9 collective-permute-start.37
  696.3 4.5 collective-permute-start.38
  700.8 10.8 %collective-permute-start.39 = (f32[13,1280]{1,0:T(8,128)S(1)}, f32[13,1280]{1,0:T(8,128)S(1)}, u32[]{:S(2)}, u32[]{:S(2)}) collective-permute-start(f32[13,1280]{1,0:T(8,128)S(1)} %add.465), channel_id=1, source_target_pairs={{0,2},{2,0},{1,3},{3,1},{4,6},{6,4},{5,7},{7,5},{8,10},{10,8},{9,1... | collective-permute-start | bytes 199688 | tf_op jit(solution)/shard_map/ppermute | solution.py:70
  711.6 10.0 %collective-permute-start.40 = (f32[13,1280]{1,0:T(8,128)S(1)}, f32[13,1280]{1,0:T(8,128)S(1)}, u32[]{:S(2)}, u32[]{:S(2)}) collective-permute-start(f32[13,1280]{1,0:T(8,128)S(1)} %add.466), channel_id=1, source_target_pairs={{0,4},{4,0},{1,5},{5,1},{2,6},{6,2},{3,7},{7,3},{8,12},{12,8},{9,1... | collective-permute-start | bytes 199688 | tf_op jit(solution)/shard_map/ppermute | solution.py:70
  (68 other events, 509.0 us)
Sparse Core Ops, SparseCore 0:
  11.5 158.1 all-gather.2
  172.6 107.3 all-gather.4
  375.9 140.7 reduce-scatter.1

commit v3 on v2

--- a/solution.py
+++ b/solution.py
@@ -119,11 +119,16 @@
 
 
 def sum_everywhere(value):
-    for axis in ("c", "x", "y", "zl", "zh"):
+    for axis, size in (("c", 2), (("x", "y"), lax.axis_size("x") * lax.axis_size("y")), (LINE, 2 * lax.axis_size("zh"))):
         far = 1
-        while far < lax.axis_size(axis):
-            value = value + swap(value, axis, far)
-            far *= 2
+        while far < size:
+            if far * 4 <= size:
+                one, two, three = (swap(value, axis, k * far) for k in (1, 2, 3))
+                value = (value + one) + (two + three)
+                far *= 4
+            else:
+                value = value + swap(value, axis, far)
+                far *= 2
     return value
 
 
@@ -650,6 +655,7 @@
     three = 3 * columns
     partial = sum(nt(some, qkv[:, g * three : (g + 1) * three]) for g, some in enumerate(heads_grad))
     partial = partial.astype(LOW).reshape(2, 2, ys, half, width)
+    heads_grad[-1] = tie(heads_grad[-1], partial)
     some = scatter_near([partial[0, l] for l in range(2)], "zl")
     some_a = scatter_near([some[j] for j in range(ys)], "y")
     some = scatter_near([partial[1, :, j] for j in range(ys)], "y")

time: 735 us -> 730 us (level)
  starting transfers between devices: 121 us -> 91.3 us
  Pallas kernels: 132 us -> 154 us
    ppermute x41 -> x43, starting transfers between devices: 100 us -> 70.2 us  [swap(): lax.ppermute(value, axis, [(i, i ^ far) for i in range(lax.axis_size(axis...]
    ppermute x41 -> x43, waiting for transfers between devices: 118 us -> 138 us  [swap(): lax.ppermute(value, axis, [(i, i ^ far) for i in range(lax.axis_size(axis...]
    all_gather x1, waiting for transfers between devices: 16.9 us -> 0.01 us  [local(): down_w = lax.all_gather(down, everyone, axis=0, tiled=True)]
    pallas_call x2, Pallas kernels: 49.4 us -> 60.9 us  [attend(): pl.pallas_call(functools.partial(attend_kernel, heads, tile), grid_spec=p...]
    pallas_call x2, Pallas kernels: 68.3 us -> 78.7 us  [attend_back(): pl.pallas_call(functools.partial(attend_back_kernel, heads, tile, members...]
    unnamed x177 -> x171, local copies, waits for them, and re-layouts: 20.4 us -> 21.5 us
  transfers between devices with their start and end apart: 48 -> 50, of which waited for: 17 -> 15; matrix products, arithmetic and copies ran while one was open for 36% -> 36% of each run, Pallas kernels for 18% -> 21%
where the time goes in v3:
time: 730 us; the launch traced here: 728 us
  waiting for transfers between devices  158 us (22%)
  Pallas kernels  154 us (21%)
  matrix products  142 us (19%)
  local copies, waits for them, and re-layouts  96 us (13%)
  starting transfers between devices  91.3 us (13%)
  other arithmetic  71 us (10%)
  between operations  15.4 us (2%)
    ppermute x43, waiting for transfers between devices, swap(): lax.ppermute(value, axis, [(i, i ^ far) for i in range(lax.axis_size(axis...  138 us
    pallas_call x2, Pallas kernels, attend_back(): pl.pallas_call(functools.partial(attend_back_kernel, heads, tile, members...  78.7 us
    ppermute x43, starting transfers between devices, swap(): lax.ppermute(value, axis, [(i, i ^ far) for i in range(lax.axis_size(axis...  70.2 us
    pallas_call x2, Pallas kernels, attend(): pl.pallas_call(functools.partial(attend_kernel, heads, tile), grid_spec=p...  60.9 us
    dot_general x5, matrix products, dot(): return lax.dot_general(a, b, (dims, ((), ())), preferred_element_type=FULL)  34 us
    unnamed x171, local copies, waits for them, and re-layouts  21.5 us
    dot_general x1, matrix products, local(): jnp.einsum('ni,tij->tnj', cotangent, down_w, preferred_element_type=FULL)  16.8 us
    dot_general x2, matrix products, first_sum(): mine = jnp.einsum('ni,tnj->tij', mine, right, preferred_element_type=FULL)  15.6 us
  transfers between devices with their start and end apart: 50, of which 15 were waited for; matrix products, arithmetic and copies ran while one was open for 36% of the time, Pallas kernels for 21%

profile of v3, /device:TPU:8, one launch (start us, length us, event | category | flops | bytes accessed | tf_op | source)
XLA Modules:
  0.0 728.2 jit_solution(8504699873119226261)
XLA Ops:
  18.4 2.7 collective-permute-start.4
  28.0 5.6 fusion.111.bias_ref
  33.6 20.8 %collective-permute-done.4 = bf16[320,480]{0,1:T(8,128)(2,1)} collective-permute-done((bf16[320,480]{0,1:T(8,128)(2,1)S(1)}, bf16[320,480]{0,1:T(8,128)(2,1)}, u32[]{:S(2)}, u32[]{:S(2)}) %collective-permute-start.4) | collective-permute-done | bytes 307232 | tf_op jit(solution)/shard_map/ppermute | solution.py:70
  56.5 2.4 copy.363
  60.4 2.4 pad_maximum_fusion.10
  67.8 21.6 %collective-permute-done.5 = bf16[320,960]{1,0:T(8,128)(2,1)} collective-permute-done((bf16[320,960]{1,0:T(8,128)(2,1)}, bf16[320,960]{1,0:T(8,128)(2,1)}, u32[]{:S(2)}, u32[]{:S(2)}) %collective-permute-start.5) | collective-permute-done | bytes 614432 | tf_op jit(solution)/shard_map/ppermute | solution.py:70
  95.5 2.5 copy.366
  101.0 9.6 %collective-permute-done.1 = bf16[512,1280]{1,0:T(8,128)(2,1)} collective-permute-done((bf16[512,1280]{1,0:T(8,128)(2,1)}, bf16[512,1280]{1,0:T(8,128)(2,1)}, u32[]{:S(2)}, u32[]{:S(2)}) %collective-permute-start.1) | collective-permute-done | bytes 1310752 | tf_op jit(solution)/shard_map/ppermute | solution.py:70
  110.6 4.1 pad_maximum_fusion.rows_ref
  114.7 2.8 copy.367
  121.9 5.0 copy.369
  126.9 8.7 %convolution_convert_fusion.w_ref = bf16[1280,1536]{1,0:T(8,128)(2,1)} fusion(bf16[1280,960]{1,0:T(8,128)(2,1)} %bitcast.319, bf16[960,1536]{1,0:T(8,128)(2,1)} %constant.297.clone), kind=kOutput, calls=%fused_computation.26 | convolution fusion | flops 3776839680 | bytes 9338880 | tf_op jit(solution)/shard_map/dot_general | solution.py:35
  135.7 14.7 %project.1 = (bf16[2048,512]{1,0:T(8,128)(2,1)S(1)}, bf16[2048,512]{1,0:T(8,128)(2,1)}, bf16[2048,512]{1,0:T(8,128)(2,1)}, bf16[512,2048]{1,0:T(8,128)(2,1)}, bf16[512,2048]{1,0:T(8,128)(2,1)}) custom-call(s32[17]{0:T(128)S(1)} %pad_add_fusion.info_ref, bf16[2048,1280]{1,0:T(8,128)(2,1)} %pad_maximum_fusion.rows_ref, ...), custom_call_target="tpu_custom_call" | custom-call | flops 8053063680 | bytes 19660800 | tf_op jit(solution)/shard_map/project/pallas_call | solution.py:170
  150.4 30.5 %attend.2 = (bf16[2048,160]{1,0:T(8,128)(2,1)S(1)}, f32[8,2,256]{2,1,0:T(2,128)S(1)}) custom-call(s32[17]{0:T(128)S(1)} %pad_add_fusion.info_ref, bf16[2048,512]{1,0:T(8,128)(2,1)S(1)} %get-tuple-element.17.q_ref, bf16[2048,512]{1,0:T(8,128)(2,1)} %get-tuple-element.18.k_ref, bf16[512,2048]{1,0:T(8,128)(2,1)} %get-tuple-element.19.vt_ref, ...), custom_call_target="tpu_custom_call" | custom-call | flops 2147483648 | bytes 4194304 | tf_op jit(solution)/shard_map/attend/pallas_call | solution.py:239
  184.2 6.3 all-to-all-start
  190.5 30.4 %attend.3 = (bf16[2048,160]{1,0:T(8,128)(2,1)S(1)}, f32[8,2,256]{2,1,0:T(2,128)S(1)}) custom-call(s32[17]{0:T(128)S(1)} %pad_add_fusion.info_ref, bf16[2048,512]{1,0:T(8,128)(2,1)S(1)} %copy-done.6, bf16[2048,512]{1,0:T(8,128)(2,1)} %get-tuple-element.18.k_ref, bf16[512,2048]{1,0:T(8,128)(2,1)} %get-tuple-element.19.vt_ref, s32[8,1,256]{2,1,0:T(1,128)S(1)} %bitcast.304, ...), custom_call_target="tpu_custom_call" | custom-call | flops 2147483648 | bytes 4194304 | tf_op jit(solution)/shard_map/attend/pallas_call | solution.py:239
  224.1 4.4 all-to-all-start.1
  230.2 2.9 broadcast_select_fusion.3
  235.1 14.0 %all-to-all-done.1 = bf16[4,512,160]{1,2,0:T(8,128)(2,1)S(1)} async-done(((bf16[4,512,160]{1,2,0:T(8,128)(2,1)}), bf16[4,512,160]{1,2,0:T(8,128)(2,1)S(1)}, u32[]{:S(2)}, u32[]{:S(2)}) %all-to-all-start.1) | async-done | bytes 655392 | tf_op jit(solution)/shard_map/all_to_all | solution.py:556
  250.0 6.1 fusion.110
  258.0 13.8 %fusion.14 = (bf16[8,512,640]{2,1,0:T(8,128)(2,1)S(1)}, f32[8,640,512]{1,2,0:T(8,128)}) fusion(f32[8,640]{1,0:T(8,128)S(1)} %add.411, bf16[8,1280,800]{2,1,0:T(8,128)(2,1)} %bitcast.346, bf16[512,1280]{1,0:T(8,128)(2,1)S(1)} %add_convert_fusion.2), kind=kOutput, calls=%fused_computation.25 | convolution fusion | flops 6729236480 | bytes 30167040 | tf_op jit(solution)/shard_map/nd,tdj->tnj/dot_general | solution.py:565
  271.8 5.4 convert_bitcast_fusion.1
  279.5 2.5 broadcast_select_fusion.1
  282.0 16.8 %fusion.9.refs_0_ = bf16[8,512,640]{2,1,0:T(8,128)(2,1)} fusion(f32[8,640,512]{1,2,0:T(8,128)} %get-tuple-element.111, f32[8,640]{1,0:T(8,128)S(1)} %add.411, bf16[8,1280,640]{2,1,0:T(8,128)(2,1)} %bitcast.349, bf16[512,1280]{1,0:T(8,128)(2,1)S(1)} %copy-done.44), kind=kOutput, calls=%fused_computation.14 | convolution fusion | flops 6744965120 | bytes 30167040 | tf_op jit(solution)/shard_map/ni,tij->tnj/dot_general | solution.py:599
  298.9 7.3 %fusion.1.refs_1_ = bf16[8,640,640]{2,1,0:T(8,128)(2,1)} fusion(bf16[8,640,640]{2,1,0:T(8,128)(2,1)} %collective-permute-done.7, bf16[512,640,1]{0,1,2:T(8,128)(2,1)S(1)} %bitcast.336, bf16[8,512,640]{2,1,0:T(8,128)(2,1)S(1)} %bitcast.352), kind=kOutput, calls=%fused_computation.6 | convolution fusion | flops 3365273600 | bytes 19005440 | tf_op jit(solution)/shard_map/ni,tnj->tij/dot_general | solution.py:580
  308.0 11.8 %multiply_reduce_fusion = (f32[1280]{0:T(1024)S(1)}, f32[512]{0:T(512)S(1)}, f32[1280]{0:T(1024)S(1)}, f32[512,1280]{1,0:T(8,128)S(1)}) fusion(f32[512,1280]{1,0:T(8,128)S(1)} %copy-done.20, f32[512]{0:T(512)S(1)} %fusion.91, f32[512]{0:T(512)S(1)} %broadcast_multiply_fusion.2, f32[1280]{0:T(1024)S(1)} %get-tuple-element.35, bf16[8,512,640]{2,1,0:T(8,128)(2,1)} %tie.3, ...), kind=kOutput, calls=%fused_computation.88 | convolution fusion | flops 6716126208 | bytes 23614464 | tf_op jit(solution)/shard_map/tnj,tdj->nd/dot_general | solution.py:602
  321.1 6.0 fusion.58
  328.3 5.6 all-to-all-start.2
  333.9 9.2 %convert_bitcast_fusion = bf16[8,640,640]{2,1,0:T(8,128)(2,1)} fusion(bf16[512,640,1]{0,1,2:T(8,128)(2,1)} %bitcast.337, bf16[8,512,640]{2,1,0:T(8,128)(2,1)} %tie.3), kind=kOutput, calls=%fused_computation.27 | convolution fusion | flops 3358720000 | bytes 12451840 | tf_op jit(solution)/shard_map/ni,tnj->tij/dot_general | solution.py:578
  353.8 4.7 all-to-all-start.3
  358.5 14.2 %fusion.41 = bf16[512,1280]{1,0:T(8,128)(2,1)} fusion(f32[512,1280]{1,0:T(8,128)S(1)} %copy-done.20, bf16[8,512,640]{2,1,0:T(8,128)(2,1)} %copy-done.72, bf16[8,1280,640]{2,1,0:T(8,128)(2,1)} %bitcast.350, f32[1280]{0:T(1024)S(1)} %copy-done.69), kind=kOutput, calls=%fused_computation.64 | convolution fusion | flops 6712852480 | bytes 22287360 | tf_op jit(solution)/shard_map/tnj,tij->ni/dot_general | solution.py:568
  372.7 3.8 fusion.23
  376.5 4.8 copy.416
  381.4 3.3 convert_reduce_fusion
  386.1 6.4 all-to-all-done.3
  403.5 3.4 collective-permute-start.10
  409.3 39.4 %attend_back.2.refs_4_ = bf16[2048,480]{1,0:T(8,128)(2,1)} custom-call(s32[17]{0:T(128)} %copy-done.13, bf16[2048,512]{1,0:T(8,128)(2,1)} %copy-done.5, bf16[2048,512]{1,0:T(8,128)(2,1)} %get-tuple-element.18.k_ref, bf16[2048,512]{1,0:T(8,128)(2,1)} %get-tuple-element.23.v_ref, bf16[512,2048]{1,0:T(8,128)(2,1)} %get-tuple-element.24.kt_ref, ...), custom_call_target="tpu_custom_call" | custom-call | flops 5368709120 | bytes 9437184 | tf_op jit(solution)/shard_map/attend_back/pallas_call | solution.py:390
  448.7 4.4 convolution_convert_fusion.3
  453.9 8.3 %fusion = bf16[8,640,640]{2,1,0:T(8,128)(2,1)S(1)} fusion(bf16[8,640,640]{2,1,0:T(8,128)(2,1)} %collective-permute-done.12, bf16[512,640,1]{0,1,2:T(8,128)(2,1)} %bitcast.335, bf16[8,512,640]{2,1,0:T(8,128)(2,1)} %tie.3), kind=kOutput, calls=%fused_computation.4 | convolution fusion | flops 3365273600 | bytes 19005440 | tf_op jit(solution)/shard_map/ni,tnj->tij/dot_general | solution.py:580
  473.9 4.5 collective-permute-start.22
  481.4 13.7 %collective-permute-done.22 = bf16[160,640]{1,0:T(8,128)(2,1)S(1)} collective-permute-done((bf16[160,640]{1,0:T(8,128)(2,1)S(1)}, bf16[160,640]{1,0:T(8,128)(2,1)S(1)}, u32[]{:S(2)}, u32[]{:S(2)}) %collective-permute-start.22) | collective-permute-done | bytes 204832 | tf_op jit(solution)/shard_map/ppermute | solution.py:70
  495.1 7.0 collective-permute-start.19
  503.9 8.5 %collective-permute-start.18 = (bf16[160,640]{1,0:T(8,128)(2,1)S(1)}, bf16[160,640]{1,0:T(8,128)(2,1)S(1)}, u32[]{:S(2)}, u32[]{:S(2)}) collective-permute-start(bf16[160,640]{1,0:T(8,128)(2,1)S(1)} %get-tuple-element.96), channel_id=1, source_target_pairs={{0,4},{2,6},{4,0},{6,2},{1,5},{3,7},{5,1},{7,3},{8,12},{10,14},{12... | collective-permute-start | bytes 614408 | tf_op jit(solution)/shard_map/ppermute | solution.py:70
  512.5 2.6 collective-permute-done.19
  515.1 5.2 collective-permute-done.18
  527.4 39.3 %attend_back.3.refs_1_.refs_0_ = bf16[2048,480]{1,0:T(8,128)(2,1)} custom-call(s32[17]{0:T(128)} %copy-done.13, bf16[2048,512]{1,0:T(8,128)(2,1)} %copy-done.5, bf16[2048,512]{1,0:T(8,128)(2,1)} %get-tuple-element.18.k_ref, bf16[2048,512]{1,0:T(8,128)(2,1)} %get-tuple-element.23.v_ref, bf16[512,2048]{1,0:T(8,128)(2,1)} %get-tuple-element.24.kt_ref, ...), custom_call_target="tpu_custom_call" | custom-call | flops 5368709120 | bytes 9437184 | tf_op jit(solution)/shard_map/attend_back/pallas_call | solution.py:390
  570.1 9.0 %fusion.66 = f32[2048,1280]{1,0:T(8,128)} fusion(bf16[2048,480]{1,0:T(8,128)(2,1)} %attend_back.2.refs_4_, bf16[1280,960]{1,0:T(8,128)(2,1)} %tie.4), kind=kOutput, calls=%fused_computation.131 | convolution fusion | flops 2516582400 | bytes 13893632 | tf_op jit(solution)/shard_map/dot_general | solution.py:35
  579.1 5.8 add_convert_fusion
  590.8 6.1 convolution_convert_fusion.2
  597.3 5.1 collective-permute-start.23
  604.8 2.5 collective-permute-start.35
  612.1 2.4 collective-permute-start.32
  614.5 29.2 %collective-permute-done.34 = bf16[160,640]{1,0:T(8,128)(2,1)S(1)} collective-permute-done((bf16[160,640]{1,0:T(8,128)(2,1)}, bf16[160,640]{1,0:T(8,128)(2,1)S(1)}, u32[]{:S(2)}, u32[]{:S(2)}) %collective-permute-start.34) | collective-permute-done | bytes 204832 | tf_op jit(solution)/shard_map/ppermute | solution.py:70
  643.7 8.0 %collective-permute-done.33 = bf16[160,640]{1,0:T(8,128)(2,1)S(1)} collective-permute-done((bf16[160,640]{1,0:T(8,128)(2,1)}, bf16[160,640]{1,0:T(8,128)(2,1)S(1)}, u32[]{:S(2)}, u32[]{:S(2)}) %collective-permute-start.33) | collective-permute-done | bytes 204832 | tf_op jit(solution)/shard_map/ppermute | solution.py:70
  651.6 2.4 collective-permute-start.30
  654.2 3.5 collective-permute-done.30
  664.5 9.4 %collective-permute-done.26 = bf16[256,1280]{1,0:T(8,128)(2,1)S(1)} collective-permute-done((bf16[256,1280]{1,0:T(8,128)(2,1)S(1)}, bf16[256,1280]{1,0:T(8,128)(2,1)S(1)}, u32[]{:S(2)}, u32[]{:S(2)}) %collective-permute-start.26) | collective-permute-done | bytes 655392 | tf_op jit(solution)/shard_map/ppermute | solution.py:70
  677.1 2.7 convert_reduce_fusion.4
  685.4 4.7 collective-permute-start.29
  691.2 3.7 collective-permute-start.41
  696.4 11.1 %collective-permute-done.29 = bf16[320,480]{1,0:T(8,128)(2,1)S(1)} collective-permute-done((bf16[320,480]{1,0:T(8,128)(2,1)S(1)}, bf16[320,480]{1,0:T(8,128)(2,1)S(1)}, u32[]{:S(2)}, u32[]{:S(2)}) %collective-permute-start.29) | collective-permute-done | bytes 307232 | tf_op jit(solution)/shard_map/ppermute | solution.py:70
  707.7 2.9 concatenate.61
  710.6 3.5 copy.417
  714.2 6.5 multiply_subtract_fusion
  (408 shorter events, 145.2 us)
Async XLA Ops:
  7.2 242.8 %all-gather.3.cloned.1.call-start = ((), (), s32[]{:S(2)}) async-start(), calls=%async_computation.5 | async-start | bytes 18923520 | tf_op jit(solution)/shard_map/all_gather | solution.py:493
  11.3 270.7 %all-gather.5.cloned.1.call-start = ((), (), s32[]{:S(2)}) async-start(), calls=%async_computation.6 | async-start | bytes 13516800 | tf_op jit(solution)/shard_map/all_gather | solution.py:495
  16.3 48.0 %copy-start.42 = (bf16[256,1280]{1,0:T(8,128)(2,1)}, bf16[256,1280]{1,0:T(8,128)(2,1)S(1)}, u32[]{:S(2)}) copy-start(bf16[256,1280]{1,0:T(8,128)(2,1)S(1)} %get-tuple-element.84) | copy-start | bytes 1966084
  16.3 44.0 %collective-permute-start.2 = (bf16[256,1280]{1,0:T(8,128)(2,1)}, bf16[256,1280]{1,0:T(8,128)(2,1)}, u32[]{:S(2)}, u32[]{:S(2)}) collective-permute-start(bf16[256,1280]{1,0:T(8,128)(2,1)} %get-tuple-element.85), channel_id=1, source_target_pairs={{0,2},{2,0},{1,3},{3,1},{4,6},{6,4},{5,7},{7,5},{8,10},{10,8},{9,1... | collective-permute-start | bytes 1966088 | tf_op jit(solution)/shard_map/ppermute | solution.py:70
  16.4 47.9 %collective-permute-start = (bf16[256,1280]{1,0:T(8,128)(2,1)S(1)}, bf16[256,1280]{1,0:T(8,128)(2,1)}, u32[]{:S(2)}, u32[]{:S(2)}) collective-permute-start(bf16[256,1280]{1,0:T(8,128)(2,1)S(1)} %get-tuple-element.84), channel_id=1, source_target_pairs={{0,1},{1,0},{2,3},{3,2},{4,5},{5,4},{6,7},{7,6},{8,9},{9,8},{10,11... | collective-permute-start | bytes 1966088 | tf_op jit(solution)/shard_map/ppermute | solution.py:70
  18.4 35.9 %collective-permute-start.4 = (bf16[320,480]{0,1:T(8,128)(2,1)S(1)}, bf16[320,480]{0,1:T(8,128)(2,1)}, u32[]{:S(2)}, u32[]{:S(2)}) collective-permute-start(bf16[320,480]{0,1:T(8,128)(2,1)S(1)} %bitcast.333), channel_id=1, source_target_pairs={{0,4},{4,0},{1,5},{5,1},{2,6},{6,2},{3,7},{7,3},{8,12},{12,8},{9,1... | collective-permute-start | bytes 921608 | tf_op jit(solution)/shard_map/ppermute | solution.py:70
  21.5 169.0 %copy-start.10 = (s32[2048]{0:T(1024)}, s32[2048]{0:T(1024)S(1)}, u32[]{:S(2)}) copy-start(s32[2048]{0:T(1024)S(1)} %convert_reduce_fusion.5) | copy-start | bytes 24580
  58.9 30.5 %collective-permute-start.5 = (bf16[320,960]{1,0:T(8,128)(2,1)}, bf16[320,960]{1,0:T(8,128)(2,1)}, u32[]{:S(2)}, u32[]{:S(2)}) collective-permute-start(bf16[320,960]{1,0:T(8,128)(2,1)} %copy.363), channel_id=1, source_target_pairs={{0,16},{16,0},{1,17},{17,1},{2,18},{18,2},{3,19},{19,3},{4,20},{20... | collective-permute-start | bytes 1843208 | tf_op jit(solution)/shard_map/ppermute | solution.py:70
  62.8 35.7 %collective-permute-start.3 = (bf16[2,256,1280]{2,1,0:T(8,128)(2,1)}, bf16[2,256,1280]{2,1,0:T(8,128)(2,1)}, u32[]{:S(2)}, u32[]{:S(2)}) collective-permute-start(bf16[2,256,1280]{2,1,0:T(8,128)(2,1)} %bitcast.3), channel_id=1, source_target_pairs={{0,1},{1,0},{2,3},{3,2},{4,5},{5,4},{6,7},{7,6},{8,9},{9,8},{10,11... | collective-permute-start | bytes 3932168 | tf_op jit(solution)/shard_map/ppermute | solution.py:70
  66.6 44.0 %collective-permute-start.1 = (bf16[512,1280]{1,0:T(8,128)(2,1)}, bf16[512,1280]{1,0:T(8,128)(2,1)}, u32[]{:S(2)}, u32[]{:S(2)}) collective-permute-start(bf16[512,1280]{1,0:T(8,128)(2,1)} %pad_maximum_fusion.9), channel_id=1, source_target_pairs={{0,2},{2,0},{1,3},{3,1},{4,6},{6,4},{5,7},{7,5},{8,10},{10,8},{9,1... | collective-permute-start | bytes 3932168 | tf_op jit(solution)/shard_map/ppermute | solution.py:70
  67.8 67.8 %copy-start.3 = (f32[2048,128]{1,0:T(8,128)}, f32[2048,128]{1,0:T(8,128)S(1)}, u32[]{:S(2)}) copy-start(f32[2048,128]{1,0:T(8,128)S(1)} %get-tuple-element.86.sin_ref) | copy-start | bytes 3145732
  67.8 67.8 %copy-start.4 = (f32[2048,128]{1,0:T(8,128)}, f32[2048,128]{1,0:T(8,128)S(1)}, u32[]{:S(2)}) copy-start(f32[2048,128]{1,0:T(8,128)S(1)} %get-tuple-element.87.cos_ref) | copy-start | bytes 3145732
  98.0 16.7 %collective-permute-start.6 = (bf16[2,320,960]{2,1,0:T(8,128)(2,1)}, bf16[2,320,960]{2,1,0:T(8,128)(2,1)}, u32[]{:S(2)}, u32[]{:S(2)}) collective-permute-start(bf16[2,320,960]{2,1,0:T(8,128)(2,1)} %copy.366), channel_id=1, source_target_pairs={{0,8},{8,0},{1,9},{9,1},{2,10},{10,2},{3,11},{11,3},{4,12},{12,4},... | collective-permute-start | bytes 3686408 | tf_op jit(solution)/shard_map/ppermute | solution.py:70
  98.4 92.1 %copy-start.2 = (s32[2048,1]{1,0:T(8,128)}, s32[2048,1]{1,0:T(8,128)S(1)}, u32[]{:S(2)}) copy-start(s32[2048,1]{1,0:T(8,128)S(1)} %copy.377.column_ids) | copy-start | bytes 24580
  98.5 92.0 %copy-start.13 = (s32[17]{0:T(128)}, s32[17]{0:T(128)S(1)}, u32[]{:S(2)}) copy-start(s32[17]{0:T(128)S(1)} %pad_add_fusion.info_ref) | copy-start | bytes 208
  181.9 39.0 %copy-start.12 = (f32[8,2,256]{2,1,0:T(2,128)}, f32[8,2,256]{2,1,0:T(2,128)S(1)}, u32[]{:S(2)}) copy-start(f32[8,2,256]{2,1,0:T(2,128)S(1)} %get-tuple-element.21.refs_0_.lse_ref) | copy-start | bytes 49156
  184.2 40.0 %all-to-all-start = ((bf16[4,512,160]{1,2,0:T(8,128)(2,1)}), bf16[4,512,160]{1,2,0:T(8,128)(2,1)}, u32[]{:S(2)}, u32[]{:S(2)}) async-start(bf16[4,512,160]{1,2,0:T(8,128)(2,1)} %copy.378), calls=%async_computation | async-start | bytes 1310720 | tf_op jit(solution)/shard_map/all_to_all | solution.py:556
  224.1 24.9 %all-to-all-start.1 = ((bf16[4,512,160]{1,2,0:T(8,128)(2,1)}), bf16[4,512,160]{1,2,0:T(8,128)(2,1)S(1)}, u32[]{:S(2)}, u32[]{:S(2)}) async-start(bf16[4,512,160]{1,2,0:T(8,128)(2,1)} %copy.380), calls=%async_computation.1 | async-start | bytes 1310720 | tf_op jit(solution)/shard_map/all_to_all | solution.py:556
  277.3 21.6 %collective-permute-start.7 = (bf16[8,640,640]{2,1,0:T(8,128)(2,1)}, bf16[8,640,640]{2,1,0:T(8,128)(2,1)}, u32[]{:S(2)}, u32[]{:S(2)}) collective-permute-start(bf16[8,640,640]{2,1,0:T(8,128)(2,1)} %convert_bitcast_fusion.1), channel_id=1, source_target_pairs={{0,8},{8,0},{1,9},{9,1},{2,10},{10,2},{3,11},{11,3},{4,12},{12,4},... | collective-permute-start | bytes 19660808 | tf_op jit(solution)/shard_map/ppermute | solution.py:70
  328.3 25.6 %all-to-all-start.2 = ((bf16[4,512,160]{1,2,0:T(8,128)(2,1)}), bf16[4,512,160]{1,2,0:T(8,128)(2,1)S(1)}, u32[]{:S(2)}, u32[]{:S(2)}) async-start(bf16[4,512,160]{1,2,0:T(8,128)(2,1)} %get-tuple-element.81), calls=%async_computation.2 | async-start | bytes 1310720 | tf_op jit(solution)/shard_map/all_to_all | solution.py:618
  343.1 110.8 %collective-permute-start.12 = (bf16[8,640,640]{2,1,0:T(8,128)(2,1)}, bf16[8,640,640]{2,1,0:T(8,128)(2,1)}, u32[]{:S(2)}, u32[]{:S(2)}) collective-permute-start(bf16[8,640,640]{2,1,0:T(8,128)(2,1)} %convert_bitcast_fusion), channel_id=1, source_target_pairs={{0,8},{8,0},{1,9},{9,1},{2,10},{10,2},{3,11},{11,3},{4,12},{12,4},... | collective-permute-start | bytes 19660808 | tf_op jit(solution)/shard_map/ppermute | solution.py:70
  347.2 47.5 %collective-permute-start.8 = (bf16[4,2,160,640]{3,2,0,1:T(8,128)(2,1)}, bf16[4,2,160,640]{3,2,0,1:T(8,128)(2,1)}, u32[]{:S(2)}, u32[]{:S(2)}) collective-permute-start(bf16[4,2,160,640]{3,2,0,1:T(8,128)(2,1)} %bitcast.296), channel_id=1, source_target_pairs={{0,1},{1,0},{2,3},{3,2},{4,5},{5,4},{6,7},{7,6},{8,9},{9,8},{10,11... | collective-permute-start | bytes 4915208 | tf_op jit(solution)/shard_map/ppermute | solution.py:70
  351.6 46.4 %collective-permute-start.9 = (bf16[4,2,160,640]{3,2,0,1:T(8,128)(2,1)}, bf16[4,2,160,640]{3,2,0,1:T(8,128)(2,1)}, u32[]{:S(2)}, u32[]{:S(2)}) collective-permute-start(bf16[4,2,160,640]{3,2,0,1:T(8,128)(2,1)} %bitcast.295), channel_id=1, source_target_pairs={{0,16},{16,0},{1,17},{17,1},{2,18},{18,2},{3,19},{19,3},{4,20},{20... | collective-permute-start | bytes 4915208 | tf_op jit(solution)/shard_map/ppermute | solution.py:70
  353.8 38.7 %all-to-all-start.3 = ((bf16[4,512,160]{1,2,0:T(8,128)(2,1)}), bf16[4,512,160]{1,2,0:T(8,128)(2,1)}, u32[]{:S(2)}, u32[]{:S(2)}) async-start(bf16[4,512,160]{1,2,0:T(8,128)(2,1)} %get-tuple-element.80), calls=%async_computation.3 | async-start | bytes 1310720 | tf_op jit(solution)/shard_map/all_to_all | solution.py:618
  358.5 349.2 %reduce-scatter.2.cloned.1.call-start = ((), (), s32[]{:S(2)}) async-start(), calls=%async_computation.7 | async-start | bytes 5406720 | tf_op jit(solution)/shard_map/reduce_scatter | solution.py:623
  401.1 47.6 %slice-start.4 = ((s8[5242880]{0:T(1024)(128)(4,1)}), s8[4194304]{0:T(1024)(128)(4,1)S(1)}, s32[]{:S(2)}) async-start(s8[5242880]{0:T(1024)(128)(4,1)} %bitcast.322), calls=%async_computation.12 | async-start | bytes 8388608
  403.5 74.9 %collective-permute-start.10 = (bf16[4,160,640]{2,1,0:T(8,128)(2,1)}, bf16[4,160,640]{2,1,0:T(8,128)(2,1)}, u32[]{:S(2)}, u32[]{:S(2)}) collective-permute-start(bf16[4,160,640]{2,1,0:T(8,128)(2,1)} %dynamic-slice_bitcast_fusion.3), channel_id=1, source_target_pairs={{0,16},{16,0},{1,17},{17,1},{2,18},{18,2},{3,19},{19,3},{4,20},{20... | collective-permute-start | bytes 2457608 | tf_op jit(solution)/shard_map/ppermute | solution.py:70
  407.8 64.1 %collective-permute-start.11 = (bf16[4,160,640]{2,1,0:T(8,128)(2,1)}, bf16[4,160,640]{2,1,0:T(8,128)(2,1)}, u32[]{:S(2)}, u32[]{:S(2)}) collective-permute-start(bf16[4,160,640]{2,1,0:T(8,128)(2,1)} %dynamic-slice_bitcast_fusion.2), channel_id=1, source_target_pairs={{0,1},{1,0},{2,3},{3,2},{4,5},{5,4},{6,7},{7,6},{8,9},{9,8},{10,11... | collective-permute-start | bytes 2457608 | tf_op jit(solution)/shard_map/ppermute | solution.py:70
  409.3 39.4 %slice-start.5 = ((s8[5242880]{0:T(1024)(128)(4,1)}), s8[1048576]{0:T(1024)(128)(4,1)S(1)}, s32[]{:S(2)}) async-start(s8[5242880]{0:T(1024)(128)(4,1)} %bitcast.322), calls=%async_computation.13 | async-start | bytes 2097152
  467.5 52.9 %collective-permute-start.13 = (bf16[4,2,160,640]{3,2,0,1:T(8,128)(2,1)}, bf16[4,2,160,640]{3,2,0,1:T(8,128)(2,1)}, u32[]{:S(2)}, u32[]{:S(2)}) collective-permute-start(bf16[4,2,160,640]{3,2,0,1:T(8,128)(2,1)} %bitcast.294), channel_id=1, source_target_pairs={{0,16},{16,0},{1,17},{17,1},{2,18},{18,2},{3,19},{19,3},{4,20},{20... | collective-permute-start | bytes 4915208 | tf_op jit(solution)/shard_map/ppermute | solution.py:70
  471.2 52.0 %collective-permute-start.14 = (bf16[4,2,160,640]{3,2,0,1:T(8,128)(2,1)S(1)}, bf16[4,2,160,640]{3,2,0,1:T(8,128)(2,1)S(1)}, u32[]{:S(2)}, u32[]{:S(2)}) collective-permute-start(bf16[4,2,160,640]{3,2,0,1:T(8,128)(2,1)S(1)} %bitcast.332), channel_id=1, source_target_pairs={{0,1},{1,0},{2,3},{3,2},{4,5},{5,4},{6,7},{7,6},{8,9},{9,8},{10,11... | collective-permute-start | bytes 4915208 | tf_op jit(solution)/shard_map/ppermute | solution.py:70
  473.8 38.7 %copy-start.35 = (bf16[4,160,640]{2,1,0:T(8,128)(2,1)}, bf16[4,160,640]{2,1,0:T(8,128)(2,1)S(1)}, u32[]{:S(2)}) copy-start(bf16[4,160,640]{2,1,0:T(8,128)(2,1)S(1)} %fusion.53.refs_1_) | copy-start | bytes 2457604
  473.9 21.2 %collective-permute-start.22 = (bf16[160,640]{1,0:T(8,128)(2,1)S(1)}, bf16[160,640]{1,0:T(8,128)(2,1)S(1)}, u32[]{:S(2)}, u32[]{:S(2)}) collective-permute-start(bf16[160,640]{1,0:T(8,128)(2,1)S(1)} %get-tuple-element.98), channel_id=1, source_target_pairs={{0,6},{2,4},{4,2},{6,0},{1,7},{3,5},{5,3},{7,1},{8,14},{10,12},{12... | collective-permute-start | bytes 614408 | tf_op jit(solution)/shard_map/ppermute | solution.py:70
  478.4 25.5 %collective-permute-start.21 = (bf16[160,640]{1,0:T(8,128)(2,1)S(1)}, bf16[160,640]{1,0:T(8,128)(2,1)S(1)}, u32[]{:S(2)}, u32[]{:S(2)}) collective-permute-start(bf16[160,640]{1,0:T(8,128)(2,1)S(1)} %get-tuple-element.99), channel_id=1, source_target_pairs={{0,4},{2,6},{4,0},{6,2},{1,5},{3,7},{5,1},{7,3},{8,12},{10,14},{12... | collective-permute-start | bytes 614408 | tf_op jit(solution)/shard_map/ppermute | solution.py:70
  478.4 42.0 %copy-start.39 = (bf16[4,2,1,1,160,640]{5,4,3,2,1,0:T(8,128)(2,1)S(1)}, bf16[4,2,1,1,160,640]{5,4,3,2,1,0:T(8,128)(2,1)}, u32[]{:S(2)}) copy-start(bf16[4,2,1,1,160,640]{5,4,3,2,1,0:T(8,128)(2,1)} %get-tuple-element.64) | copy-start | bytes 4915204
  478.4 34.0 %collective-permute-start.20 = (bf16[160,640]{1,0:T(8,128)(2,1)S(1)}, bf16[160,640]{1,0:T(8,128)(2,1)S(1)}, u32[]{:S(2)}, u32[]{:S(2)}) collective-permute-start(bf16[160,640]{1,0:T(8,128)(2,1)S(1)} %get-tuple-element.97), channel_id=1, source_target_pairs={{0,2},{2,0},{4,6},{6,4},{1,3},{3,1},{5,7},{7,5},{8,10},{10,8},{12,... | collective-permute-start | bytes 614408 | tf_op jit(solution)/shard_map/ppermute | solution.py:70
  481.3 41.0 %copy-start.36 = (bf16[4,160,640]{2,1,0:T(8,128)(2,1)}, bf16[4,160,640]{2,1,0:T(8,128)(2,1)S(1)}, u32[]{:S(2)}) copy-start(bf16[4,160,640]{2,1,0:T(8,128)(2,1)S(1)} %fusion.54.refs_0_) | copy-start | bytes 2457604
  495.1 20.0 %collective-permute-start.19 = (bf16[160,640]{1,0:T(8,128)(2,1)S(1)}, bf16[160,640]{1,0:T(8,128)(2,1)S(1)}, u32[]{:S(2)}, u32[]{:S(2)}) collective-permute-start(bf16[160,640]{1,0:T(8,128)(2,1)S(1)} %get-tuple-element.95), channel_id=1, source_target_pairs={{0,6},{2,4},{4,2},{6,0},{1,7},{3,5},{5,3},{7,1},{8,14},{10,12},{12... | collective-permute-start | bytes 614408 | tf_op jit(solution)/shard_map/ppermute | solution.py:70
  503.9 16.4 %collective-permute-start.18 = (bf16[160,640]{1,0:T(8,128)(2,1)S(1)}, bf16[160,640]{1,0:T(8,128)(2,1)S(1)}, u32[]{:S(2)}, u32[]{:S(2)}) collective-permute-start(bf16[160,640]{1,0:T(8,128)(2,1)S(1)} %get-tuple-element.96), channel_id=1, source_target_pairs={{0,4},{2,6},{4,0},{6,2},{1,5},{3,7},{5,1},{7,3},{8,12},{10,14},{12... | collective-permute-start | bytes 614408 | tf_op jit(solution)/shard_map/ppermute | solution.py:70
  512.4 7.9 %collective-permute-start.17 = (bf16[160,640]{1,0:T(8,128)(2,1)S(1)}, bf16[160,640]{1,0:T(8,128)(2,1)S(1)}, u32[]{:S(2)}, u32[]{:S(2)}) collective-permute-start(bf16[160,640]{1,0:T(8,128)(2,1)S(1)} %get-tuple-element.94), channel_id=1, source_target_pairs={{0,2},{2,0},{4,6},{6,4},{1,3},{3,1},{5,7},{7,5},{8,10},{10,8},{12,... | collective-permute-start | bytes 614408 | tf_op jit(solution)/shard_map/ppermute | solution.py:70
  523.2 43.5 %collective-permute-start.15 = (bf16[4,160,640]{2,1,0:T(8,128)(2,1)}, bf16[4,160,640]{2,1,0:T(8,128)(2,1)}, u32[]{:S(2)}, u32[]{:S(2)}) collective-permute-start(bf16[4,160,640]{2,1,0:T(8,128)(2,1)} %dynamic-slice_bitcast_fusion.1), channel_id=1, source_target_pairs={{0,1},{1,0},{2,3},{3,2},{4,5},{5,4},{6,7},{7,6},{8,9},{9,8},{10,11... | collective-permute-start | bytes 2457608 | tf_op jit(solution)/shard_map/ppermute | solution.py:70
  523.7 45.3 %collective-permute-start.16 = (bf16[4,160,640]{2,1,0:T(8,128)(2,1)S(1)}, bf16[4,160,640]{2,1,0:T(8,128)(2,1)S(1)}, u32[]{:S(2)}, u32[]{:S(2)}) collective-permute-start(bf16[4,160,640]{2,1,0:T(8,128)(2,1)S(1)} %dynamic-slice_bitcast_fusion), channel_id=1, source_target_pairs={{0,16},{16,0},{1,17},{17,1},{2,18},{18,2},{3,19},{19,3},{4,20},{20... | collective-permute-start | bytes 2457608 | tf_op jit(solution)/shard_map/ppermute | solution.py:70
  597.3 60.6 %collective-permute-start.23 = (bf16[2,256,1280]{2,1,0:T(8,128)(2,1)}, bf16[2,256,1280]{2,1,0:T(8,128)(2,1)}, u32[]{:S(2)}, u32[]{:S(2)}) collective-permute-start(bf16[2,256,1280]{2,1,0:T(8,128)(2,1)} %slice_bitcast_fusion.4), channel_id=1, source_target_pairs={{0,2},{2,0},{1,3},{3,1},{4,6},{6,4},{5,7},{7,5},{8,10},{10,8},{9,1... | collective-permute-start | bytes 3932168 | tf_op jit(solution)/shard_map/ppermute | solution.py:70
  602.5 55.5 %collective-permute-start.25 = (bf16[2,256,1280]{2,1,0:T(8,128)(2,1)}, bf16[2,256,1280]{2,1,0:T(8,128)(2,1)}, u32[]{:S(2)}, u32[]{:S(2)}) collective-permute-start(bf16[2,256,1280]{2,1,0:T(8,128)(2,1)} %slice_bitcast_fusion.1), channel_id=1, source_target_pairs={{0,1},{1,0},{2,3},{3,2},{4,5},{5,4},{6,7},{7,6},{8,9},{9,8},{10,11... | collective-permute-start | bytes 3932168 | tf_op jit(solution)/shard_map/ppermute | solution.py:70
  604.8 7.3 collective-permute-start.35
  607.3 36.4 %collective-permute-start.34 = (bf16[160,640]{1,0:T(8,128)(2,1)}, bf16[160,640]{1,0:T(8,128)(2,1)S(1)}, u32[]{:S(2)}, u32[]{:S(2)}) collective-permute-start(bf16[160,640]{1,0:T(8,128)(2,1)} %get-tuple-element.93), channel_id=1, source_target_pairs={{0,4},{2,6},{4,0},{6,2},{1,5},{3,7},{5,1},{7,3},{8,12},{10,14},{12... | collective-permute-start | bytes 614408 | tf_op jit(solution)/shard_map/ppermute | solution.py:70
  607.3 44.3 %collective-permute-start.33 = (bf16[160,640]{1,0:T(8,128)(2,1)}, bf16[160,640]{1,0:T(8,128)(2,1)S(1)}, u32[]{:S(2)}, u32[]{:S(2)}) collective-permute-start(bf16[160,640]{1,0:T(8,128)(2,1)} %get-tuple-element.91), channel_id=1, source_target_pairs={{0,2},{2,0},{4,6},{6,4},{1,3},{3,1},{5,7},{7,5},{8,10},{10,8},{12,... | collective-permute-start | bytes 614408 | tf_op jit(solution)/shard_map/ppermute | solution.py:70
  609.1 48.9 %slice-start.2 = ((s8[5242880]{0:T(1024)(128)(4,1)}), s8[4194304]{0:T(1024)(128)(4,1)S(1)}, s32[]{:S(2)}) async-start(s8[5242880]{0:T(1024)(128)(4,1)} %bitcast.313), calls=%async_computation.10 | async-start | bytes 8388608
  610.8 47.1 %slice-start.3 = ((s8[5242880]{0:T(1024)(128)(4,1)}), s8[1048576]{0:T(1024)(128)(4,1)S(1)}, s32[]{:S(2)}) async-start(s8[5242880]{0:T(1024)(128)(4,1)} %bitcast.313), calls=%async_computation.11 | async-start | bytes 2097152
  612.1 42.0 %collective-permute-start.32 = (bf16[160,640]{1,0:T(8,128)(2,1)S(1)}, bf16[160,640]{1,0:T(8,128)(2,1)S(1)}, u32[]{:S(2)}, u32[]{:S(2)}) collective-permute-start(bf16[160,640]{1,0:T(8,128)(2,1)S(1)} %get-tuple-element.89), channel_id=1, source_target_pairs={{0,6},{2,4},{4,2},{6,0},{1,7},{3,5},{5,3},{7,1},{8,14},{10,12},{12... | collective-permute-start | bytes 614408 | tf_op jit(solution)/shard_map/ppermute | solution.py:70
  643.7 10.6 %collective-permute-start.31 = (bf16[160,640]{1,0:T(8,128)(2,1)S(1)}, bf16[160,640]{1,0:T(8,128)(2,1)S(1)}, u32[]{:S(2)}, u32[]{:S(2)}) collective-permute-start(bf16[160,640]{1,0:T(8,128)(2,1)S(1)} %get-tuple-element.90), channel_id=1, source_target_pairs={{0,4},{2,6},{4,0},{6,2},{1,5},{3,7},{5,1},{7,3},{8,12},{10,14},{12... | collective-permute-start | bytes 614408 | tf_op jit(solution)/shard_map/ppermute | solution.py:70
  651.6 6.1 collective-permute-start.30
  654.1 9.1 %collective-permute-start.27 = (bf16[2,2,320,480]{3,2,0,1:T(8,128)(2,1)S(1)}, bf16[2,2,320,480]{3,2,0,1:T(8,128)(2,1)S(1)}, u32[]{:S(2)}, u32[]{:S(2)}) collective-permute-start(bf16[2,2,320,480]{3,2,0,1:T(8,128)(2,1)S(1)} %bitcast.334), channel_id=1, source_target_pairs={{0,8},{8,0},{1,9},{9,1},{2,10},{10,2},{3,11},{11,3},{4,12},{12,4},... | collective-permute-start | bytes 3686408 | tf_op jit(solution)/shard_map/ppermute | solution.py:70
  660.3 13.7 %collective-permute-start.26 = (bf16[256,1280]{1,0:T(8,128)(2,1)S(1)}, bf16[256,1280]{1,0:T(8,128)(2,1)S(1)}, u32[]{:S(2)}, u32[]{:S(2)}) collective-permute-start(bf16[256,1280]{1,0:T(8,128)(2,1)S(1)} %fusion.76), channel_id=1, source_target_pairs={{0,2},{2,0},{1,3},{3,1},{4,6},{6,4},{5,7},{7,5},{8,10},{10,8},{9,1... | collective-permute-start | bytes 1966088 | tf_op jit(solution)/shard_map/ppermute | solution.py:70
  662.4 11.7 %collective-permute-start.24 = (bf16[256,1280]{1,0:T(8,128)(2,1)S(1)}, bf16[256,1280]{1,0:T(8,128)(2,1)S(1)}, u32[]{:S(2)}, u32[]{:S(2)}) collective-permute-start(bf16[256,1280]{1,0:T(8,128)(2,1)S(1)} %fusion.75), channel_id=1, source_target_pairs={{0,1},{1,0},{2,3},{3,2},{4,5},{5,4},{6,7},{7,6},{8,9},{9,8},{10,11... | collective-permute-start | bytes 1966088 | tf_op jit(solution)/shard_map/ppermute | solution.py:70
  664.5 15.6 %collective-permute-start.28 = (bf16[2,320,480]{2,1,0:T(8,128)(2,1)}, bf16[2,320,480]{2,1,0:T(8,128)(2,1)}, u32[]{:S(2)}, u32[]{:S(2)}) collective-permute-start(bf16[2,320,480]{2,1,0:T(8,128)(2,1)} %dynamic-slice_bitcast_fusion.4), channel_id=1, source_target_pairs={{0,16},{16,0},{1,17},{17,1},{2,18},{18,2},{3,19},{19,3},{4,20},{20... | collective-permute-start | bytes 1843208 | tf_op jit(solution)/shard_map/ppermute | solution.py:70
  680.0 1.4 collective-permute-start.36
  681.4 8.7 %collective-permute-start.38 = (f32[13,1280]{1,0:T(8,128)S(1)}, f32[13,1280]{1,0:T(8,128)S(1)}, u32[]{:S(2)}, u32[]{:S(2)}) collective-permute-start(f32[13,1280]{1,0:T(8,128)S(1)} %add.469), channel_id=1, source_target_pairs={{0,16},{1,17},{16,0},{17,1},{2,18},{3,19},{18,2},{19,3},{4,20},{5,... | collective-permute-start | bytes 199688 | tf_op jit(solution)/shard_map/ppermute | solution.py:70
  683.7 6.5 collective-permute-start.39
  684.9 6.3 collective-permute-start.37
  685.4 22.2 %collective-permute-start.29 = (bf16[320,480]{1,0:T(8,128)(2,1)S(1)}, bf16[320,480]{1,0:T(8,128)(2,1)S(1)}, u32[]{:S(2)}, u32[]{:S(2)}) collective-permute-start(bf16[320,480]{1,0:T(8,128)(2,1)S(1)} %dynamic-slice_bitcast_fusion.5), channel_id=1, source_target_pairs={{0,4},{4,0},{1,5},{5,1},{2,6},{6,2},{3,7},{7,3},{8,12},{12,8},{9,1... | collective-permute-start | bytes 921608 | tf_op jit(solution)/shard_map/ppermute | solution.py:70
  691.2 29.4 %collective-permute-start.41 = (f32[13,1280]{1,0:T(8,128)S(1)}, f32[13,1280]{1,0:T(8,128)S(1)}, u32[]{:S(2)}, u32[]{:S(2)}) collective-permute-start(f32[13,1280]{1,0:T(8,128)S(1)} %add_add_fusion.3), channel_id=1, source_target_pairs={{0,4},{2,6},{4,0},{6,2},{1,5},{3,7},{5,1},{7,3},{8,12},{10,14},{12... | collective-permute-start | bytes 199688 | tf_op jit(solution)/shard_map/ppermute | solution.py:70
  694.9 25.8 %collective-permute-start.42 = (f32[13,1280]{1,0:T(8,128)S(1)}, f32[13,1280]{1,0:T(8,128)S(1)}, u32[]{:S(2)}, u32[]{:S(2)}) collective-permute-start(f32[13,1280]{1,0:T(8,128)S(1)} %add_add_fusion.3), channel_id=1, source_target_pairs={{0,6},{2,4},{4,2},{6,0},{1,7},{3,5},{5,3},{7,1},{8,14},{10,12},{12... | collective-permute-start | bytes 199688 | tf_op jit(solution)/shard_map/ppermute | solution.py:70
  694.9 25.8 %collective-permute-start.40 = (f32[13,1280]{1,0:T(8,128)S(1)}, f32[13,1280]{1,0:T(8,128)S(1)}, u32[]{:S(2)}, u32[]{:S(2)}) collective-permute-start(f32[13,1280]{1,0:T(8,128)S(1)} %add_add_fusion.3), channel_id=1, source_target_pairs={{0,2},{2,0},{4,6},{6,4},{1,3},{3,1},{5,7},{7,5},{8,10},{10,8},{12,... | collective-permute-start | bytes 199688 | tf_op jit(solution)/shard_map/ppermute | solution.py:70
  (67 other events, 510.7 us)
Sparse Core Ops, SparseCore 0:
  11.5 158.1 all-gather.2
  172.5 102.0 all-gather.4
  381.4 132.3 reduce-scatter.1
